TPU v7x, 256 devices: a whole 4x4x8 slice. The times are simulated.
256 devices in a mesh: section: 8 (over z_hi, core), dp: 32 (over y, x, z_lo).
Axes of the slice: x: 4, y: 4, z: 8 (z_hi: 4, z_lo: 2; z = z_hi * 2 + z_lo), core: 2. Of those that a mesh axis runs over, the one named last changes fastest.
Arguments:
- inputs: bfloat16 [4096, 7168], P('dp'), may hold values from -6 to 6
- cotangent: bfloat16 [4096, 7168], P('dp'), may hold values from -6 to 6
- adapt_in: bfloat16 [8, 7168, 128], P('section'), may hold values from -0.0625 to 0.0625
- adapt_out: bfloat16 [8, 7168, 128], P('section'), may hold values from -0.5 to 0.5
- probe_in: bfloat16 [8, 7168, 128], P('section'), may hold values from -0.0625 to 0.0625
- probe_out: bfloat16 [8, 7168, 128], P('section'), may hold values from -0.5 to 0.5
Outputs:
- diag_in: float32 [8, 7168, 128], P('section', 'dp')
- diag_out: float32 [8, 7168, 128], P('section', 'dp')
All inputs are finite; a program needn't handle non-finite values.
Results may differ from a plain program's by a relative error of at most 0.027.
Values may be sent and summed in bfloat16 or wider, within the bound.
No kernel may reach another device: no remote copies, remote signals or barrier semaphores. Data moves between devices by JAX's collectives and lax.ppermute only.
A program may use at most 128 MiB of HBM per device.

v0:
```python
import jax
import jax.numpy as jnp
from jax import lax
from jax.sharding import PartitionSpec as P

MB = 16
MICRO = 8


eps = 1e-05


def shifted(value, axis, steps):
    count = lax.axis_size(axis)
    initial, last = (max(0, -steps), min(count, count - steps))
    return lax.ppermute(value, axis, [(source, source + steps) for source in range(initial, last)])


def matmul(left, right):
    return jnp.dot(left, right, preferred_element_type=jnp.float32)


def matmul_last(left, right):
    return lax.dot_general(
        left, right, (((1,), (1,)), ((), ())), preferred_element_type=jnp.float32
    )


def matmul_rows(left, right):
    return lax.dot_general(
        left, right, (((0,), (0,)), ((), ())), preferred_element_type=jnp.float32
    )


def rms_scale(values):
    return values * lax.rsqrt(jnp.mean(values * values, axis=-1, keepdims=True) + eps)


def rms_back(values, grads):
    scale = lax.rsqrt(jnp.mean(values * values, axis=-1, keepdims=True) + eps)
    return scale * grads - values * scale**3 * jnp.mean(grads * values, axis=-1, keepdims=True)


def activations(primal, tangent, w_in, p_in):
    primal32 = primal.astype(jnp.float32)
    tangent32 = tangent.astype(jnp.float32)
    normed, normed_t = jax.jvp(rms_scale, (primal32,), (tangent32,))
    normed_b = normed.astype(jnp.bfloat16)
    normed_tb = normed_t.astype(jnp.bfloat16)
    pre_act = matmul(normed_b, w_in)
    pre_tan = matmul(normed_tb, w_in) + matmul(normed_b, p_in)
    sigmoid_a = jax.nn.sigmoid(pre_act)
    slope = sigmoid_a * (1.0 + pre_act * (1.0 - sigmoid_a))
    hidden_b = (pre_act * sigmoid_a).astype(jnp.bfloat16)
    hidden_tb = (slope * pre_tan).astype(jnp.bfloat16)
    return (
        primal32,
        tangent32,
        normed_b,
        normed_tb,
        pre_act,
        pre_tan,
        sigmoid_a,
        slope,
        hidden_b,
        hidden_tb,
    )


def forward_section(primal, tangent, w_in, w_out, p_in, p_out):
    primal32, tangent32, _, _, _, _, _, _, hidden_b, hidden_tb = activations(
        primal, tangent, w_in, p_in
    )
    result = primal32 + matmul_last(hidden_b, w_out)
    result_t = tangent32 + matmul_last(hidden_tb, w_out) + matmul_last(hidden_b, p_out)
    return (result.astype(jnp.bfloat16), result_t.astype(jnp.bfloat16))


def backward_section(primal, tangent, adjoint, adj_tangent, w_in, w_out, p_in, p_out):
    (
        primal32,
        tangent32,
        normed_b,
        normed_tb,
        pre_act,
        pre_tan,
        sigmoid_a,
        slope,
        hidden_b,
        hidden_tb,
    ) = activations(primal, tangent, w_in, p_in)
    bend = sigmoid_a * (1.0 - sigmoid_a) * (2.0 + pre_act * (1.0 - 2.0 * sigmoid_a))
    grad_h = matmul(adjoint, w_out)
    grad_ht = matmul(adj_tangent, w_out) + matmul(adjoint, p_out)
    term_out = matmul_rows(adj_tangent, hidden_b) + matmul_rows(adjoint, hidden_tb)
    grad_pre = (grad_h * slope).astype(jnp.bfloat16)
    grad_pt = (grad_ht * slope + grad_h * bend * pre_tan).astype(jnp.bfloat16)
    term_in = matmul_rows(normed_tb, grad_pre) + matmul_rows(normed_b, grad_pt)
    grad_n = matmul_last(grad_pre, w_in)
    grad_nt = matmul_last(grad_pt, w_in) + matmul_last(grad_pre, p_in)
    back, back_t = jax.jvp(rms_back, (primal32, grad_n), (tangent32, grad_nt))
    grad_x = adjoint.astype(jnp.float32) + back
    grad_xt = adj_tangent.astype(jnp.float32) + back_t
    return (
        grad_x.astype(jnp.bfloat16),
        grad_xt.astype(jnp.bfloat16),
        p_in.astype(jnp.float32) * term_in,
        p_out.astype(jnp.float32) * term_out,
    )


def on_device(inputs, cotangent, adapt_in, adapt_out, probe_in, probe_out):
    sections = lax.axis_size("section")
    position = lax.axis_index("section")
    w_in, w_out, p_in, p_out = (adapt_in[0], adapt_out[0], probe_in[0], probe_out[0])
    rows_mb = MB
    width = inputs.shape[1]
    zero_rows = jnp.zeros((rows_mb, width), jnp.bfloat16)
    zero_terms = jnp.zeros(w_in.shape, jnp.float32)

    def forward_part(recv_p, recv_t, stash_p, stash_t, turn):
        micro_idx = turn - position
        active = (micro_idx >= 0) & (micro_idx < MICRO)
        slot_index = jnp.clip(micro_idx, 0, MICRO - 1)
        fresh = lax.dynamic_slice_in_dim(inputs, slot_index * rows_mb, rows_mb, 0)
        primal = jnp.where(position == 0, fresh, recv_p)
        tangent = jnp.where(position == 0, zero_rows, recv_t)
        stash_p = jnp.where(
            active, lax.dynamic_update_index_in_dim(stash_p, primal, slot_index, 0), stash_p
        )
        stash_t = jnp.where(
            active, lax.dynamic_update_index_in_dim(stash_t, tangent, slot_index, 0), stash_t
        )
        out_p, out_t = lax.cond(
            active,
            lambda: forward_section(primal, tangent, w_in, w_out, p_in, p_out),
            lambda: (zero_rows, zero_rows),
        )
        return (out_p, out_t, stash_p, stash_t)

    def backward_part(recv_g, recv_gt, stash_p, stash_t, sum_in, sum_out, micro_idx):
        active = (micro_idx >= 0) & (micro_idx < MICRO)
        slot_index = jnp.clip(micro_idx, 0, MICRO - 1)
        primal = lax.dynamic_index_in_dim(stash_p, slot_index, 0, keepdims=False)
        tangent = lax.dynamic_index_in_dim(stash_t, slot_index, 0, keepdims=False)
        fresh = lax.dynamic_slice_in_dim(cotangent, slot_index * rows_mb, rows_mb, 0)
        last_section = position == sections - 1
        adjoint = jnp.where(last_section, fresh, recv_g)
        adj_tangent = jnp.where(last_section, zero_rows, recv_gt)
        grad_x, grad_xt, term_in, term_out = lax.cond(
            active,
            lambda: backward_section(
                primal, tangent, adjoint, adj_tangent, w_in, w_out, p_in, p_out
            ),
            lambda: (zero_rows, zero_rows, zero_terms, zero_terms),
        )
        return (grad_x, grad_xt, sum_in + term_in, sum_out + term_out)

    stash_p = jnp.zeros((MICRO, rows_mb, width), jnp.bfloat16)
    stash_t = jnp.zeros((MICRO, rows_mb, width), jnp.bfloat16)

    def forward_turn(carry, turn):
        recv_p, recv_t, stash_p, stash_t = carry
        out_p, out_t, stash_p, stash_t = forward_part(recv_p, recv_t, stash_p, stash_t, turn)
        recv_p, recv_t = shifted((out_p, out_t), "section", 1)
        return ((recv_p, recv_t, stash_p, stash_t), None)

    forward_done, _ = lax.scan(
        forward_turn,
        (zero_rows, zero_rows, stash_p, stash_t),
        jnp.arange(MICRO + sections - 1, dtype=jnp.int32),
    )
    stash_p, stash_t = (forward_done[2], forward_done[3])

    def backward_turn(carry, turn):
        recv_g, recv_gt, sum_in, sum_out = carry
        back_idx = turn - (sections - 1 - position)
        grad_x, grad_xt, sum_in, sum_out = backward_part(
            recv_g, recv_gt, stash_p, stash_t, sum_in, sum_out, back_idx
        )
        recv_g, recv_gt = shifted((grad_x, grad_xt), "section", -1)
        return ((recv_g, recv_gt, sum_in, sum_out), None)

    backward_done, _ = lax.scan(
        backward_turn,
        (zero_rows, zero_rows, zero_terms, zero_terms),
        jnp.arange(MICRO + sections - 1, dtype=jnp.int32),
    )
    sum_in, sum_out = (backward_done[2], backward_done[3])
    owned_in, owned_out = (
        lax.psum_scatter(sum_in, "dp", scatter_dimension=0, tiled=True),
        lax.psum_scatter(sum_out, "dp", scatter_dimension=0, tiled=True),
    )
    return (owned_in[None], owned_out[None])


def solution(mesh):
    in_specs = (
        P("dp", None),
        P("dp", None),
        P("section", None, None),
        P("section", None, None),
        P("section", None, None),
        P("section", None, None),
    )
    out_specs = (P("section", "dp", None), P("section", "dp", None))
    return jax.shard_map(
        on_device, mesh=mesh, in_specs=in_specs, out_specs=out_specs, check_vma=False
    )
```

profile of v0, /device:TPU:2, one launch (start us, length us, event | category | flops | bytes accessed | tf_op | source)
XLA Modules:
  0.0 1182.3 jit_solution(5846924332728605946)
XLA Ops:
  10.2 332.4 %while.36 = (s32[]{:T(128)}, bf16[16,7168]{1,0:T(8,128)(2,1)S(1)}, bf16[16,7168]{1,0:T(8,128)(2,1)S(1)}, bf16[8,16,7168]{2,1,0:T(8,128)(2,1)}, bf16[8,16,7168]{2...) while((s32[]{:T(128)}, bf16[16,7168]{1,0:T(8,128)(2,1)S(1)}, ...), condition=%wide.region_5.6_spmd, body=%wide.region_0.5_spmd.sunk | while | flops 179642448 | bytes 26429044 | solution.py:168
  98.5 9.5 collective-permute-start
  193.0 14.9 %collective-permute-start = (bf16[16,7168]{1,0:T(8,128)(2,1)S(1)}, bf16[16,7168]{1,0:T(8,128)(2,1)S(1)}, u32[]{:S(2)}, u32[]{:S(2)}) collective-permute-start(bf16[16,7168]{1,0:T(8,128)(2,1)S(1)} %get-tuple-element.766), channel_id=1, source_target_pairs={{0,32},{32,64},{64,96},{96,128},{128,160},{160,192},{192,224},{1,3... | collective-permute-start | bytes 688136 | tf_op jit(solution)/shard_map/while/body/eval_jaxpr/ppermute | solution.py:16
  225.3 12.1 %collective-permute-start.1 = (bf16[16,7168]{1,0:T(8,128)(2,1)}, bf16[16,7168]{1,0:T(8,128)(2,1)S(1)}, u32[]{:S(2)}, u32[]{:S(2)}) collective-permute-start(bf16[16,7168]{1,0:T(8,128)(2,1)} %copy-done.6), channel_id=1, source_target_pairs={{0,32},{32,64},{64,96},{96,128},{128,160},{160,192},{192,224},{1,3... | collective-permute-start | bytes 688136 | tf_op jit(solution)/shard_map/while/body/eval_jaxpr/ppermute | solution.py:16
  261.7 13.5 %collective-permute-start = (bf16[16,7168]{1,0:T(8,128)(2,1)S(1)}, bf16[16,7168]{1,0:T(8,128)(2,1)S(1)}, u32[]{:S(2)}, u32[]{:S(2)}) collective-permute-start(bf16[16,7168]{1,0:T(8,128)(2,1)S(1)} %get-tuple-element.766), channel_id=1, source_target_pairs={{0,32},{32,64},{64,96},{96,128},{128,160},{160,192},{192,224},{1,3... | collective-permute-start | bytes 688136 | tf_op jit(solution)/shard_map/while/body/eval_jaxpr/ppermute | solution.py:16
  291.3 11.3 collective-permute-start.1
  308.2 9.2 collective-permute-start
  342.6 488.8 %while.37 = (s32[]{:T(128)}, bf16[16,7168]{1,0:T(8,128)(2,1)S(1)}, bf16[16,7168]{1,0:T(8,128)(2,1)S(1)}, f32[7168,128]{1,0:T(8,128)}, f32[7168,128]{1,0:T(8,128)...) while((s32[]{:T(128)}, bf16[16,7168]{1,0:T(8,128)(2,1)S(1)}, ...), condition=%wide.region_13.14_spmd.clone, body=%wide.region_6.13_spmd.clone.sunk | while | flops 398170240 | bytes 104514504 | solution.py:184
  367.4 8.9 select_add_fusion.3
  425.4 8.9 select_add_fusion.3
  471.0 78.0 %collective-permute-done.2 = bf16[16,7168]{1,0:T(8,128)(2,1)S(1)} collective-permute-done((bf16[16,7168]{1,0:T(8,128)(2,1)S(1)}, bf16[16,7168]{1,0:T(8,128)(2,1)S(1)}, u32[]{:S(2)}, u32[]{:S(2)}) %collective-permute-start.2) | collective-permute-done | bytes 229408 | tf_op jit(solution)/shard_map/while/body/eval_jaxpr/ppermute | solution.py:16
  552.2 21.2 %conditional.6 = (bf16[16,7168]{1,0:T(8,128)(2,1)S(1)}, bf16[16,7168]{1,0:T(8,128)(2,1)S(1)}, f32[7168,128]{1,0:T(8,128)}, f32[7168,128]{1,0:T(8,128)}) conditional(s32[]{:T(128)} %convert_element_type.191, () %tuple.111, (pred[]{:T(512)}, s32[]{:T(128)}, bf16[128,7168]{1,0:T(8,128)(2,1)}, bf16[16,7168]{1,0:T(8,128)(2,1)S(1)}, ...), branch_computations={%region_7.7_spmd, %region_8.12_spmd} | conditional | flops 394500224 | bytes 80659008 | solution.py:150
  587.4 21.2 %conditional.6 = (bf16[16,7168]{1,0:T(8,128)(2,1)S(1)}, bf16[16,7168]{1,0:T(8,128)(2,1)S(1)}, f32[7168,128]{1,0:T(8,128)}, f32[7168,128]{1,0:T(8,128)}) conditional(s32[]{:T(128)} %convert_element_type.191, () %tuple.111, (pred[]{:T(512)}, s32[]{:T(128)}, bf16[128,7168]{1,0:T(8,128)(2,1)}, bf16[16,7168]{1,0:T(8,128)(2,1)S(1)}, ...), branch_computations={%region_7.7_spmd, %region_8.12_spmd} | conditional | flops 394500224 | bytes 80659008 | solution.py:150
  622.6 21.2 %conditional.6 = (bf16[16,7168]{1,0:T(8,128)(2,1)S(1)}, bf16[16,7168]{1,0:T(8,128)(2,1)S(1)}, f32[7168,128]{1,0:T(8,128)}, f32[7168,128]{1,0:T(8,128)}) conditional(s32[]{:T(128)} %convert_element_type.191, () %tuple.111, (pred[]{:T(512)}, s32[]{:T(128)}, bf16[128,7168]{1,0:T(8,128)(2,1)}, bf16[16,7168]{1,0:T(8,128)(2,1)S(1)}, ...), branch_computations={%region_7.7_spmd, %region_8.12_spmd} | conditional | flops 394500224 | bytes 80659008 | solution.py:150
  646.4 8.9 select_add_fusion.3
  657.8 21.2 %conditional.6 = (bf16[16,7168]{1,0:T(8,128)(2,1)S(1)}, bf16[16,7168]{1,0:T(8,128)(2,1)S(1)}, f32[7168,128]{1,0:T(8,128)}, f32[7168,128]{1,0:T(8,128)}) conditional(s32[]{:T(128)} %convert_element_type.191, () %tuple.111, (pred[]{:T(512)}, s32[]{:T(128)}, bf16[128,7168]{1,0:T(8,128)(2,1)}, bf16[16,7168]{1,0:T(8,128)(2,1)S(1)}, ...), branch_computations={%region_7.7_spmd, %region_8.12_spmd} | conditional | flops 394500224 | bytes 80659008 | solution.py:150
  693.0 21.2 %conditional.6 = (bf16[16,7168]{1,0:T(8,128)(2,1)S(1)}, bf16[16,7168]{1,0:T(8,128)(2,1)S(1)}, f32[7168,128]{1,0:T(8,128)}, f32[7168,128]{1,0:T(8,128)}) conditional(s32[]{:T(128)} %convert_element_type.191, () %tuple.111, (pred[]{:T(512)}, s32[]{:T(128)}, bf16[128,7168]{1,0:T(8,128)(2,1)}, bf16[16,7168]{1,0:T(8,128)(2,1)S(1)}, ...), branch_computations={%region_7.7_spmd, %region_8.12_spmd} | conditional | flops 394500224 | bytes 80659008 | solution.py:150
  716.9 8.9 select_add_fusion.3
  728.3 21.2 %conditional.6 = (bf16[16,7168]{1,0:T(8,128)(2,1)S(1)}, bf16[16,7168]{1,0:T(8,128)(2,1)S(1)}, f32[7168,128]{1,0:T(8,128)}, f32[7168,128]{1,0:T(8,128)}) conditional(s32[]{:T(128)} %convert_element_type.191, () %tuple.111, (pred[]{:T(512)}, s32[]{:T(128)}, bf16[128,7168]{1,0:T(8,128)(2,1)}, bf16[16,7168]{1,0:T(8,128)(2,1)S(1)}, ...), branch_computations={%region_7.7_spmd, %region_8.12_spmd} | conditional | flops 394500224 | bytes 80659008 | solution.py:150
  763.5 21.2 %conditional.6 = (bf16[16,7168]{1,0:T(8,128)(2,1)S(1)}, bf16[16,7168]{1,0:T(8,128)(2,1)S(1)}, f32[7168,128]{1,0:T(8,128)}, f32[7168,128]{1,0:T(8,128)}) conditional(s32[]{:T(128)} %convert_element_type.191, () %tuple.111, (pred[]{:T(512)}, s32[]{:T(128)}, bf16[128,7168]{1,0:T(8,128)(2,1)}, bf16[16,7168]{1,0:T(8,128)(2,1)S(1)}, ...), branch_computations={%region_7.7_spmd, %region_8.12_spmd} | conditional | flops 394500224 | bytes 80659008 | solution.py:150
  787.3 8.9 select_add_fusion.3
  798.7 21.2 %conditional.6 = (bf16[16,7168]{1,0:T(8,128)(2,1)S(1)}, bf16[16,7168]{1,0:T(8,128)(2,1)S(1)}, f32[7168,128]{1,0:T(8,128)}, f32[7168,128]{1,0:T(8,128)}) conditional(s32[]{:T(128)} %convert_element_type.191, () %tuple.111, (pred[]{:T(512)}, s32[]{:T(128)}, bf16[128,7168]{1,0:T(8,128)(2,1)}, bf16[16,7168]{1,0:T(8,128)(2,1)S(1)}, ...), branch_computations={%region_7.7_spmd, %region_8.12_spmd} | conditional | flops 394500224 | bytes 80659008 | solution.py:150
  832.2 169.7 %reduce-scatter.3.cloned.1.call-done = f32[224,128]{1,0:T(8,128)} async-done(((f32[7168,128]{1,0:T(8,128)}), f32[224,128]{1,0:T(8,128)}) %reduce-scatter.3.cloned.1.call-update) | async-done | bytes 114704 | tf_op jit(solution)/shard_map/reduce_scatter | solution.py:191
  1001.9 173.5 %reduce-scatter.5.cloned.1.call-done = f32[224,128]{1,0:T(8,128)} async-done(((f32[7168,128]{1,0:T(8,128)}), f32[224,128]{1,0:T(8,128)}) %reduce-scatter.5.cloned.1.call-update) | async-done | bytes 114704 | tf_op jit(solution)/shard_map/reduce_scatter | solution.py:192
  (558 shorter events, 695.8 us)
Async XLA Ops:
  7.2 994.7 %reduce-scatter.3.cloned.1.call-start = ((), (), s32[]{:S(2)}) async-start(), calls=%async_computation.2 | async-start | bytes 3784704 | tf_op jit(solution)/shard_map/reduce_scatter | solution.py:191
  98.5 14.8 %collective-permute-start = (bf16[16,7168]{1,0:T(8,128)(2,1)S(1)}, bf16[16,7168]{1,0:T(8,128)(2,1)S(1)}, u32[]{:S(2)}, u32[]{:S(2)}) collective-permute-start(bf16[16,7168]{1,0:T(8,128)(2,1)S(1)} %get-tuple-element.766), channel_id=1, source_target_pairs={{0,32},{32,64},{64,96},{96,128},{128,160},{160,192},{192,224},{1,3... | collective-permute-start | bytes 688136 | tf_op jit(solution)/shard_map/while/body/eval_jaxpr/ppermute | solution.py:16
  149.1 14.1 %collective-permute-start = (bf16[16,7168]{1,0:T(8,128)(2,1)S(1)}, bf16[16,7168]{1,0:T(8,128)(2,1)S(1)}, u32[]{:S(2)}, u32[]{:S(2)}) collective-permute-start(bf16[16,7168]{1,0:T(8,128)(2,1)S(1)} %get-tuple-element.766), channel_id=1, source_target_pairs={{0,32},{32,64},{64,96},{96,128},{128,160},{160,192},{192,224},{1,3... | collective-permute-start | bytes 688136 | tf_op jit(solution)/shard_map/while/body/eval_jaxpr/ppermute | solution.py:16
  175.6 11.9 %collective-permute-start = (bf16[16,7168]{1,0:T(8,128)(2,1)S(1)}, bf16[16,7168]{1,0:T(8,128)(2,1)S(1)}, u32[]{:S(2)}, u32[]{:S(2)}) collective-permute-start(bf16[16,7168]{1,0:T(8,128)(2,1)S(1)} %get-tuple-element.766), channel_id=1, source_target_pairs={{0,32},{32,64},{64,96},{96,128},{128,160},{160,192},{192,224},{1,3... | collective-permute-start | bytes 688136 | tf_op jit(solution)/shard_map/while/body/eval_jaxpr/ppermute | solution.py:16
  193.0 20.1 %collective-permute-start = (bf16[16,7168]{1,0:T(8,128)(2,1)S(1)}, bf16[16,7168]{1,0:T(8,128)(2,1)S(1)}, u32[]{:S(2)}, u32[]{:S(2)}) collective-permute-start(bf16[16,7168]{1,0:T(8,128)(2,1)S(1)} %get-tuple-element.766), channel_id=1, source_target_pairs={{0,32},{32,64},{64,96},{96,128},{128,160},{160,192},{192,224},{1,3... | collective-permute-start | bytes 688136 | tf_op jit(solution)/shard_map/while/body/eval_jaxpr/ppermute | solution.py:16
  218.6 18.8 %collective-permute-start = (bf16[16,7168]{1,0:T(8,128)(2,1)S(1)}, bf16[16,7168]{1,0:T(8,128)(2,1)S(1)}, u32[]{:S(2)}, u32[]{:S(2)}) collective-permute-start(bf16[16,7168]{1,0:T(8,128)(2,1)S(1)} %get-tuple-element.766), channel_id=1, source_target_pairs={{0,32},{32,64},{64,96},{96,128},{128,160},{160,192},{192,224},{1,3... | collective-permute-start | bytes 688136 | tf_op jit(solution)/shard_map/while/body/eval_jaxpr/ppermute | solution.py:16
  225.3 13.4 %collective-permute-start.1 = (bf16[16,7168]{1,0:T(8,128)(2,1)}, bf16[16,7168]{1,0:T(8,128)(2,1)S(1)}, u32[]{:S(2)}, u32[]{:S(2)}) collective-permute-start(bf16[16,7168]{1,0:T(8,128)(2,1)} %copy-done.6), channel_id=1, source_target_pairs={{0,32},{32,64},{64,96},{96,128},{128,160},{160,192},{192,224},{1,3... | collective-permute-start | bytes 688136 | tf_op jit(solution)/shard_map/while/body/eval_jaxpr/ppermute | solution.py:16
  242.9 13.2 %collective-permute-start = (bf16[16,7168]{1,0:T(8,128)(2,1)S(1)}, bf16[16,7168]{1,0:T(8,128)(2,1)S(1)}, u32[]{:S(2)}, u32[]{:S(2)}) collective-permute-start(bf16[16,7168]{1,0:T(8,128)(2,1)S(1)} %get-tuple-element.766), channel_id=1, source_target_pairs={{0,32},{32,64},{64,96},{96,128},{128,160},{160,192},{192,224},{1,3... | collective-permute-start | bytes 688136 | tf_op jit(solution)/shard_map/while/body/eval_jaxpr/ppermute | solution.py:16
  261.7 18.7 %collective-permute-start = (bf16[16,7168]{1,0:T(8,128)(2,1)S(1)}, bf16[16,7168]{1,0:T(8,128)(2,1)S(1)}, u32[]{:S(2)}, u32[]{:S(2)}) collective-permute-start(bf16[16,7168]{1,0:T(8,128)(2,1)S(1)} %get-tuple-element.766), channel_id=1, source_target_pairs={{0,32},{32,64},{64,96},{96,128},{128,160},{160,192},{192,224},{1,3... | collective-permute-start | bytes 688136 | tf_op jit(solution)/shard_map/while/body/eval_jaxpr/ppermute | solution.py:16
  285.9 16.8 %collective-permute-start = (bf16[16,7168]{1,0:T(8,128)(2,1)S(1)}, bf16[16,7168]{1,0:T(8,128)(2,1)S(1)}, u32[]{:S(2)}, u32[]{:S(2)}) collective-permute-start(bf16[16,7168]{1,0:T(8,128)(2,1)S(1)} %get-tuple-element.766), channel_id=1, source_target_pairs={{0,32},{32,64},{64,96},{96,128},{128,160},{160,192},{192,224},{1,3... | collective-permute-start | bytes 688136 | tf_op jit(solution)/shard_map/while/body/eval_jaxpr/ppermute | solution.py:16
  291.3 12.6 %collective-permute-start.1 = (bf16[16,7168]{1,0:T(8,128)(2,1)}, bf16[16,7168]{1,0:T(8,128)(2,1)S(1)}, u32[]{:S(2)}, u32[]{:S(2)}) collective-permute-start(bf16[16,7168]{1,0:T(8,128)(2,1)} %copy-done.6), channel_id=1, source_target_pairs={{0,32},{32,64},{64,96},{96,128},{128,160},{160,192},{192,224},{1,3... | collective-permute-start | bytes 688136 | tf_op jit(solution)/shard_map/while/body/eval_jaxpr/ppermute | solution.py:16
  308.2 14.5 %collective-permute-start = (bf16[16,7168]{1,0:T(8,128)(2,1)S(1)}, bf16[16,7168]{1,0:T(8,128)(2,1)S(1)}, u32[]{:S(2)}, u32[]{:S(2)}) collective-permute-start(bf16[16,7168]{1,0:T(8,128)(2,1)S(1)} %get-tuple-element.766), channel_id=1, source_target_pairs={{0,32},{32,64},{64,96},{96,128},{128,160},{160,192},{192,224},{1,3... | collective-permute-start | bytes 688136 | tf_op jit(solution)/shard_map/while/body/eval_jaxpr/ppermute | solution.py:16
  328.1 13.2 %collective-permute-start = (bf16[16,7168]{1,0:T(8,128)(2,1)S(1)}, bf16[16,7168]{1,0:T(8,128)(2,1)S(1)}, u32[]{:S(2)}, u32[]{:S(2)}) collective-permute-start(bf16[16,7168]{1,0:T(8,128)(2,1)S(1)} %get-tuple-element.766), channel_id=1, source_target_pairs={{0,32},{32,64},{64,96},{96,128},{128,160},{160,192},{192,224},{1,3... | collective-permute-start | bytes 688136 | tf_op jit(solution)/shard_map/while/body/eval_jaxpr/ppermute | solution.py:16
  364.8 13.8 %collective-permute-start.2 = (bf16[16,7168]{1,0:T(8,128)(2,1)S(1)}, bf16[16,7168]{1,0:T(8,128)(2,1)S(1)}, u32[]{:S(2)}, u32[]{:S(2)}) collective-permute-start(bf16[16,7168]{1,0:T(8,128)(2,1)S(1)} %get-tuple-element.785), channel_id=1, source_target_pairs={{32,0},{64,32},{96,64},{128,96},{160,128},{192,160},{224,192},{33,... | collective-permute-start | bytes 688136 | tf_op jit(solution)/shard_map/while/body/eval_jaxpr/ppermute | solution.py:16
  366.1 14.4 %collective-permute-start.3 = (bf16[16,7168]{1,0:T(8,128)(2,1)S(1)}, bf16[16,7168]{1,0:T(8,128)(2,1)S(1)}, u32[]{:S(2)}, u32[]{:S(2)}) collective-permute-start(bf16[16,7168]{1,0:T(8,128)(2,1)S(1)} %get-tuple-element.786), channel_id=1, source_target_pairs={{32,0},{64,32},{96,64},{128,96},{160,128},{192,160},{224,192},{33,... | collective-permute-start | bytes 688136 | tf_op jit(solution)/shard_map/while/body/eval_jaxpr/ppermute | solution.py:16
  386.1 11.5 collective-permute-start.2
  404.4 11.5 collective-permute-start.2
  422.8 11.5 collective-permute-start.2
  441.2 11.5 collective-permute-start.2
  459.5 89.4 %collective-permute-start.2 = (bf16[16,7168]{1,0:T(8,128)(2,1)S(1)}, bf16[16,7168]{1,0:T(8,128)(2,1)S(1)}, u32[]{:S(2)}, u32[]{:S(2)}) collective-permute-start(bf16[16,7168]{1,0:T(8,128)(2,1)S(1)} %get-tuple-element.785), channel_id=1, source_target_pairs={{32,0},{64,32},{96,64},{128,96},{160,128},{192,160},{224,192},{33,... | collective-permute-start | bytes 688136 | tf_op jit(solution)/shard_map/while/body/eval_jaxpr/ppermute | solution.py:16
  460.8 90.1 %collective-permute-start.3 = (bf16[16,7168]{1,0:T(8,128)(2,1)S(1)}, bf16[16,7168]{1,0:T(8,128)(2,1)S(1)}, u32[]{:S(2)}, u32[]{:S(2)}) collective-permute-start(bf16[16,7168]{1,0:T(8,128)(2,1)S(1)} %get-tuple-element.786), channel_id=1, source_target_pairs={{32,0},{64,32},{96,64},{128,96},{160,128},{192,160},{224,192},{33,... | collective-permute-start | bytes 688136 | tf_op jit(solution)/shard_map/while/body/eval_jaxpr/ppermute | solution.py:16
  714.3 11.5 collective-permute-start.2
  784.7 11.5 collective-permute-start.2
  831.5 344.0 %reduce-scatter.5.cloned.1.call-start = ((), (), s32[]{:S(2)}) async-start(), calls=%async_computation.3 | async-start | bytes 3784704 | tf_op jit(solution)/shard_map/reduce_scatter | solution.py:192
  (94 other events, 438.6 us)
Sparse Core Ops, SparseCore 0:
  831.6 170.2 reduce-scatter.2
  1005.2 170.2 reduce-scatter.4
where the time goes:
time: 1190 us; the launch traced here: 1180 us
  waiting for transfers between devices  463 us (39%)
  starting transfers between devices  233 us (20%)
  other arithmetic  195 us (16%)
  matrix products  184 us (15%)
  local copies, waits for them, and re-layouts  70.1 us (6%)
  loops' own time  22.5 us (2%)
  between operations  14.1 us (1%)
    ppermute x60, starting transfers between devices, shifted(): lax.ppermute(value, axis, [(source, source + steps) for source in range(i...  233 us
    reduce_scatter x1, waiting for transfers between devices, on_device(): lax.psum_scatter(sum_out, 'dp', scatter_dimension=0, tiled=True)  174 us
    reduce_scatter x1, waiting for transfers between devices, on_device(): lax.psum_scatter(sum_in, 'dp', scatter_dimension=0, tiled=True)  170 us
    add x15, other arithmetic, backward_part(): return (grad_x, grad_xt, sum_in + term_in, sum_out + term_out)  131 us
    ppermute x60, waiting for transfers between devices, shifted(): lax.ppermute(value, axis, [(source, source + steps) for source in range(i...  119 us
    dot_general x48, matrix products, matmul_last(): lax.dot_general(left, right, (((1,), (1,)), ((), ())), preferred_element_...  69.5 us
    dot_general x32, matrix products, matmul_rows(): lax.dot_general(left, right, (((0,), (0,)), ((), ())), preferred_element_...  61.8 us
    dot_general x64, matrix products, matmul(): return jnp.dot(left, right, preferred_element_type=jnp.float32)  53 us
  transfers between devices with their start and end apart: 62, of which 33 were waited for; matrix products, arithmetic and copies ran while one was open for 11% of the time, Pallas kernels for 0%

commit v1 on v0

v1 whole, which is shorter than its diff:
```python
import functools

import jax
import jax.numpy as jnp
from jax import lax
from jax.experimental import pallas as pl
from jax.experimental.pallas import tpu as pltpu
from jax.sharding import Mesh, PartitionSpec as P

EPS = 1e-05
R = 128
SECTIONS = 8
BLOCKS = 24
SEC = ("zh", "c")
DP = ("y", "x", "zl")
BF = jnp.bfloat16
F32 = jnp.float32


def mm(left, right):
    return jnp.dot(left, right, preferred_element_type=F32)


def mm_nt(left, right):
    return lax.dot_general(left, right, (((1,), (1,)), ((), ())), preferred_element_type=F32)


def mm_tn(left, right):
    return lax.dot_general(left, right, (((0,), (0,)), ((), ())), preferred_element_type=F32)


def call(kernel, **kw):
    return pl.pallas_call(kernel, **kw)


def project_kernel(x_ref, c_ref, a_ref, p_ref, b_ref, q_ref, out_ref, ss_ref, acc, acc_ss):
    step = pl.program_id(0)

    @pl.when(step == 0)
    def _():
        acc[...] = jnp.zeros_like(acc)
        acc_ss[...] = jnp.zeros_like(acc_ss)

    x = x_ref[...]
    rows = x.shape[0]
    x32 = x.astype(F32)
    acc_ss[...] += jnp.sum(x32 * x32, axis=-1, keepdims=True)
    ap = jnp.concatenate([a_ref[0], p_ref[0]], axis=1)
    bq = jnp.concatenate([b_ref[0], q_ref[0]], axis=1)
    acc[:, : 2 * R] += mm(x, ap)
    both = mm(jnp.concatenate([x, c_ref[...]], axis=0), bq)
    acc[:, 2 * R : 4 * R] += both[:rows]
    acc[:, 4 * R :] += both[rows:]

    @pl.when(step == pl.num_programs(0) - 1)
    def _():
        out_ref[...] = acc[...].astype(BF)
        ss_ref[...] = acc_ss[...]


def project(x, c, a, p, b, q):
    rows, width = x.shape
    block = width // 7
    wide = pl.BlockSpec((rows, block), lambda k: (0, k))
    weight = pl.BlockSpec((1, block, R), lambda k: (0, k, 0))
    return call(
        project_kernel,
        grid=(7,),
        in_specs=[wide, wide, weight, weight, weight, weight],
        out_specs=[
            pl.BlockSpec((rows, 6 * R), lambda k: (0, 0)),
            pl.BlockSpec((rows, R), lambda k: (0, 0)),
        ],
        out_shape=[
            jax.ShapeDtypeStruct((rows, 6 * R), BF),
            jax.ShapeDtypeStruct((rows, R), F32),
        ],
        scratch_shapes=[pltpu.VMEM((rows, 6 * R), F32), pltpu.VMEM((rows, R), F32)],
        compiler_params=pltpu.CompilerParams(vmem_limit_bytes=32 * 1024 * 1024),
        cost_estimate=pl.CostEstimate(
            flops=2 * rows * width * 6 * R,
            bytes_accessed=4 * rows * width + 8 * width * R,
            transcendentals=0,
        ),
    )(x, c, a, p, b, q)


def gram_kernel(me_ref, w_ref, out_ref):
    me = me_ref[0]

    def cols(section, names):
        return jnp.concatenate([w_ref[section, n] for n in names], axis=1)

    def put(at, block):
        out_ref[at * R : (at + 1) * R] = block.astype(BF)

    for k in range(1, 5):
        other = lax.rem(me + k, SECTIONS)
        low, high = jnp.minimum(me, other), jnp.maximum(me, other)
        right = cols(high, (0, 1, 2, 3))
        from_b = mm_tn(w_ref[low, 2], right)
        from_q = mm_tn(w_ref[low, 3], cols(high, (0, 2)))
        six = [from_b[:, i * R : (i + 1) * R] for i in range(4)]
        six += [from_q[:, i * R : (i + 1) * R] for i in range(2)]
        if k < 4:
            for i in range(6):
                put((k - 1) * 6 + i, six[i])
        else:
            first = me < 4
            for i in range(3):
                put(18 + i, jnp.where(first, six[i], six[3 + i]))
    own = mm_tn(w_ref[me, 2], cols(me, (2, 3)))
    put(21, own[:, :R])
    put(22, own[:, R:])
    put(23, jnp.zeros((R, R), F32))


def gram(me, w_all):
    return call(
        gram_kernel,
        in_specs=[
            pl.BlockSpec(memory_space=pltpu.SMEM),
            pl.BlockSpec(memory_space=pltpu.VMEM),
        ],
        out_specs=pl.BlockSpec(memory_space=pltpu.VMEM),
        out_shape=jax.ShapeDtypeStruct((BLOCKS * R, R), BF),
        compiler_params=pltpu.CompilerParams(vmem_limit_bytes=32 * 1024 * 1024),
        cost_estimate=pl.CostEstimate(
            flops=2 * w_all.shape[2] * BLOCKS * R * R,
            bytes_accessed=w_all.size * 2,
            transcendentals=0,
        ),
    )(me, w_all)


def place(low, high):
    gap = high - low
    if gap <= 3:
        return [(low, (gap - 1) * 6 + i) for i in range(6)]
    if gap == 4:
        return [(low, 18 + i) for i in range(3)] + [(high, 18 + i) for i in range(3)]
    return [(high, (7 - gap) * 6 + i) for i in range(6)]


def relay_kernel(axes, piece, width, pxc_ref, ss_ref, g_hbm, out_ref, g, sem, saved, left, dleft):
    nzh, nc, ny, nx, nzl = axes
    ndp = ny * nx * nzl

    def fetch(index, _):
        zl = lax.rem(index, nzl)
        zh = lax.rem(index // nzl, nzh)
        x = lax.rem(index // (nzl * nzh), nx)
        y = lax.rem(index // (nzl * nzh * nx), ny)
        c = index // (nzl * nzh * nx * ny)
        owner = zh * nc + c
        dp = (y * nx + x) * nzl + zl
        pltpu.make_async_copy(
            g_hbm.at[pl.ds(pl.multiple_of(index * piece, 16), piece)],
            g.at[pl.ds(pl.multiple_of((owner * ndp + dp) * piece, 16), piece)],
            sem,
        ).start()
        return 0

    lax.fori_loop(0, SECTIONS * ndp, fetch, 0)
    pltpu.make_async_copy(g_hbm, g, sem).wait()

    def block(at):
        start = (at[0] * BLOCKS + at[1]) * R
        return g[start : start + R]

    rows = pxc_ref.shape[1]
    ss = ss_ref[...][:, :1]
    st = jnp.zeros_like(ss)
    rsum = lambda v: jnp.sum(v, axis=-1, keepdims=True)
    hs, dhs, scales, mus = [], [], [], []
    for s in range(SECTIONS):
        base = pxc_ref[s][:, : 4 * R].astype(F32)
        prim, tan = base, None
        if s:
            both = None
            from_q = None
            for j in range(s):
                at = place(j, s)
                right = jnp.concatenate([block(at[i]) for i in range(4)], axis=1)
                part = mm(jnp.concatenate([hs[j], dhs[j]], axis=0), right)
                both = part if both is None else both + part
                rq = jnp.concatenate([block(at[4]), block(at[5])], axis=1)
                part = mm(hs[j], rq)
                from_q = part if from_q is None else from_q + part
            prim = base + both[:rows]
            ta = both[rows:, :R] + from_q[:, :R]
            tb = both[rows:, 2 * R : 3 * R] + from_q[:, R:]
        else:
            ta = tb = jnp.zeros((rows, R), F32)
        xa, xp = prim[:, :R], prim[:, R : 2 * R]
        r = lax.rsqrt(ss / width + EPS)
        mu = r * r * r * (st / width)
        pre = r * xa
        dpre = r * (ta + xp) - mu * xa
        sig = 1.0 / (1.0 + jnp.exp(-pre))
        slope = sig * (1.0 + pre * (1.0 - sig))
        bend = sig * (1.0 - sig) * (2.0 + pre * (1.0 - 2.0 * sig))
        h = (pre * sig).astype(BF)
        dh = (slope * dpre).astype(BF)
        hs.append(h)
        dhs.append(dh)
        scales.append(r)
        mus.append(mu)
        own = jnp.concatenate([block((s, 21)), block((s, 22))], axis=1)
        step = mm(h, own)
        xb_new = prim[:, 2 * R : 3 * R] + step[:, :R]
        xq_new = prim[:, 3 * R :] + step[:, R:]
        tb_new = tb + mm(dh, block((s, 21))) + mm_nt(h, block((s, 22)))
        h32, dh32 = h.astype(F32), dh.astype(F32)
        ss = ss + rsum(h32 * (prim[:, 2 * R : 3 * R] + xb_new))
        st = st + rsum(dh32 * xb_new + h32 * (xq_new + tb))
        for i, value in enumerate((xa, ta + xp, xb_new, xq_new, tb_new, slope, bend * dpre)):
            saved[s, i] = value
        out_ref[s, 0] = h
        out_ref[s, 1] = dh

    total = jnp.zeros_like(ss)
    dtotal = jnp.zeros_like(ss)
    for s in reversed(range(SECTIONS)):
        xa, xd, xb_new, xq_new, tb_new, slope, curve = [saved[s, i] for i in range(7)]
        fresh = pxc_ref[s][:, 4 * R :].astype(F32)
        gb = fresh[:, :R] - total * xb_new
        gq = fresh[:, R:] - total * xq_new
        dgb = -(dtotal * xb_new + total * tb_new)
        for i in range(s + 1, SECTIONS):
            at = place(s, i)
            right = jnp.concatenate([block(at[n]) for n in range(4)], axis=1)
            both = mm_nt(jnp.concatenate([left[i], dleft[i]], axis=0), right)
            gb = gb + both[:rows]
            dgb = dgb + both[rows:]
            rq = jnp.concatenate([block(at[4]), block(at[5])], axis=1)
            li = left[i]
            gq = gq + mm_nt(jnp.concatenate([li[:, :R], li[:, 2 * R : 3 * R]], axis=1), rq)
        dgh = dgb + gq
        ga = gb * slope
        dga = dgh * slope + gb * curve
        r, mu = scales[s], mus[s]
        u = (r * dga - mu * ga).astype(BF)
        v = (r * ga).astype(BF)
        h, dh = hs[s], dhs[s]
        h32, dh32 = h.astype(F32), dh.astype(F32)
        z = (-total * h32).astype(BF)
        y = (-(dtotal * h32 + total * dh32)).astype(BF)
        zero = jnp.zeros_like(z)
        left[s] = jnp.concatenate([v, zero, z, zero], axis=1)
        dleft[s] = jnp.concatenate([u, v, y, z], axis=1)
        out_ref[s, 2] = u
        out_ref[s, 3] = v
        out_ref[s, 4] = z
        out_ref[s, 5] = y
        inner = rsum(ga * xa) / width
        dinner = rsum(dga * xa + ga * xd) / width
        total = total + r * r * r * inner
        dtotal = dtotal + r * r * r * dinner - 3.0 * r * r * mu * inner


def relay(axes, width, pxc, ss, g):
    rows = pxc.shape[1]
    piece = g.shape[0] // (axes[0] * axes[1] * axes[2] * axes[3] * axes[4])
    vm = pl.BlockSpec(memory_space=pltpu.VMEM)
    return call(
        functools.partial(relay_kernel, axes, piece, float(width)),
        in_specs=[vm, vm, pl.BlockSpec(memory_space=pl.ANY)],
        out_specs=vm,
        out_shape=jax.ShapeDtypeStruct((SECTIONS, 6, rows, R), BF),
        scratch_shapes=[
            pltpu.VMEM(g.shape, BF),
            pltpu.SemaphoreType.DMA,
            pltpu.VMEM((SECTIONS, 7, rows, R), F32),
            pltpu.VMEM((SECTIONS, rows, 4 * R), BF),
            pltpu.VMEM((SECTIONS, rows, 4 * R), BF),
        ],
        compiler_params=pltpu.CompilerParams(vmem_limit_bytes=48 * 1024 * 1024),
        cost_estimate=pl.CostEstimate(
            flops=2 * 28 * 20 * rows * R * R, bytes_accessed=g.size * 2, transcendentals=0
        ),
    )(pxc, ss, g)


def terms_kernel(me_ref, x_ref, c_ref, own_ref, other_ref, out_ref):
    me = me_ref[0]
    i = pl.program_id(0)
    part = out_ref.shape[0]
    slab = x_ref.shape[1] // part
    h, dh, u, v, z, y = [own_ref[0, n] for n in range(6)]
    hi, dhi, ui, vi, zi, yi = [other_ref[0, n] for n in range(6)]
    from_x = mm_tn(x_ref[...], jnp.concatenate([u, y], axis=1))
    from_c = mm_tn(c_ref[...], dh)
    t_in = from_x[:, :R].astype(BF)
    t_out = (from_x[:, R:] + from_c).astype(BF)
    for n in range(part):
        out_ref[n, :slab] = t_in[n * slab : (n + 1) * slab]
        out_ref[n, slab : 2 * slab] = t_out[n * slab : (n + 1) * slab]

    below = i < me
    upto = i <= me

    def pair(p0, p1, r0, r1):
        wide = mm_tn(p0, jnp.concatenate([r0, r1], axis=1))
        return wide[:, :R] + mm_tn(p1, r1), wide[:, R:]

    m0, m1 = pair(
        jnp.where(below, hi, vi),
        jnp.where(below, dhi, ui),
        jnp.where(below, u, dh),
        jnp.where(below, v, h),
    )
    m2, m3 = pair(
        jnp.where(upto, hi, zi),
        jnp.where(upto, dhi, yi),
        jnp.where(upto, y, dh),
        jnp.where(upto, z, h),
    )
    keep = i != me
    four = [jnp.where(keep, m0, 0.0), jnp.where(keep, m1, 0.0), m2, m3]
    each = 4 // part
    for n in range(part):
        for e in range(each):
            out_ref[n, 2 * slab + e * R : 2 * slab + (e + 1) * R] = four[n * each + e].astype(BF)


def terms(me, ndp, x, c, coef):
    rows, width = x.shape
    part = ndp // SECTIONS
    slab = width // ndp
    high = 2 * slab + 4 // part * R
    block = width // SECTIONS
    wide = pl.BlockSpec((rows, block), lambda i, me: (0, i))
    one = (1, 6, rows, R)
    return call(
        terms_kernel,
        grid_spec=pltpu.PrefetchScalarGridSpec(
            num_scalar_prefetch=1,
            grid=(SECTIONS,),
            in_specs=[
                wide,
                wide,
                pl.BlockSpec(one, lambda i, me: (me[0], 0, 0, 0)),
                pl.BlockSpec(one, lambda i, me: (i, 0, 0, 0)),
            ],
            out_specs=pl.BlockSpec((part, high, R), lambda i, me: (i, 0, 0)),
        ),
        out_shape=jax.ShapeDtypeStruct((ndp, high, R), BF),
        compiler_params=pltpu.CompilerParams(vmem_limit_bytes=32 * 1024 * 1024),
        cost_estimate=pl.CostEstimate(
            flops=2 * rows * width * 3 * R, bytes_accessed=8 * rows * width, transcendentals=0
        ),
    )(me, x, c, coef, coef)


def finish_kernel(me_ref, t_ref, w_ref, m_ref, in_ref, out_ref):
    me = me_ref[0]
    slab = w_ref.shape[2]
    t_in, t_out = t_ref[:slab], t_ref[slab:]
    for i in range(SECTIONS):
        below = i < me
        a, p, b, q = [w_ref[i, n] for n in range(4)]
        first = jnp.concatenate([jnp.where(below, b, a), jnp.where(below, q, p)], axis=1)
        product = mm(first, m_ref[i, : 2 * R])
        t_in = t_in + jnp.where(below, product, 0.0)
        t_out = t_out + jnp.where(below, 0.0, product)
        t_out = t_out + mm(jnp.concatenate([b, q], axis=1), m_ref[i, 2 * R :])
    in_ref[...] = w_ref[me, 1].astype(F32) * t_in
    out_ref[...] = w_ref[me, 3].astype(F32) * t_out


def finish(me, t, w_all, m):
    vm = pl.BlockSpec(memory_space=pltpu.VMEM)
    shape = jax.ShapeDtypeStruct((w_all.shape[2], R), F32)
    return call(
        finish_kernel,
        in_specs=[pl.BlockSpec(memory_space=pltpu.SMEM), vm, vm, vm],
        out_specs=[vm, vm],
        out_shape=[shape, shape],
        compiler_params=pltpu.CompilerParams(vmem_limit_bytes=32 * 1024 * 1024),
    )(me, t, w_all, m)


def on_device(axes, inputs, cotangent, adapt_in, adapt_out, probe_in, probe_out):
    nzh, nc, ny, nx, nzl = axes
    ndp = ny * nx * nzl
    rows, width = inputs.shape
    slab = width // ndp
    me = lax.axis_index(SEC).astype(jnp.int32).reshape(1)
    dp = lax.axis_index(DP)

    own = jnp.stack(
        [
            lax.dynamic_slice_in_dim(w[0], dp * slab, slab, 0)
            for w in (adapt_in, probe_in, adapt_out, probe_out)
        ]
    )
    w_all = lax.all_gather(own, SEC)
    projected, ss = project(inputs, cotangent, adapt_in, probe_in, adapt_out, probe_out)
    pxc = lax.all_gather(projected, SEC)

    partial = gram(me, w_all)
    arrived = lax.all_to_all(partial.reshape(ndp, -1, R), DP, 0, 0, tiled=True)
    piece = jnp.sum(arrived.astype(F32), axis=0).astype(BF)
    line = lax.all_gather(piece, ("zh", "zl"), tiled=True)
    g = lax.all_gather(line, ("c", "y", "x"), tiled=True)

    coef = relay(axes, width, pxc, ss, g)
    mine = terms(me, ndp, inputs, cotangent, coef)
    arrived = lax.all_to_all(mine, DP, 0, 0, tiled=True)
    total = jnp.sum(arrived.astype(F32), axis=0)
    m_own = total[2 * slab :].astype(BF)
    m_all = lax.all_to_all(jnp.broadcast_to(m_own[None], (ndp,) + m_own.shape), DP, 0, 0, tiled=True)
    m_all = m_all.reshape(SECTIONS, 4 * R, R)
    diag_in, diag_out = finish(me, total[: 2 * slab], w_all, m_all)
    return diag_in[None], diag_out[None]


def solution(mesh, axes=(4, 2, 4, 4, 2)):
    fine = Mesh(mesh.devices.reshape(axes), SEC + DP)
    tokens, weights = P(DP, None), P(SEC, None, None)
    return jax.shard_map(
        functools.partial(on_device, axes),
        mesh=fine,
        in_specs=(tokens, tokens, weights, weights, weights, weights),
        out_specs=(P(SEC, DP, None), P(SEC, DP, None)),
        check_vma=False,
    )
```

time: 1190 us -> 273 us (0.23)
  waiting for transfers between devices: 463 us -> 88.2 us
  starting transfers between devices: 233 us -> 5.11 us
  other arithmetic: 195 us -> 1.49 us
  matrix products: 184 us -> 0 us
  blocking collectives: 0 us -> 123 us
  local copies, waits for them, and re-layouts: 70.1 us -> 14.9 us
  Pallas kernels: 0 us -> 25.5 us
  loops' own time: 22.5 us -> 0 us
    reduce_scatter x2 -> x0, waiting for transfers between devices: 343 us -> none  [the longest x1 174 us: on_device(): lax.psum_scatter(sum_out, 'dp', scatter_dimension=0, tiled=True)]
    ppermute x60 -> x0, starting transfers between devices: 233 us -> none  [shifted(): lax.ppermute(value, axis, [(source, source + steps) for source in range(i...]
    dot_general x144 -> x0, matrix products: 184 us -> none  [the longest x48 69.5 us: matmul_last(): lax.dot_general(left, right, (((1,), (1,)), ((), ())), preferred_element_...]
    add x15 -> x0, other arithmetic: 131 us -> none  [backward_part(): return (grad_x, grad_xt, sum_in + term_in, sum_out + term_out)]
    ppermute x60 -> x0, waiting for transfers between devices: 119 us -> none  [shifted(): lax.ppermute(value, axis, [(source, source + steps) for source in range(i...]
    all_to_all x0 -> x2, blocking collectives: none -> 96.1 us  [the longest x1 63.1 us: on_device(): arrived = lax.all_to_all(mine, DP, 0, 0, tiled=True)]
    all_gather x0 -> x3, waiting for transfers between devices: none -> 72.1 us  [the longest x1 47.6 us: on_device(): g = lax.all_gather(line, ('c', 'y', 'x'), tiled=True)]
    select_n x23 -> x0, other arithmetic: 41 us -> none  [the longest x15 31.9 us: forward_part(): jnp.where(active, lax.dynamic_update_index_in_dim(stash_t, tangent, slot_...]
  transfers between devices with their start and end apart: 62 -> 4, of which waited for: 33 -> 3; matrix products, arithmetic and copies ran while one was open for 11% -> 0% of each run, Pallas kernels for 0% -> 2%
where the time goes in v1:
time: 273 us; the launch traced here: 272 us
  blocking collectives  123 us (45%)
  waiting for transfers between devices  88.2 us (32%)
  Pallas kernels  25.5 us (9%)
  local copies, waits for them, and re-layouts  14.9 us (5%)
  between operations  13.9 us (5%)
  starting transfers between devices  5.11 us (2%)
    all_to_all x1, blocking collectives, on_device(): arrived = lax.all_to_all(mine, DP, 0, 0, tiled=True)  63.1 us
    all_gather x1, waiting for transfers between devices, on_device(): g = lax.all_gather(line, ('c', 'y', 'x'), tiled=True)  47.6 us
    all_to_all x1, blocking collectives, on_device(): arrived = lax.all_to_all(partial.reshape(ndp, -1, R), DP, 0, 0, tiled=True)  33 us
    all_gather x1, blocking collectives, on_device(): line = lax.all_gather(piece, ('zh', 'zl'), tiled=True)  26.7 us
    all_gather x1, waiting for transfers between devices, on_device(): w_all = lax.all_gather(own, SEC)  24.5 us
    pallas_call x1, Pallas kernels, relay(): call(functools.partial(relay_kernel, axes, piece, float(width)), in_specs...  16.1 us
    all_to_all x1, waiting for transfers between devices, on_device(): lax.all_to_all(jnp.broadcast_to(m_own[None], (ndp,) + m_own.shape), DP, 0...  16 us
    unnamed x22, local copies, waits for them, and re-layouts  11.9 us
  transfers between devices with their start and end apart: 4, of which 3 were waited for; matrix products, arithmetic and copies ran while one was open for 0% of the time, Pallas kernels for 2%

profile of v1, /device:TPU:2, one launch (start us, length us, event | category | flops | bytes accessed | tf_op | source)
XLA Modules:
  0.0 271.9 jit_solution(16203143396753091974)
XLA Ops:
  7.2 0.9 constant_dynamic-slice_fusion.2
  8.1 0.9 constant_dynamic-slice_fusion
  8.9 0.7 pad_maximum_fusion
  9.7 1.5 copy-done.2
  11.2 1.5 copy-done.4
  12.7 1.5 copy-done.6
  14.2 1.5 copy-done.7
  15.7 1.5 copy-done.8
  17.2 1.5 copy-done.9
  18.7 3.7 %shard_map.77 = (bf16[128,768]{1,0:T(8,128)(2,1)}, f32[128,128]{1,0:T(8,128)S(1)}) custom-call(bf16[128,7168]{1,0:T(8,128)(2,1)S(1)} %copy-done.2, bf16[128,7168]{1,0:T(8,128)(2,1)S(1)} %copy-done.4, bf16[1,7168,128]{2,1,0:T(8,128)(2,1)S(1)} %copy-done.9, bf16[1,7168,128]{2,1,0:T(8,128)(2,1)S(1)} %copy-done.8, bf16[1,7168,128]{2,1,0:T(8,128)(2,1)S(1)} %copy-done.7, ...), custom_call_target="tpu_custom_call" | custom-call | flops 1409286144 | bytes 11010048 | tf_op jit(solution)/shard_map/pallas_call | solution.py:66
  22.5 24.5 %all-gather.10.cloned.1.call-done = bf16[32,224,128]{2,1,0:T(8,128)(2,1)} async-done(((bf16[4,224,128]{2,1,0:T(8,128)(2,1)}), bf16[32,224,128]{2,1,0:T(8,128)(2,1)}) %all-gather.10.cloned.1.call-update) | async-done | bytes 1835024 | tf_op jit(solution)/shard_map/all_gather | solution.py:398
  47.1 1.5 copy-done
  49.0 33.0 %all_to_all.15 = bf16[32,96,128]{2,1,0:T(8,128)(2,1)S(1)} all-to-all(bf16[32,96,128]{2,1,0:T(8,128)(2,1)S(1)} %bitcast.10), channel_id=1, replica_groups=mesh['zh'=4,'c'=2,'y'=4,'x'=4,'zl'=2] {'y','x','zl'}, dimensions={0} | all-to-all | bytes 1572864 | tf_op jit(solution)/shard_map/all_to_all | solution.py:403
  82.1 26.7 %all_gather.22 = bf16[768,128]{1,0:T(8,128)(2,1)} all-gather(bf16[96,128]{1,0:T(8,128)(2,1)S(1)} %reduce_sum.21), channel_id=1, replica_groups=mesh['zh'=4,'c'=2,'y'=4,'x'=4,'zl'=2] {'zh','zl'}, dimensions={0}, use_global_device_ids=true | all-gather | bytes 221184 | tf_op jit(solution)/shard_map/all_gather | solution.py:405
  108.9 47.6 %all-gather.6.cloned.1.call-done.g_hbm = bf16[24576,128]{1,0:T(8,128)(2,1)} async-done(((bf16[768,128]{1,0:T(8,128)(2,1)}), bf16[24576,128]{1,0:T(8,128)(2,1)}) %all-gather.6.cloned.1.call-update) | async-done | bytes 6291472 | tf_op jit(solution)/shard_map/all_gather | solution.py:406
  156.5 1.4 copy-done.10
  157.9 16.1 %shard_map.79.own_ref.other_ref = bf16[8,6,128,128]{3,2,1,0:T(8,128)(2,1)S(1)} custom-call(bf16[8,128,768]{2,1,0:T(8,128)(2,1)S(1)} %bitcast.11, f32[128,128]{1,0:T(8,128)S(1)} %get-tuple-element.7.ss_ref, bf16[24576,128]{1,0:T(8,128)(2,1)} %all-gather.6.cloned.1.call-done.g_hbm), custom_call_target="tpu_custom_call" | custom-call | flops 2348810240 | bytes 6291456 | tf_op jit(solution)/shard_map/pallas_call | solution.py:266
  174.0 3.9 %shard_map.80 = bf16[32,576,128]{2,1,0:T(8,128)(2,1)S(1)} custom-call(s32[1]{0:T(128)} %bitcast.me_ref, bf16[128,7168]{1,0:T(8,128)(2,1)S(1)} %copy-done.3, bf16[128,7168]{1,0:T(8,128)(2,1)S(1)} %copy-done.5, bf16[8,6,128,128]{3,2,1,0:T(8,128)(2,1)S(1)} %shard_map.79.own_ref.other_ref, bf16[8,6,128,128]{3,2,1,0:T(8,128)(2,1)S(1)} %shard_map.79.own_ref.other_ref), custom_call_target="tpu_custom_call" | custom-call | flops 704643072 | bytes 7340032 | tf_op jit(solution)/shard_map/pallas_call | solution.py:335
  178.0 63.1 %all_to_all.16 = bf16[32,576,128]{2,1,0:T(8,128)(2,1)S(1)} all-to-all(bf16[32,576,128]{2,1,0:T(8,128)(2,1)S(1)} %shard_map.80), channel_id=1, replica_groups=mesh['zh'=4,'c'=2,'y'=4,'x'=4,'zl'=2] {'y','x','zl'}, dimensions={0} | all-to-all | bytes 9437184 | tf_op jit(solution)/shard_map/all_to_all | solution.py:410
  241.1 0.7 convert_reduce_fusion
  241.7 1.2 broadcast_in_dim.12
  243.0 5.0 %all-to-all-start.2 = ((bf16[32,128,128]{2,1,0:T(8,128)(2,1)}), bf16[32,128,128]{2,1,0:T(8,128)(2,1)S(1)}, u32[]{:S(2)}, u32[]{:S(2)}) async-start(bf16[32,128,128]{2,1,0:T(8,128)(2,1)} %broadcast_in_dim.12), calls=%async_computation.2 | async-start | bytes 2097152 | tf_op jit(solution)/shard_map/all_to_all | solution.py:413
  248.0 16.0 %all-to-all-done.2 = bf16[32,128,128]{2,1,0:T(8,128)(2,1)S(1)} async-done(((bf16[32,128,128]{2,1,0:T(8,128)(2,1)}), bf16[32,128,128]{2,1,0:T(8,128)(2,1)S(1)}, u32[]{:S(2)}, u32[]{:S(2)}) %all-to-all-start.2) | async-done | bytes 1048608 | tf_op jit(solution)/shard_map/all_to_all | solution.py:413
  264.0 1.3 shard_map.81
  (25 shorter events, 0.8 us)
Async XLA Ops:
  7.2 39.9 %all-gather.10.cloned.1.call-start = ((), (), s32[]{:S(2)}) async-start(), calls=%async_computation.5 | async-start | bytes 2064384 | tf_op jit(solution)/shard_map/all_gather | solution.py:398
  9.7 99.2 %all-gather.8.cloned.1.call-start = ((), (), s32[]{:S(2)}) async-start(), calls=%async_computation.4 | async-start | bytes 1769472 | tf_op jit(solution)/shard_map/all_gather | solution.py:400
  9.7 1.5 copy-start.2
  11.2 1.5 copy-start.4
  12.7 1.5 copy-start.6
  14.2 1.5 copy-start.7
  15.7 1.5 copy-start.8
  17.2 1.5 copy-start.9
  22.5 134.0 %all-gather.6.cloned.1.call-start = ((), (), s32[]{:S(2)}) async-start(), calls=%async_computation.3 | async-start | bytes 6488064 | tf_op jit(solution)/shard_map/all_gather | solution.py:406
  47.1 1.5 copy-start
  156.5 1.4 copy-start.10
  157.9 16.1 %copy-start.3 = (bf16[128,7168]{1,0:T(8,128)(2,1)S(1)}, bf16[128,7168]{1,0:T(8,128)(2,1)}, u32[]{:S(2)}) copy-start(bf16[128,7168]{1,0:T(8,128)(2,1)} %x_ref.3) | copy-start | bytes 5505028
  157.9 16.1 %copy-start.5 = (bf16[128,7168]{1,0:T(8,128)(2,1)S(1)}, bf16[128,7168]{1,0:T(8,128)(2,1)}, u32[]{:S(2)}) copy-start(bf16[128,7168]{1,0:T(8,128)(2,1)} %c_ref.3) | copy-start | bytes 5505028
  241.7 22.3 %copy-start.1 = (bf16[32,224,128]{2,1,0:T(8,128)(2,1)S(1)}, bf16[32,224,128]{2,1,0:T(8,128)(2,1)}, u32[]{:S(2)}) copy-start(bf16[32,224,128]{2,1,0:T(8,128)(2,1)} %all-gather.10.cloned.1.call-done) | copy-start | bytes 5505028
  243.0 21.0 %all-to-all-start.2 = ((bf16[32,128,128]{2,1,0:T(8,128)(2,1)}), bf16[32,128,128]{2,1,0:T(8,128)(2,1)S(1)}, u32[]{:S(2)}, u32[]{:S(2)}) async-start(bf16[32,128,128]{2,1,0:T(8,128)(2,1)} %broadcast_in_dim.12), calls=%async_computation.2 | async-start | bytes 2097152 | tf_op jit(solution)/shard_map/all_to_all | solution.py:413
Sparse Core Ops, SparseCore 0:
  9.8 37.2 all-gather.9
  48.9 33.3 all-gather.7
  109.0 47.4 all-gather.5

commit v2 on v1

v2 whole, which is shorter than its diff:
```python
import functools

import jax
import jax.numpy as jnp
from jax import lax
from jax.experimental import pallas as pl
from jax.experimental.pallas import tpu as pltpu
from jax.sharding import Mesh, PartitionSpec as P

EPS = 1e-05
R = 128
SECTIONS = 8
BLOCKS = 16
SEC = ("zh", "c")
DP = ("y", "x", "zl")
BF = jnp.bfloat16
F32 = jnp.float32


def mm(left, right):
    return jnp.dot(left, right, preferred_element_type=F32)


def mm_nt(left, right):
    return lax.dot_general(left, right, (((1,), (1,)), ((), ())), preferred_element_type=F32)


def mm_tn(left, right):
    return lax.dot_general(left, right, (((0,), (0,)), ((), ())), preferred_element_type=F32)


def call(kernel, **kw):
    return pl.pallas_call(kernel, **kw)


def project_kernel(slab, pos_ref, x_ref, c_ref, a_ref, p_ref, b_ref, q_ref, *refs):
    out_ref, ss_ref, keep_x_ref, keep_c_ref, send_ref, acc, acc_ss = refs
    step = pl.program_id(0)

    @pl.when(step == 0)
    def _():
        acc[...] = jnp.zeros_like(acc)
        acc_ss[...] = jnp.zeros_like(acc_ss)

    x, c = x_ref[...], c_ref[...]
    rows, width = x.shape
    x32 = x.astype(F32)
    acc_ss[...] += jnp.sum(x32 * x32, axis=-1, keepdims=True)
    ap = jnp.concatenate([a_ref[0], p_ref[0]], axis=1)
    bq = jnp.concatenate([b_ref[0], q_ref[0]], axis=1)
    acc[:, : 2 * R] += mm(x, ap)
    both = mm(jnp.concatenate([x, c], axis=0), bq)
    acc[:, 2 * R : 4 * R] += both[:rows]
    acc[:, 4 * R :] += both[rows:]

    core, odd = pos_ref[1], pos_ref[4] == 1

    def split(value):
        pick = lambda n: jnp.concatenate(
            [value[:, k * slab : (k + 1) * slab] for k in range(n, width // slab, 2)], axis=1
        )
        first, second = pick(0), pick(1)
        return jnp.where(odd, second, first), jnp.where(odd, first, second)

    keep_x, send_x = split(x)
    keep_c, send_c = split(c)
    keep_x_ref[...] = keep_x
    keep_c_ref[...] = keep_c
    send_ref[...] = jnp.where(core == 0, send_x, send_c)

    @pl.when(step == pl.num_programs(0) - 1)
    def _():
        out_ref[...] = acc[...].astype(BF)
        ss_ref[...] = acc_ss[...]


def project(pos, slab, x, c, a, p, b, q):
    rows, width = x.shape
    steps = 4
    block = width // steps
    wide = pl.BlockSpec((rows, block), lambda k: (0, k))
    half = pl.BlockSpec((rows, block // 2), lambda k: (0, k))
    weight = pl.BlockSpec((1, block, R), lambda k: (0, k, 0))
    half_shape = jax.ShapeDtypeStruct((rows, width // 2), BF)
    return call(
        functools.partial(project_kernel, slab),
        grid=(steps,),
        in_specs=[pl.BlockSpec(memory_space=pltpu.SMEM)]
        + [wide, wide, weight, weight, weight, weight],
        out_specs=[
            pl.BlockSpec((rows, 6 * R), lambda k: (0, 0)),
            pl.BlockSpec((rows, R), lambda k: (0, 0)),
            half,
            half,
            half,
        ],
        out_shape=[
            jax.ShapeDtypeStruct((rows, 6 * R), BF),
            jax.ShapeDtypeStruct((rows, R), F32),
            half_shape,
            half_shape,
            half_shape,
        ],
        scratch_shapes=[pltpu.VMEM((rows, 6 * R), F32), pltpu.VMEM((rows, R), F32)],
        compiler_params=pltpu.CompilerParams(vmem_limit_bytes=60 * 1024 * 1024),
        cost_estimate=pl.CostEstimate(
            flops=2 * rows * width * 6 * R,
            bytes_accessed=4 * rows * width + 8 * width * R,
            transcendentals=0,
        ),
    )(pos, x, c, a, p, b, q)


def gram_kernel(pos_ref, own_ref, own_sib_ref, prev_ref, prev_sib_ref, next_ref, next_sib_ref, out_ref):
    chip, core = pos_ref[0], pos_ref[1]

    def cols(value, names):
        return jnp.concatenate([value[n] for n in names], axis=1)

    def four(low, high):
        from_b = mm_tn(low[2], cols(high, (0, 2, 1, 3)))
        from_q = mm_tn(low[3], cols(high, (0, 2)))
        mixed = from_b[:, 2 * R :] + from_q
        return [from_b[:, :R], from_b[:, R : 2 * R], mixed[:, :R], mixed[:, R:]]

    def put(at, block):
        out_ref[at * R : (at + 1) * R] = block.astype(BF)

    own, own_sib = own_ref[...], own_sib_ref[...]
    prev, prev_sib = prev_ref[...], prev_sib_ref[...]
    after, after_sib = next_ref[...], next_sib_ref[...]
    wrap = chip == 3
    for slot, other in enumerate((after, after_sib)):
        pair = four(jnp.where(wrap, other, own), jnp.where(wrap, own, other))
        for i in range(4):
            put(slot * 4 + i, pair[i])
    middle = (chip == 1) | (chip == 2)
    pair = four(jnp.where(middle, prev, after), jnp.where(middle, after, prev_sib))
    for i in range(4):
        put(8 + i, pair[i])
    first = core == 0
    pair = four(jnp.where(first, own, own_sib), jnp.where(first, own_sib, own))
    for i in range(2):
        put(12 + i, jnp.where(first, pair[i], pair[2 + i]))
    self_b = mm_tn(own[2], cols(own, (2, 3)))
    put(14, self_b[:, :R])
    put(15, self_b[:, R:] + mm_tn(own[3], own[2]))


def gram(pos, *slices):
    return call(
        gram_kernel,
        in_specs=[pl.BlockSpec(memory_space=pltpu.SMEM)]
        + [pl.BlockSpec(memory_space=pltpu.VMEM)] * 6,
        out_specs=pl.BlockSpec(memory_space=pltpu.VMEM),
        out_shape=jax.ShapeDtypeStruct((BLOCKS * R, R), BF),
        compiler_params=pltpu.CompilerParams(vmem_limit_bytes=60 * 1024 * 1024),
        cost_estimate=pl.CostEstimate(
            flops=2 * slices[0].shape[1] * BLOCKS * R * R,
            bytes_accessed=slices[0].size * 12,
            transcendentals=0,
        ),
    )(pos, *slices)


def place(low, high):
    gap = high // 2 - low // 2
    same = low % 2 == high % 2
    if gap == 0:
        return [(low, 12), (low, 13), (high, 12), (high, 13)]
    if gap == 2:
        chip = low // 2 + 1 if same else (low // 2 + 3) % 4
        return [(chip * 2 + low % 2, 8 + i) for i in range(4)]
    return [(low if gap == 1 else high, (0 if same else 4) + i) for i in range(4)]


def relay_kernel(axes, piece, width, pos_ref, ss_ref, *refs):
    nzh, nc, ny, nx, nzl = axes
    parts, (g_mine, g_sib, own_ref, m_ref, g, pxc, sem, sem_p, saved, coef) = refs[:8], refs[8:]
    chip, core = pos_ref[0], pos_ref[1]

    for n in range(8):
        section = lax.rem(chip + n // 2, nzh) * nc + (core if n % 2 == 0 else 1 - core)
        pltpu.make_async_copy(parts[n], pxc.at[section], sem_p).start()
    for source, c in ((g_mine, core), (g_sib, 1 - core)):

        def fetch(index, _):
            owner = lax.rem(index, nzh) * nc + c
            to = (owner * (ny * nx) + index // nzh) * piece
            pltpu.make_async_copy(
                source.at[pl.ds(pl.multiple_of(index * piece, 16), piece)],
                g.at[pl.ds(pl.multiple_of(to, 16), piece)],
                sem,
            ).start()
            return 0

        lax.fori_loop(0, nzh * ny * nx, fetch, 0)
    pltpu.make_async_copy(pxc, pxc, sem_p).wait()
    pltpu.make_async_copy(g, g, sem).wait()

    def block(at):
        start = (at[0] * BLOCKS + at[1]) * R
        return g[start : start + R]

    def pair(at):
        plain = jnp.concatenate([block(at[0]), block(at[1])], axis=1)
        return plain, jnp.concatenate([block(at[2]), block(at[3])], axis=1)

    rows = pxc.shape[1]
    ss = ss_ref[...][:, :1]
    st = jnp.zeros_like(ss)
    rsum = lambda v: jnp.sum(v, axis=-1, keepdims=True)
    hs, dhs, scales, mus = [], [], [], []
    for s in range(SECTIONS):
        base = pxc[s]
        xa, xd, xb, xs = [base[:, i * R : (i + 1) * R].astype(F32) for i in range(4)]
        for j in range(s):
            plain, mixed = pair(place(j, s))
            both = mm(jnp.concatenate([hs[j], dhs[j]], axis=0), plain)
            cross = mm(hs[j], mixed)
            xa = xa + both[:rows, :R]
            xb = xb + both[:rows, R:]
            xd = xd + (both[rows:, :R] + cross[:, :R])
            xs = xs + (both[rows:, R:] + cross[:, R:])
        r = lax.rsqrt(ss / width + EPS)
        mu = r * r * r * (st / width)
        pre = r * xa
        dpre = r * xd - mu * xa
        sig = 1.0 / (1.0 + jnp.exp(-pre))
        slope = sig * (1.0 + pre * (1.0 - sig))
        bend = sig * (1.0 - sig) * (2.0 + pre * (1.0 - 2.0 * sig))
        h = (pre * sig).astype(BF)
        dh = (slope * dpre).astype(BF)
        hs.append(h)
        dhs.append(dh)
        scales.append(r)
        mus.append(mu)
        same, cross = block((s, 14)), block((s, 15))
        both = mm(jnp.concatenate([h, dh], axis=0), same)
        turn = mm(h, cross)
        xb_new = xb + both[:rows]
        h32, dh32 = h.astype(F32), dh.astype(F32)
        ss = ss + rsum(h32 * (xb + xb_new))
        st = st + rsum(dh32 * xb_new + h32 * (xs + 0.5 * turn))
        xs_new = xs + turn + both[rows:]
        for i, value in enumerate((xa, xd, xb_new, xs_new, slope, bend * dpre)):
            saved[s, i] = value
        coef[s, 0] = h
        coef[s, 1] = dh

    total = jnp.zeros_like(ss)
    dtotal = jnp.zeros_like(ss)
    left, dleft = [None] * SECTIONS, [None] * SECTIONS
    for s in reversed(range(SECTIONS)):
        xa, xd, xb_new, xs_new, slope, curve = [saved[s, i] for i in range(6)]
        base = pxc[s]
        gh = base[:, 4 * R : 5 * R].astype(F32) - total * xb_new
        dgh = base[:, 5 * R :].astype(F32) - (dtotal * xb_new + total * xs_new)
        for i in range(s + 1, SECTIONS):
            plain, mixed = pair(place(s, i))
            both = mm_nt(jnp.concatenate([left[i], dleft[i]], axis=0), plain)
            gh = gh + both[:rows]
            dgh = dgh + (both[rows:] + mm_nt(left[i], mixed))
        ga = gh * slope
        dga = dgh * slope + gh * curve
        r, mu = scales[s], mus[s]
        u = (r * dga - mu * ga).astype(BF)
        v = (r * ga).astype(BF)
        h32, dh32 = hs[s].astype(F32), dhs[s].astype(F32)
        z = (-total * h32).astype(BF)
        y = (-(dtotal * h32 + total * dh32)).astype(BF)
        left[s] = jnp.concatenate([v, z], axis=1)
        dleft[s] = jnp.concatenate([u, y], axis=1)
        coef[s, 2] = u
        coef[s, 3] = v
        coef[s, 4] = z
        coef[s, 5] = y
        inner = rsum(ga * xa) / width
        dinner = rsum(dga * xa + ga * xd) / width
        total = total + r * r * r * inner
        dtotal = dtotal + r * r * r * dinner - 3.0 * r * r * mu * inner

    me = chip * nc + core
    h, dh, u, v, z, y = [coef[me, n] for n in range(6)]
    for n, value in enumerate((u, y, dh)):
        own_ref[n] = value

    ht, dht, ut, vt, zt, yt = [value.T for value in (h, dh, u, v, z, y)]

    def products(p0, p1, r0t, r1t):
        first = mm(jnp.concatenate([r0t, r1t], axis=1), jnp.concatenate([p0, p1], axis=0))
        return first, mm(r1t, p0)

    for i in range(SECTIONS):
        hi, dhi, ui, vi, zi, yi = [coef[i, n] for n in range(6)]
        below, upto = i < me, i <= me
        m0, m1 = products(
            jnp.where(below, hi, vi),
            jnp.where(below, dhi, ui),
            jnp.where(below, ut, dht),
            jnp.where(below, vt, ht),
        )
        m2, m3 = products(
            jnp.where(upto, hi, zi),
            jnp.where(upto, dhi, yi),
            jnp.where(upto, yt, dht),
            jnp.where(upto, zt, ht),
        )
        keep = i != me
        for n, m in enumerate((jnp.where(keep, m0, 0.0), jnp.where(keep, m1, 0.0), m2, m3)):
            m_ref[i * 4 + n] = m.astype(BF)


def relay(axes, width, pos, ss, parts, g_mine, g_sib):
    rows = ss.shape[0]
    total = 2 * g_mine.shape[0]
    piece = total // (axes[0] * axes[1] * axes[2] * axes[3])
    vm = pl.BlockSpec(memory_space=pltpu.VMEM)
    far = pl.BlockSpec(memory_space=pl.ANY)
    return call(
        functools.partial(relay_kernel, axes, piece, float(width)),
        in_specs=[pl.BlockSpec(memory_space=pltpu.SMEM), vm] + [far] * 10,
        out_specs=[vm, vm],
        out_shape=[
            jax.ShapeDtypeStruct((3, rows, R), BF),
            jax.ShapeDtypeStruct((4 * SECTIONS, R, R), BF),
        ],
        scratch_shapes=[
            pltpu.VMEM((total, R), BF),
            pltpu.VMEM((SECTIONS, rows, 6 * R), BF),
            pltpu.SemaphoreType.DMA,
            pltpu.SemaphoreType.DMA,
            pltpu.VMEM((SECTIONS, 6, rows, R), F32),
            pltpu.VMEM((SECTIONS, 6, rows, R), BF),
        ],
        compiler_params=pltpu.CompilerParams(vmem_limit_bytes=60 * 1024 * 1024),
        cost_estimate=pl.CostEstimate(
            flops=2 * 28 * 12 * rows * R * R, bytes_accessed=total * R * 2, transcendentals=0
        ),
    )(pos, ss, *parts, g_mine, g_sib)


def terms_kernel(pos_ref, x_ref, c_ref, recv_ref, sib_ref, own_ref, far_ref, out_ref):
    first = pos_ref[1] == 0
    part = out_ref.shape[0]
    slab = x_ref.shape[1] // part
    out_ref[:, 2 * slab :] = jnp.zeros_like(out_ref[:, 2 * slab :])
    recv, sib = recv_ref[...], sib_ref[...]
    x = jnp.concatenate([x_ref[...], jnp.where(first, recv, sib)], axis=0)
    c = jnp.concatenate([c_ref[...], jnp.where(first, sib, recv)], axis=0)
    u, y, dh = [jnp.concatenate([own_ref[n], far_ref[n]], axis=0) for n in range(3)]
    from_x = mm_tn(x, jnp.concatenate([u, y], axis=1))
    t_in = from_x[:, :R].astype(BF)
    t_out = (from_x[:, R:] + mm_tn(c, dh)).astype(BF)
    for n in range(part):
        out_ref[n, :slab] = t_in[n * slab : (n + 1) * slab]
        out_ref[n, slab : 2 * slab] = t_out[n * slab : (n + 1) * slab]


def terms(pos, slab, room, x, c, recv, recv_sib, own, far):
    rows, width = x.shape
    steps = 4
    block = width // steps
    wide = pl.BlockSpec((rows, block), lambda i: (0, i))
    small = pl.BlockSpec(own.shape, lambda i: (0, 0, 0))
    part = block // slab
    return call(
        terms_kernel,
        grid=(steps,),
        in_specs=[pl.BlockSpec(memory_space=pltpu.SMEM), wide, wide, wide, wide, small, small],
        out_specs=pl.BlockSpec((part, 2 * slab + room, R), lambda i: (i, 0, 0)),
        out_shape=jax.ShapeDtypeStruct((width // slab, 2 * slab + room, R), BF),
        compiler_params=pltpu.CompilerParams(vmem_limit_bytes=60 * 1024 * 1024),
        cost_estimate=pl.CostEstimate(
            flops=4 * rows * width * 3 * R, bytes_accessed=12 * rows * width, transcendentals=0
        ),
    )(pos, x, c, recv, recv_sib, own, far)


def finish_kernel(axes, pos_ref, all_ref, *refs):
    nzh, nc, ny, nx, nzl = axes
    slices, (in_ref, out_ref) = refs[:8], refs[8:]
    chip, core = pos_ref[0], pos_ref[1]
    me = nc * chip + core
    own = slices[0]
    slab = own.shape[1]
    each = 4 * SECTIONS // (ny * nx)
    t = all_ref[0, : 2 * slab].astype(F32)
    for n in range(1, ny * nx):
        t = t + all_ref[n, : 2 * slab].astype(F32)
    t_in, t_out = t[:slab], t[slab:]

    def m_block(at):
        row = 2 * slab + lax.rem(at, each) * R
        return all_ref[at // each, pl.ds(pl.multiple_of(row, 16), R)]

    for n in range(8):
        i = nc * lax.rem(chip + n // 2, nzh) + (core if n % 2 == 0 else 1 - core)
        below = i < me
        a, p, b, q = [slices[n][k] for k in range(4)]
        first = jnp.concatenate([jnp.where(below, b, a), jnp.where(below, q, p)], axis=1)
        ms = [m_block(i * 4 + k) for k in range(4)]
        product = mm_nt(first, jnp.concatenate(ms[:2], axis=1))
        t_in = t_in + jnp.where(below, product, 0.0)
        t_out = t_out + jnp.where(below, 0.0, product)
        t_out = t_out + mm_nt(jnp.concatenate([b, q], axis=1), jnp.concatenate(ms[2:], axis=1))
    in_ref[...] = own[1].astype(F32) * t_in
    out_ref[...] = own[3].astype(F32) * t_out


def finish(axes, pos, arrived, slices):
    vm = pl.BlockSpec(memory_space=pltpu.VMEM)
    shape = jax.ShapeDtypeStruct((slices[0].shape[1], R), F32)
    return call(
        functools.partial(finish_kernel, axes),
        in_specs=[pl.BlockSpec(memory_space=pltpu.SMEM)] + [vm] * 9,
        out_specs=[vm, vm],
        out_shape=[shape, shape],
        compiler_params=pltpu.CompilerParams(vmem_limit_bytes=60 * 1024 * 1024),
    )(pos, arrived, *slices)


def shifted(value, axis, steps):
    count = lax.axis_size(axis)
    return lax.ppermute(value, axis, [(i, (i + steps) % count) for i in range(count)])


def spread(value, axis):
    copies = jnp.broadcast_to(value[None], (lax.axis_size(axis),) + value.shape)
    return lax.all_to_all(copies, axis, 0, 0, tiled=True).reshape((-1,) + value.shape[1:])


def on_device(axes, inputs, cotangent, adapt_in, adapt_out, probe_in, probe_out):
    nzh, nc, ny, nx, nzl = axes
    ndp = ny * nx * nzl
    rows, width = inputs.shape
    slab = width // ndp
    pos = jnp.stack([lax.axis_index(n) for n in SEC + DP]).astype(jnp.int32)
    dp = lax.axis_index(DP)
    sib = lambda w: shifted(w, "c", 1)

    own = jnp.stack(
        [
            lax.dynamic_slice_in_dim(w[0], dp * slab, slab, 0)
            for w in (adapt_in, probe_in, adapt_out, probe_out)
        ]
    )
    prev, after = shifted(own, "zh", 1), shifted(own, "zh", -1)
    own_sib = sib(own)
    projected, ss, keep_x, keep_c, send = project(
        pos, slab, inputs, cotangent, adapt_in, probe_in, adapt_out, probe_out
    )
    prev, after, projected, send = lax.optimization_barrier((prev, after, projected, send))
    prev_sib, after_sib = sib(prev), sib(after)
    partial = gram(pos, own, own_sib, prev, prev_sib, after, after_sib)

    near = [projected] + [shifted(projected, "zh", -k) for k in (1, 2, 3)]
    recv = shifted(send, "zl", 1)
    opposite = shifted(own, "zh", 2)

    arrived = lax.all_to_all(partial.reshape(ny * nx, -1, R), ("y", "x"), 0, 0, tiled=True)
    arrived, near[1], near[3] = lax.optimization_barrier((arrived, near[1], near[3]))
    piece = jnp.sum(arrived.astype(F32), axis=0).astype(BF)
    line = spread(piece, ("zh", "zl")).reshape(nzh, nzl, -1, R)
    line = jnp.sum(line.astype(F32), axis=1).astype(BF).reshape(-1, R)
    g_mine = spread(line, ("y", "x"))
    g_mine, near = lax.optimization_barrier((g_mine, near))
    parts = [v for w in near for v in (w, sib(w))]
    g_sib = sib(g_mine)

    own3, m_part = relay(axes, width, pos, ss, parts, g_mine, g_sib)
    own3, recv = lax.optimization_barrier((own3, recv))
    far3 = shifted(own3, "zl", 1)
    m_arrived = lax.all_to_all(m_part.reshape(ny * nx, -1, R), ("y", "x"), 0, 0, tiled=True)
    m_own = jnp.sum(m_arrived.astype(F32), axis=0)
    room = m_own.shape[0]
    mine = terms(pos, slab, room, keep_x, keep_c, recv, sib(recv), own3, far3)
    m_own = (m_own + shifted(m_own, "zl", 1)).astype(BF)
    copies = jnp.broadcast_to(m_own[None], (ny * nx,) + m_own.shape)
    mine = lax.dynamic_update_slice(mine, copies, (0, 2 * slab, 0))
    arrived = lax.all_to_all(mine, ("y", "x"), 0, 0, tiled=True)
    arrived, opposite = lax.optimization_barrier((arrived, opposite))
    slices = [own, own_sib, after, after_sib, opposite, sib(opposite), prev, prev_sib]
    diag_in, diag_out = finish(axes, pos, arrived, slices)
    return diag_in[None], diag_out[None]


def solution(mesh, axes=(4, 2, 4, 4, 2)):
    fine = Mesh(mesh.devices.reshape(axes), SEC + DP)
    tokens, weights = P(DP, None), P(SEC, None, None)
    return jax.shard_map(
        functools.partial(on_device, axes),
        mesh=fine,
        in_specs=(tokens, tokens, weights, weights, weights, weights),
        out_specs=(P(SEC, DP, None), P(SEC, DP, None)),
        check_vma=False,
    )
```

time: 273 us -> 206 us (0.75)
  the two profiles are of different devices: /device:TPU:2 before, /device:TPU:1 now
where the time goes in v2:
time: 206 us; the launch traced here: 205 us
  waiting for transfers between devices  99.8 us (48%)
  starting transfers between devices  47.4 us (23%)
  Pallas kernels  32.3 us (16%)
  blocking collectives  15 us (7%)
  local copies, waits for them, and re-layouts  9.5 us (5%)
    ppermute x19, waiting for transfers between devices, shifted(): lax.ppermute(value, axis, [(i, (i + steps) % count) for i in range(count)])  36.9 us
    all_to_all x1, waiting for transfers between devices, on_device(): arrived = lax.all_to_all(mine, ('y', 'x'), 0, 0, tiled=True)  30.8 us
    ppermute x19, starting transfers between devices, shifted(): lax.ppermute(value, axis, [(i, (i + steps) % count) for i in range(count)])  26 us
    all_to_all x1, waiting for transfers between devices, spread(): lax.all_to_all(copies, axis, 0, 0, tiled=True)  16.3 us
    all_to_all x1, waiting for transfers between devices, on_device(): lax.all_to_all(m_part.reshape(ny * nx, -1, R), ('y', 'x'), 0, 0, tiled=True)  15.9 us
    all_to_all x1, blocking collectives, spread(): lax.all_to_all(copies, axis, 0, 0, tiled=True)  15 us
    pallas_call x1, Pallas kernels, relay(): call(functools.partial(relay_kernel, axes, piece, float(width)), in_specs...  13 us
    pallas_call x1, Pallas kernels, project(): call(functools.partial(project_kernel, slab), grid=(steps,), in_specs=[pl...  7.18 us
  transfers between devices with their start and end apart: 23, of which 13 were waited for; matrix products, arithmetic and copies ran while one was open for 0% of the time, Pallas kernels for 13%

profile of v2, /device:TPU:1, one launch (start us, length us, event | category | flops | bytes accessed | tf_op | source)
XLA Modules:
  0.0 205.2 jit_solution(17768261527931143001)
XLA Ops:
  2.4 3.9 %collective-permute-start.1 = (bf16[4,224,128]{2,1,0:T(8,128)(2,1)S(1)}, bf16[4,224,128]{2,1,0:T(8,128)(2,1)S(1)}, u32[]{:S(2)}, u32[]{:S(2)}) collective-permute-start(bf16[4,224,128]{2,1,0:T(8,128)(2,1)S(1)} %pad_maximum_fusion.own_ref.refs_0_), channel_id=1, source_target_pairs={{0,64},{64,128},{128,192},{192,0},{1,65},{65,129},{129,193},{193,1... | collective-permute-start | bytes 688136 | tf_op jit(solution)/shard_map/ppermute | solution.py:425
  6.3 3.1 %collective-permute-start.2 = (bf16[4,224,128]{2,1,0:T(8,128)(2,1)S(1)}, bf16[4,224,128]{2,1,0:T(8,128)(2,1)S(1)}, u32[]{:S(2)}, u32[]{:S(2)}) collective-permute-start(bf16[4,224,128]{2,1,0:T(8,128)(2,1)S(1)} %pad_maximum_fusion.own_ref.refs_0_), channel_id=1, source_target_pairs={{0,192},{64,0},{128,64},{192,128},{1,193},{65,1},{129,65},{193,129... | collective-permute-start | bytes 688136 | tf_op jit(solution)/shard_map/ppermute | solution.py:425
  11.1 7.2 %shard_map.77 = (bf16[128,768]{1,0:T(8,128)(2,1)}, f32[128,128]{1,0:T(8,128)}, bf16[128,3584]{1,0:T(8,128)(2,1)}, bf16[128,3584]{1,0:T(8,128)(2,1)}, bf16[128,3584]{1,0:T(8,128)(2,1)}) custom-call(s32[5]{0:T(128)} %stack.30.pos_ref, bf16[128,7168]{1,0:T(8,128)(2,1)} %x_ref.1, bf16[128,7168]{1,0:T(8,128)(2,1)} %c_ref.1, bf16[1,7168,128]{2,1,0:T(8,128)(2,1)} %a_ref.1, ...), custom_call_target="tpu_custom_call" | custom-call | flops 1409286144 | bytes 11010048 | tf_op jit(solution)/shard_map/pallas_call | solution.py:85
  18.3 2.7 %collective-permute-done.2.next_ref.refs_2_ = bf16[4,224,128]{2,1,0:T(8,128)(2,1)S(1)} collective-permute-done((bf16[4,224,128]{2,1,0:T(8,128)(2,1)S(1)}, bf16[4,224,128]{2,1,0:T(8,128)(2,1)S(1)}, u32[]{:S(2)}, u32[]{:S(2)}) %collective-permute-start.2) | collective-permute-done | bytes 229408 | tf_op jit(solution)/shard_map/ppermute | solution.py:425
  24.5 2.7 %shard_map.78 = bf16[2048,128]{1,0:T(8,128)(2,1)} custom-call(s32[5]{0:T(128)} %stack.30.pos_ref, bf16[4,224,128]{2,1,0:T(8,128)(2,1)} %copy-done.3, bf16[4,224,128]{2,1,0:T(8,128)(2,1)} %copy-done.9, bf16[4,224,128]{2,1,0:T(8,128)(2,1)} %copy-done.7, bf16[4,224,128]{2,1,0:T(8,128)(2,1)} %copy-done.10, bf16[4,224,128]{2,1,0:T(8,128)(2,1)} %copy-done.8, ...), custom_call_target="tpu_custom_call" | custom-call | flops 117440512 | bytes 1376256 | tf_op jit(solution)/shard_map/pallas_call | solution.py:151
  27.2 6.8 %all-to-all-start = ((bf16[16,128,128]{2,1,0:T(8,128)(2,1)}), bf16[16,128,128]{2,1,0:T(8,128)(2,1)S(1)}, u32[]{:S(2)}, u32[]{:S(2)}) async-start(bf16[16,128,128]{2,1,0:T(8,128)(2,1)} %bitcast.15), calls=%async_computation | async-start | bytes 1048576 | tf_op jit(solution)/shard_map/all_to_all | solution.py:461
  33.9 2.6 %collective-permute-start.5 = (bf16[128,768]{1,0:T(8,128)(2,1)S(1)}, bf16[128,768]{1,0:T(8,128)(2,1)S(1)}, u32[]{:S(2)}, u32[]{:S(2)}) collective-permute-start(bf16[128,768]{1,0:T(8,128)(2,1)S(1)} %copy-done.14), channel_id=1, source_target_pairs={{0,192},{64,0},{128,64},{192,128},{1,193},{65,1},{129,65},{193,129... | collective-permute-start | bytes 589832 | tf_op jit(solution)/shard_map/ppermute | solution.py:425
  37.5 9.3 %collective-permute-done.5.refs_2_ = bf16[128,768]{1,0:T(8,128)(2,1)S(1)} collective-permute-done((bf16[128,768]{1,0:T(8,128)(2,1)S(1)}, bf16[128,768]{1,0:T(8,128)(2,1)S(1)}, u32[]{:S(2)}, u32[]{:S(2)}) %collective-permute-start.5) | collective-permute-done | bytes 196640 | tf_op jit(solution)/shard_map/ppermute | solution.py:425
  48.1 15.0 %all_to_all.25 = bf16[8,128,128]{2,1,0:T(8,128)(2,1)S(1)} all-to-all(bf16[8,128,128]{2,1,0:T(8,128)(2,1)S(1)} %broadcast_in_dim.12), channel_id=1, replica_groups=mesh['zh'=4,'c'=2,'y'=4,'x'=4,'zl'=2] {'zh','zl'}, dimensions={0} | all-to-all | bytes 524288 | tf_op jit(solution)/shard_map/all_to_all | solution.py:430
  63.2 1.7 broadcast_in_dim.27
  64.9 6.7 %all-to-all-start.2 = ((bf16[16,512,128]{2,1,0:T(8,128)(2,1)}), bf16[16,512,128]{2,1,0:T(8,128)(2,1)S(1)}, u32[]{:S(2)}, u32[]{:S(2)}) async-start(bf16[16,512,128]{2,1,0:T(8,128)(2,1)} %broadcast_in_dim.27), calls=%async_computation.2 | async-start | bytes 4194304 | tf_op jit(solution)/shard_map/all_to_all | solution.py:430
  72.4 7.8 %collective-permute-done.7.refs_4_ = bf16[128,768]{1,0:T(8,128)(2,1)S(1)} collective-permute-done((bf16[128,768]{1,0:T(8,128)(2,1)S(1)}, bf16[128,768]{1,0:T(8,128)(2,1)S(1)}, u32[]{:S(2)}, u32[]{:S(2)}) %collective-permute-start.7) | collective-permute-done | bytes 196640 | tf_op jit(solution)/shard_map/ppermute | solution.py:425
  80.2 16.3 %all-to-all-done.2 = bf16[16,512,128]{2,1,0:T(8,128)(2,1)S(1)} async-done(((bf16[16,512,128]{2,1,0:T(8,128)(2,1)}), bf16[16,512,128]{2,1,0:T(8,128)(2,1)S(1)}, u32[]{:S(2)}, u32[]{:S(2)}) %all-to-all-start.2) | async-done | bytes 2097184 | tf_op jit(solution)/shard_map/all_to_all | solution.py:430
  96.5 5.8 %collective-permute-start.12 = (bf16[8192,128]{1,0:T(8,128)(2,1)S(1)}, bf16[8192,128]{1,0:T(8,128)(2,1)S(1)}, u32[]{:S(2)}, u32[]{:S(2)}) collective-permute-start(bf16[8192,128]{1,0:T(8,128)(2,1)S(1)} %bitcast.13), channel_id=1, source_target_pairs={{0,32},{32,0},{1,33},{33,1},{2,34},{34,2},{3,35},{35,3},{4,36},{36... | collective-permute-start | bytes 6291464 | tf_op jit(solution)/shard_map/ppermute | solution.py:425
  103.8 2.9 %collective-permute-done.8.refs_1_ = bf16[128,768]{1,0:T(8,128)(2,1)S(1)} collective-permute-done((bf16[128,768]{1,0:T(8,128)(2,1)S(1)}, bf16[128,768]{1,0:T(8,128)(2,1)S(1)}, u32[]{:S(2)}, u32[]{:S(2)}) %collective-permute-start.8) | collective-permute-done | bytes 196640 | tf_op jit(solution)/shard_map/ppermute | solution.py:425
  109.7 13.0 %shard_map.79 = (bf16[3,128,128]{2,1,0:T(8,128)(2,1)}, bf16[32,128,128]{2,1,0:T(8,128)(2,1)}) custom-call(s32[5]{0:T(128)} %stack.30.pos_ref, f32[128,128]{1,0:T(8,128)} %get-tuple-element.29.ss_ref, bf16[128,768]{1,0:T(8,128)(2,1)} %get-tuple-element.38.refs_0_, bf16[128,768]{1,0:T(8,128)(2,1)} %copy-done.18, bf16[128,768]{1,0:T(8,128)(2,1)} %copy-done.15, ...), custom_call_target="tpu_custom_call" | custom-call | flops 1409286144 | bytes 4194304 | tf_op jit(solution)/shard_map/pallas_call | solution.py:320
  122.7 3.8 %all-to-all-start.3 = ((bf16[16,256,128]{2,1,0:T(8,128)(2,1)}), bf16[16,256,128]{2,1,0:T(8,128)(2,1)S(1)}, u32[]{:S(2)}, u32[]{:S(2)}) async-start(bf16[16,256,128]{2,1,0:T(8,128)(2,1)} %bitcast.16), calls=%async_computation.3 | async-start | bytes 2097152 | tf_op jit(solution)/shard_map/all_to_all | solution.py:474
  127.6 15.9 %all-to-all-done.3 = bf16[16,256,128]{2,1,0:T(8,128)(2,1)S(1)} async-done(((bf16[16,256,128]{2,1,0:T(8,128)(2,1)}), bf16[16,256,128]{2,1,0:T(8,128)(2,1)S(1)}, u32[]{:S(2)}, u32[]{:S(2)}) %all-to-all-start.3) | async-done | bytes 1048608 | tf_op jit(solution)/shard_map/all_to_all | solution.py:474
  145.3 5.5 %shard_map.80 = bf16[16,704,128]{2,1,0:T(8,128)(2,1)} custom-call(s32[5]{0:T(128)} %stack.30.pos_ref, bf16[128,3584]{1,0:T(8,128)(2,1)} %get-tuple-element.27.x_ref, bf16[128,3584]{1,0:T(8,128)(2,1)} %get-tuple-element.28.c_ref, bf16[128,3584]{1,0:T(8,128)(2,1)} %copy-done.5, bf16[128,3584]{1,0:T(8,128)(2,1)} %copy-done.6, ...), custom_call_target="tpu_custom_call" | custom-call | flops 704643072 | bytes 5505024 | tf_op jit(solution)/shard_map/pallas_call | solution.py:367
  152.1 4.2 %all-to-all-start.4 = ((bf16[16,704,128]{2,1,0:T(8,128)(2,1)}), bf16[16,704,128]{2,1,0:T(8,128)(2,1)S(1)}, u32[]{:S(2)}, u32[]{:S(2)}) async-start(bf16[16,704,128]{2,1,0:T(8,128)(2,1)} %broadcast_dynamic-update-slice_fusion), calls=%async_computation.4 | async-start | bytes 5767168 | tf_op jit(solution)/shard_map/all_to_all | solution.py:481
  156.7 9.1 %collective-permute-done.17.refs_4_ = bf16[4,224,128]{2,1,0:T(8,128)(2,1)S(1)} collective-permute-done((bf16[4,224,128]{2,1,0:T(8,128)(2,1)S(1)}, bf16[4,224,128]{2,1,0:T(8,128)(2,1)S(1)}, u32[]{:S(2)}, u32[]{:S(2)}) %collective-permute-start.17) | collective-permute-done | bytes 229408 | tf_op jit(solution)/shard_map/ppermute | solution.py:425
  165.8 30.8 %all-to-all-done.4.all_ref = bf16[16,704,128]{2,1,0:T(8,128)(2,1)S(1)} async-done(((bf16[16,704,128]{2,1,0:T(8,128)(2,1)}), bf16[16,704,128]{2,1,0:T(8,128)(2,1)S(1)}, u32[]{:S(2)}, u32[]{:S(2)}) %all-to-all-start.4) | async-done | bytes 2883616 | tf_op jit(solution)/shard_map/all_to_all | solution.py:481
  196.6 2.8 %collective-permute-start.18 = (bf16[4,224,128]{2,1,0:T(8,128)(2,1)S(1)}, bf16[4,224,128]{2,1,0:T(8,128)(2,1)S(1)}, u32[]{:S(2)}, u32[]{:S(2)}) collective-permute-start(bf16[4,224,128]{2,1,0:T(8,128)(2,1)S(1)} %collective-permute-done.17.refs_4_), channel_id=1, source_target_pairs={{0,32},{32,0},{1,33},{33,1},{2,34},{34,2},{3,35},{35,3},{4,36},{36... | collective-permute-start | bytes 688136 | tf_op jit(solution)/shard_map/ppermute | solution.py:425
  201.2 4.0 %shard_map.81 = (f32[224,128]{1,0:T(8,128)}, f32[224,128]{1,0:T(8,128)}) custom-call(s32[5]{0:T(128)} %stack.30.pos_ref, bf16[16,704,128]{2,1,0:T(8,128)(2,1)} %copy-done, bf16[4,224,128]{2,1,0:T(8,128)(2,1)} %copy-done.3, bf16[4,224,128]{2,1,0:T(8,128)(2,1)} %copy-done.9, bf16[4,224,128]{2,1,0:T(8,128)(2,1)} %copy-done.8, bf16[4,224,128]{2,1,0:T(8,128)(2,1)} %copy-done.11, ...), custom_call_target="tpu_custom_call" | custom-call | tf_op jit(solution)/shard_map/pallas_call | solution.py:414
  (87 shorter events, 20.9 us)
Async XLA Ops:
  2.4 15.9 %collective-permute-start.1 = (bf16[4,224,128]{2,1,0:T(8,128)(2,1)S(1)}, bf16[4,224,128]{2,1,0:T(8,128)(2,1)S(1)}, u32[]{:S(2)}, u32[]{:S(2)}) collective-permute-start(bf16[4,224,128]{2,1,0:T(8,128)(2,1)S(1)} %pad_maximum_fusion.own_ref.refs_0_), channel_id=1, source_target_pairs={{0,64},{64,128},{128,192},{192,0},{1,65},{65,129},{129,193},{193,1... | collective-permute-start | bytes 688136 | tf_op jit(solution)/shard_map/ppermute | solution.py:425
  6.3 14.7 %collective-permute-start.2 = (bf16[4,224,128]{2,1,0:T(8,128)(2,1)S(1)}, bf16[4,224,128]{2,1,0:T(8,128)(2,1)S(1)}, u32[]{:S(2)}, u32[]{:S(2)}) collective-permute-start(bf16[4,224,128]{2,1,0:T(8,128)(2,1)S(1)} %pad_maximum_fusion.own_ref.refs_0_), channel_id=1, source_target_pairs={{0,192},{64,0},{128,64},{192,128},{1,193},{65,1},{129,65},{193,129... | collective-permute-start | bytes 688136 | tf_op jit(solution)/shard_map/ppermute | solution.py:425
  9.4 12.6 %collective-permute-start = (bf16[4,224,128]{2,1,0:T(8,128)(2,1)S(1)}, bf16[4,224,128]{2,1,0:T(8,128)(2,1)S(1)}, u32[]{:S(2)}, u32[]{:S(2)}) collective-permute-start(bf16[4,224,128]{2,1,0:T(8,128)(2,1)S(1)} %pad_maximum_fusion.own_ref.refs_0_), channel_id=1, source_target_pairs={{0,32},{32,0},{1,33},{33,1},{2,34},{34,2},{3,35},{35,3},{4,36},{36... | collective-permute-start | bytes 688136 | tf_op jit(solution)/shard_map/ppermute | solution.py:425
  21.0 2.1 %collective-permute-start.3 = (bf16[4,224,128]{2,1,0:T(8,128)(2,1)S(1)}, bf16[4,224,128]{2,1,0:T(8,128)(2,1)S(1)}, u32[]{:S(2)}, u32[]{:S(2)}) collective-permute-start(bf16[4,224,128]{2,1,0:T(8,128)(2,1)S(1)} %collective-permute-done.1.prev_ref.refs_6_), channel_id=1, source_target_pairs={{0,32},{32,0},{1,33},{33,1},{2,34},{34,2},{3,35},{35,3},{4,36},{36... | collective-permute-start | bytes 688136 | tf_op jit(solution)/shard_map/ppermute | solution.py:425
  22.0 1.5 collective-permute-start.4
  27.2 20.9 %all-to-all-start = ((bf16[16,128,128]{2,1,0:T(8,128)(2,1)}), bf16[16,128,128]{2,1,0:T(8,128)(2,1)S(1)}, u32[]{:S(2)}, u32[]{:S(2)}) async-start(bf16[16,128,128]{2,1,0:T(8,128)(2,1)} %bitcast.15), calls=%async_computation | async-start | bytes 1048576 | tf_op jit(solution)/shard_map/all_to_all | solution.py:461
  33.9 12.9 %collective-permute-start.5 = (bf16[128,768]{1,0:T(8,128)(2,1)S(1)}, bf16[128,768]{1,0:T(8,128)(2,1)S(1)}, u32[]{:S(2)}, u32[]{:S(2)}) collective-permute-start(bf16[128,768]{1,0:T(8,128)(2,1)S(1)} %copy-done.14), channel_id=1, source_target_pairs={{0,192},{64,0},{128,64},{192,128},{1,193},{65,1},{129,65},{193,129... | collective-permute-start | bytes 589832 | tf_op jit(solution)/shard_map/ppermute | solution.py:425
  36.5 11.5 %collective-permute-start.6 = (bf16[128,768]{1,0:T(8,128)(2,1)S(1)}, bf16[128,768]{1,0:T(8,128)(2,1)S(1)}, u32[]{:S(2)}, u32[]{:S(2)}) collective-permute-start(bf16[128,768]{1,0:T(8,128)(2,1)S(1)} %copy-done.14), channel_id=1, source_target_pairs={{0,64},{64,128},{128,192},{192,0},{1,65},{65,129},{129,193},{193,1... | collective-permute-start | bytes 589832 | tf_op jit(solution)/shard_map/ppermute | solution.py:425
  46.8 56.5 %copy-start.15 = (bf16[128,768]{1,0:T(8,128)(2,1)}, bf16[128,768]{1,0:T(8,128)(2,1)S(1)}, u32[]{:S(2)}) copy-start(bf16[128,768]{1,0:T(8,128)(2,1)S(1)} %collective-permute-done.5.refs_2_) | copy-start | bytes 589828
  64.9 31.6 %all-to-all-start.2 = ((bf16[16,512,128]{2,1,0:T(8,128)(2,1)}), bf16[16,512,128]{2,1,0:T(8,128)(2,1)S(1)}, u32[]{:S(2)}, u32[]{:S(2)}) async-start(bf16[16,512,128]{2,1,0:T(8,128)(2,1)} %broadcast_in_dim.27), calls=%async_computation.2 | async-start | bytes 4194304 | tf_op jit(solution)/shard_map/all_to_all | solution.py:430
  71.6 8.6 %collective-permute-start.7 = (bf16[128,768]{1,0:T(8,128)(2,1)S(1)}, bf16[128,768]{1,0:T(8,128)(2,1)S(1)}, u32[]{:S(2)}, u32[]{:S(2)}) collective-permute-start(bf16[128,768]{1,0:T(8,128)(2,1)S(1)} %copy-done.14), channel_id=1, source_target_pairs={{0,128},{64,192},{128,0},{192,64},{1,129},{65,193},{129,1},{193,65... | collective-permute-start | bytes 589832 | tf_op jit(solution)/shard_map/ppermute | solution.py:425
  96.5 11.8 %collective-permute-start.12 = (bf16[8192,128]{1,0:T(8,128)(2,1)S(1)}, bf16[8192,128]{1,0:T(8,128)(2,1)S(1)}, u32[]{:S(2)}, u32[]{:S(2)}) collective-permute-start(bf16[8192,128]{1,0:T(8,128)(2,1)S(1)} %bitcast.13), channel_id=1, source_target_pairs={{0,32},{32,0},{1,33},{33,1},{2,34},{34,2},{3,35},{35,3},{4,36},{36... | collective-permute-start | bytes 6291464 | tf_op jit(solution)/shard_map/ppermute | solution.py:425
  102.3 24.2 %collective-permute-start.13 = (bf16[128,3584]{1,0:T(8,128)(2,1)}, bf16[128,3584]{1,0:T(8,128)(2,1)S(1)}, u32[]{:S(2)}, u32[]{:S(2)}) collective-permute-start(bf16[128,3584]{1,0:T(8,128)(2,1)} %get-tuple-element.44), channel_id=1, source_target_pairs={{0,1},{1,0},{2,3},{3,2},{4,5},{5,4},{6,7},{7,6},{8,9},{9,8},{10,11... | collective-permute-start | bytes 2752520 | tf_op jit(solution)/shard_map/ppermute | solution.py:425
  102.9 3.8 %collective-permute-start.8 = (bf16[128,768]{1,0:T(8,128)(2,1)S(1)}, bf16[128,768]{1,0:T(8,128)(2,1)S(1)}, u32[]{:S(2)}, u32[]{:S(2)}) collective-permute-start(bf16[128,768]{1,0:T(8,128)(2,1)S(1)} %copy-done.14), channel_id=1, source_target_pairs={{0,32},{32,0},{1,33},{33,1},{2,34},{34,2},{3,35},{35,3},{4,36},{36... | collective-permute-start | bytes 589832 | tf_op jit(solution)/shard_map/ppermute | solution.py:425
  103.3 3.8 %collective-permute-start.9 = (bf16[128,768]{1,0:T(8,128)(2,1)S(1)}, bf16[128,768]{1,0:T(8,128)(2,1)S(1)}, u32[]{:S(2)}, u32[]{:S(2)}) collective-permute-start(bf16[128,768]{1,0:T(8,128)(2,1)S(1)} %collective-permute-done.5.refs_2_), channel_id=1, source_target_pairs={{0,32},{32,0},{1,33},{33,1},{2,34},{34,2},{3,35},{35,3},{4,36},{36... | collective-permute-start | bytes 589832 | tf_op jit(solution)/shard_map/ppermute | solution.py:425
  103.4 3.6 %collective-permute-start.10 = (bf16[128,768]{1,0:T(8,128)(2,1)}, bf16[128,768]{1,0:T(8,128)(2,1)S(1)}, u32[]{:S(2)}, u32[]{:S(2)}) collective-permute-start(bf16[128,768]{1,0:T(8,128)(2,1)} %copy-done.17), channel_id=1, source_target_pairs={{0,32},{32,0},{1,33},{33,1},{2,34},{34,2},{3,35},{35,3},{4,36},{36... | collective-permute-start | bytes 589832 | tf_op jit(solution)/shard_map/ppermute | solution.py:425
  106.6 1.7 collective-permute-start.11
  122.7 20.7 %all-to-all-start.3 = ((bf16[16,256,128]{2,1,0:T(8,128)(2,1)}), bf16[16,256,128]{2,1,0:T(8,128)(2,1)S(1)}, u32[]{:S(2)}, u32[]{:S(2)}) async-start(bf16[16,256,128]{2,1,0:T(8,128)(2,1)} %bitcast.16), calls=%async_computation.3 | async-start | bytes 2097152 | tf_op jit(solution)/shard_map/all_to_all | solution.py:474
  126.5 17.8 %collective-permute-start.14 = (bf16[128,3584]{1,0:T(8,128)(2,1)S(1)}, bf16[128,3584]{1,0:T(8,128)(2,1)S(1)}, u32[]{:S(2)}, u32[]{:S(2)}) collective-permute-start(bf16[128,3584]{1,0:T(8,128)(2,1)S(1)} %collective-permute-done.13.recv_ref), channel_id=1, source_target_pairs={{0,32},{32,0},{1,33},{33,1},{2,34},{34,2},{3,35},{35,3},{4,36},{36... | collective-permute-start | bytes 2752520 | tf_op jit(solution)/shard_map/ppermute | solution.py:425
  127.0 17.3 %collective-permute-start.15 = (bf16[3,128,128]{2,1,0:T(8,128)(2,1)S(1)}, bf16[3,128,128]{2,1,0:T(8,128)(2,1)S(1)}, u32[]{:S(2)}, u32[]{:S(2)}) collective-permute-start(bf16[3,128,128]{2,1,0:T(8,128)(2,1)S(1)} %copy-done.22), channel_id=1, source_target_pairs={{0,1},{1,0},{2,3},{3,2},{4,5},{5,4},{6,7},{7,6},{8,9},{9,8},{10,11... | collective-permute-start | bytes 294920 | tf_op jit(solution)/shard_map/ppermute | solution.py:425
  143.6 7.2 %collective-permute-start.16 = (f32[256,128]{1,0:T(8,128)S(1)}, f32[256,128]{1,0:T(8,128)S(1)}, u32[]{:S(2)}, u32[]{:S(2)}) collective-permute-start(f32[256,128]{1,0:T(8,128)S(1)} %convert_reduce_fusion), channel_id=1, source_target_pairs={{0,1},{1,0},{2,3},{3,2},{4,5},{5,4},{6,7},{7,6},{8,9},{9,8},{10,11... | collective-permute-start | bytes 393224 | tf_op jit(solution)/shard_map/ppermute | solution.py:425
  152.1 44.5 %all-to-all-start.4 = ((bf16[16,704,128]{2,1,0:T(8,128)(2,1)}), bf16[16,704,128]{2,1,0:T(8,128)(2,1)S(1)}, u32[]{:S(2)}, u32[]{:S(2)}) async-start(bf16[16,704,128]{2,1,0:T(8,128)(2,1)} %broadcast_dynamic-update-slice_fusion), calls=%async_computation.4 | async-start | bytes 5767168 | tf_op jit(solution)/shard_map/all_to_all | solution.py:481
  156.3 9.5 %collective-permute-start.17 = (bf16[4,224,128]{2,1,0:T(8,128)(2,1)S(1)}, bf16[4,224,128]{2,1,0:T(8,128)(2,1)S(1)}, u32[]{:S(2)}, u32[]{:S(2)}) collective-permute-start(bf16[4,224,128]{2,1,0:T(8,128)(2,1)S(1)} %copy-done.4), channel_id=1, source_target_pairs={{0,128},{64,192},{128,0},{192,64},{1,129},{65,193},{129,1},{193,65... | collective-permute-start | bytes 688136 | tf_op jit(solution)/shard_map/ppermute | solution.py:425
  196.6 3.9 %collective-permute-start.18 = (bf16[4,224,128]{2,1,0:T(8,128)(2,1)S(1)}, bf16[4,224,128]{2,1,0:T(8,128)(2,1)S(1)}, u32[]{:S(2)}, u32[]{:S(2)}) collective-permute-start(bf16[4,224,128]{2,1,0:T(8,128)(2,1)S(1)} %collective-permute-done.17.refs_4_), channel_id=1, source_target_pairs={{0,32},{32,0},{1,33},{33,1},{2,34},{34,2},{3,35},{35,3},{4,36},{36... | collective-permute-start | bytes 688136 | tf_op jit(solution)/shard_map/ppermute | solution.py:425
  (23 other events, 165.5 us)

commit v3 on v2

--- a/solution.py
+++ b/solution.py
@@ -185,7 +185,7 @@
     for source, c in ((g_mine, core), (g_sib, 1 - core)):
 
         def fetch(index, _):
-            owner = lax.rem(index, nzh) * nc + c
+            owner = lax.rem(chip + index, nzh) * nc + c
             to = (owner * (ny * nx) + index // nzh) * piece
             pltpu.make_async_copy(
                 source.at[pl.ds(pl.multiple_of(index * piece, 16), piece)],
@@ -211,56 +211,53 @@
     st = jnp.zeros_like(ss)
     rsum = lambda v: jnp.sum(v, axis=-1, keepdims=True)
     hs, dhs, scales, mus = [], [], [], []
+    sums = [[pxc[s, :, i * R : (i + 1) * R].astype(F32) for i in range(4)] for s in range(SECTIONS)]
     for s in range(SECTIONS):
-        base = pxc[s]
-        xa, xd, xb, xs = [base[:, i * R : (i + 1) * R].astype(F32) for i in range(4)]
-        for j in range(s):
-            plain, mixed = pair(place(j, s))
-            both = mm(jnp.concatenate([hs[j], dhs[j]], axis=0), plain)
-            cross = mm(hs[j], mixed)
-            xa = xa + both[:rows, :R]
-            xb = xb + both[:rows, R:]
-            xd = xd + (both[rows:, :R] + cross[:, :R])
-            xs = xs + (both[rows:, R:] + cross[:, R:])
+        xa, xd, xb, xs = sums[s]
         r = lax.rsqrt(ss / width + EPS)
         mu = r * r * r * (st / width)
         pre = r * xa
         dpre = r * xd - mu * xa
         sig = 1.0 / (1.0 + jnp.exp(-pre))
         slope = sig * (1.0 + pre * (1.0 - sig))
-        bend = sig * (1.0 - sig) * (2.0 + pre * (1.0 - 2.0 * sig))
         h = (pre * sig).astype(BF)
         dh = (slope * dpre).astype(BF)
         hs.append(h)
         dhs.append(dh)
         scales.append(r)
         mus.append(mu)
-        same, cross = block((s, 14)), block((s, 15))
-        both = mm(jnp.concatenate([h, dh], axis=0), same)
-        turn = mm(h, cross)
+        coef[s, 0] = h
+        coef[s, 1] = dh
+        stacked = jnp.concatenate([h, dh], axis=0)
+        both = mm(stacked, block((s, 14)))
+        turn = mm(h, block((s, 15)))
         xb_new = xb + both[:rows]
+        xs_new = xs + turn + both[rows:]
         h32, dh32 = h.astype(F32), dh.astype(F32)
         ss = ss + rsum(h32 * (xb + xb_new))
         st = st + rsum(dh32 * xb_new + h32 * (xs + 0.5 * turn))
-        xs_new = xs + turn + both[rows:]
+        for later in range(s + 1, SECTIONS):
+            plain, mixed = pair(place(s, later))
+            both = mm(stacked, plain)
+            cross = mm(h, mixed)
+            la, ld, lb, ls = sums[later]
+            sums[later] = [
+                la + both[:rows, :R],
+                ld + (both[rows:, :R] + cross[:, :R]),
+                lb + both[:rows, R:],
+                ls + (both[rows:, R:] + cross[:, R:]),
+            ]
+        bend = sig * (1.0 - sig) * (2.0 + pre * (1.0 - 2.0 * sig))
         for i, value in enumerate((xa, xd, xb_new, xs_new, slope, bend * dpre)):
             saved[s, i] = value
-        coef[s, 0] = h
-        coef[s, 1] = dh
 
     total = jnp.zeros_like(ss)
     dtotal = jnp.zeros_like(ss)
-    left, dleft = [None] * SECTIONS, [None] * SECTIONS
+    back = [[pxc[s, :, i * R : (i + 1) * R].astype(F32) for i in (4, 5)] for s in range(SECTIONS)]
     for s in reversed(range(SECTIONS)):
         xa, xd, xb_new, xs_new, slope, curve = [saved[s, i] for i in range(6)]
-        base = pxc[s]
-        gh = base[:, 4 * R : 5 * R].astype(F32) - total * xb_new
-        dgh = base[:, 5 * R :].astype(F32) - (dtotal * xb_new + total * xs_new)
-        for i in range(s + 1, SECTIONS):
-            plain, mixed = pair(place(s, i))
-            both = mm_nt(jnp.concatenate([left[i], dleft[i]], axis=0), plain)
-            gh = gh + both[:rows]
-            dgh = dgh + (both[rows:] + mm_nt(left[i], mixed))
+        gh = back[s][0] - total * xb_new
+        dgh = back[s][1] - (dtotal * xb_new + total * xs_new)
         ga = gh * slope
         dga = dgh * slope + gh * curve
         r, mu = scales[s], mus[s]
@@ -269,12 +266,15 @@
         h32, dh32 = hs[s].astype(F32), dhs[s].astype(F32)
         z = (-total * h32).astype(BF)
         y = (-(dtotal * h32 + total * dh32)).astype(BF)
-        left[s] = jnp.concatenate([v, z], axis=1)
-        dleft[s] = jnp.concatenate([u, y], axis=1)
-        coef[s, 2] = u
-        coef[s, 3] = v
-        coef[s, 4] = z
-        coef[s, 5] = y
+        left = jnp.concatenate([v, z], axis=1)
+        stacked = jnp.concatenate([left, jnp.concatenate([u, y], axis=1)], axis=0)
+        for early in reversed(range(s)):
+            plain, mixed = pair(place(early, s))
+            both = mm_nt(stacked, plain)
+            gh, dgh = back[early]
+            back[early] = [gh + both[:rows], dgh + (both[rows:] + mm_nt(left, mixed))]
+        for n, value in enumerate((u, v, z, y)):
+            coef[s, 2 + n] = value
         inner = rsum(ga * xa) / width
         dinner = rsum(dga * xa + ga * xd) / width
         total = total + r * r * r * inner
@@ -344,7 +344,6 @@
     first = pos_ref[1] == 0
     part = out_ref.shape[0]
     slab = x_ref.shape[1] // part
-    out_ref[:, 2 * slab :] = jnp.zeros_like(out_ref[:, 2 * slab :])
     recv, sib = recv_ref[...], sib_ref[...]
     x = jnp.concatenate([x_ref[...], jnp.where(first, recv, sib)], axis=0)
     c = jnp.concatenate([c_ref[...], jnp.where(first, sib, recv)], axis=0)
@@ -454,33 +453,39 @@
     prev_sib, after_sib = sib(prev), sib(after)
     partial = gram(pos, own, own_sib, prev, prev_sib, after, after_sib)
 
+    recv = shifted(send, "zl", 1)
+
+    arrived = lax.all_to_all(partial.reshape(ny * nx, -1, R), ("y", "x"), 0, 0, tiled=True)
+    arrived, projected = lax.optimization_barrier((arrived, projected))
     near = [projected] + [shifted(projected, "zh", -k) for k in (1, 2, 3)]
-    recv = shifted(send, "zl", 1)
-    opposite = shifted(own, "zh", 2)
-
-    arrived = lax.all_to_all(partial.reshape(ny * nx, -1, R), ("y", "x"), 0, 0, tiled=True)
-    arrived, near[1], near[3] = lax.optimization_barrier((arrived, near[1], near[3]))
     piece = jnp.sum(arrived.astype(F32), axis=0).astype(BF)
-    line = spread(piece, ("zh", "zl")).reshape(nzh, nzl, -1, R)
-    line = jnp.sum(line.astype(F32), axis=1).astype(BF).reshape(-1, R)
+    piece = (piece.astype(F32) + shifted(piece, "zl", 1).astype(F32)).astype(BF)
+    line = jnp.concatenate([piece] + [shifted(piece, "zh", -k) for k in (1, 2, 3)], axis=0)
+    line, recv = lax.optimization_barrier((line, recv))
     g_mine = spread(line, ("y", "x"))
-    g_mine, near = lax.optimization_barrier((g_mine, near))
-    parts = [v for w in near for v in (w, sib(w))]
+    projected_sib = sib(projected)
+    g_mine, near[1:], projected_sib, prev = lax.optimization_barrier(
+        (g_mine, near[1:], projected_sib, prev)
+    )
+    opposite = shifted(prev, "zh", 1)
+    parts = [projected, projected_sib] + [v for w in near[1:] for v in (w, sib(w))]
     g_sib = sib(g_mine)
 
     own3, m_part = relay(axes, width, pos, ss, parts, g_mine, g_sib)
-    own3, recv = lax.optimization_barrier((own3, recv))
+    own3, m_part, opposite = lax.optimization_barrier((own3, m_part, opposite))
     far3 = shifted(own3, "zl", 1)
     m_arrived = lax.all_to_all(m_part.reshape(ny * nx, -1, R), ("y", "x"), 0, 0, tiled=True)
+    room = m_arrived.shape[1]
+    mine = terms(pos, slab, room, keep_x, keep_c, recv, sib(recv), own3, far3)
+    m_arrived, mine = lax.optimization_barrier((m_arrived, mine))
+    opposite_sib = sib(opposite)
     m_own = jnp.sum(m_arrived.astype(F32), axis=0)
-    room = m_own.shape[0]
-    mine = terms(pos, slab, room, keep_x, keep_c, recv, sib(recv), own3, far3)
     m_own = (m_own + shifted(m_own, "zl", 1)).astype(BF)
     copies = jnp.broadcast_to(m_own[None], (ny * nx,) + m_own.shape)
     mine = lax.dynamic_update_slice(mine, copies, (0, 2 * slab, 0))
+    mine, opposite_sib = lax.optimization_barrier((mine, opposite_sib))
     arrived = lax.all_to_all(mine, ("y", "x"), 0, 0, tiled=True)
-    arrived, opposite = lax.optimization_barrier((arrived, opposite))
-    slices = [own, own_sib, after, after_sib, opposite, sib(opposite), prev, prev_sib]
+    slices = [own, own_sib, after, after_sib, opposite, opposite_sib, prev, prev_sib]
     diag_in, diag_out = finish(axes, pos, arrived, slices)
     return diag_in[None], diag_out[None]
 

time: 206 us -> 187 us (0.908)
  the two profiles are of different devices: /device:TPU:1 before, /device:TPU:2 now
where the time goes in v3:
time: 187 us; the launch traced here: 186 us
  blocking collectives  60.1 us (32%)
  waiting for transfers between devices  51.4 us (27%)
  starting transfers between devices  34.4 us (18%)
  Pallas kernels  29.6 us (16%)
  local copies, waits for them, and re-layouts  9.6 us (5%)
    all_to_all x1, blocking collectives, on_device(): arrived = lax.all_to_all(mine, ('y', 'x'), 0, 0, tiled=True)  42.2 us
    ppermute x23, waiting for transfers between devices, shifted(): lax.ppermute(value, axis, [(i, (i + steps) % count) for i in range(count)])  41.3 us
    ppermute x23, starting transfers between devices, shifted(): lax.ppermute(value, axis, [(i, (i + steps) % count) for i in range(count)])  23 us
    all_to_all x1, blocking collectives, on_device(): lax.all_to_all(partial.reshape(ny * nx, -1, R), ('y', 'x'), 0, 0, tiled=T...  17.9 us
    pallas_call x1, Pallas kernels, relay(): call(functools.partial(relay_kernel, axes, piece, float(width)), in_specs...  10.3 us
    pallas_call x1, Pallas kernels, project(): call(functools.partial(project_kernel, slab), grid=(steps,), in_specs=[pl...  7.15 us
    all_to_all x1, starting transfers between devices, on_device(): lax.all_to_all(m_part.reshape(ny * nx, -1, R), ('y', 'x'), 0, 0, tiled=True)  6.31 us
    all_to_all x1, waiting for transfers between devices, on_device(): lax.all_to_all(m_part.reshape(ny * nx, -1, R), ('y', 'x'), 0, 0, tiled=True)  5.74 us
  transfers between devices with their start and end apart: 25, of which 15 were waited for; matrix products, arithmetic and copies ran while one was open for 1% of the time, Pallas kernels for 14%

profile of v3, /device:TPU:2, one launch (start us, length us, event | category | flops | bytes accessed | tf_op | source)
XLA Modules:
  0.0 186.2 jit_solution(533882069755091335)
XLA Ops:
  2.4 3.3 %collective-permute-start.1 = (bf16[4,224,128]{2,1,0:T(8,128)(2,1)S(1)}, bf16[4,224,128]{2,1,0:T(8,128)(2,1)S(1)}, u32[]{:S(2)}, u32[]{:S(2)}) collective-permute-start(bf16[4,224,128]{2,1,0:T(8,128)(2,1)S(1)} %pad_maximum_fusion.own_ref.refs_0_), channel_id=1, source_target_pairs={{0,64},{64,128},{128,192},{192,0},{1,65},{65,129},{129,193},{193,1... | collective-permute-start | bytes 688136 | tf_op jit(solution)/shard_map/ppermute | solution.py:424
  5.8 3.1 %collective-permute-start.2 = (bf16[4,224,128]{2,1,0:T(8,128)(2,1)S(1)}, bf16[4,224,128]{2,1,0:T(8,128)(2,1)S(1)}, u32[]{:S(2)}, u32[]{:S(2)}) collective-permute-start(bf16[4,224,128]{2,1,0:T(8,128)(2,1)S(1)} %pad_maximum_fusion.own_ref.refs_0_), channel_id=1, source_target_pairs={{0,192},{64,0},{128,64},{192,128},{1,193},{65,1},{129,65},{193,129... | collective-permute-start | bytes 688136 | tf_op jit(solution)/shard_map/ppermute | solution.py:424
  9.5 7.1 %shard_map.77 = (bf16[128,768]{1,0:T(8,128)(2,1)}, f32[128,128]{1,0:T(8,128)}, bf16[128,3584]{1,0:T(8,128)(2,1)}, bf16[128,3584]{1,0:T(8,128)(2,1)}, bf16[128,3584]{1,0:T(8,128)(2,1)}) custom-call(s32[5]{0:T(128)} %stack.30.pos_ref, bf16[128,7168]{1,0:T(8,128)(2,1)} %x_ref.1, bf16[128,7168]{1,0:T(8,128)(2,1)} %c_ref.1, bf16[1,7168,128]{2,1,0:T(8,128)(2,1)} %a_ref.1, ...), custom_call_target="tpu_custom_call" | custom-call | flops 1409286144 | bytes 11010048 | tf_op jit(solution)/shard_map/pallas_call | solution.py:85
  16.7 3.8 %collective-permute-done.2.next_ref.refs_2_ = bf16[4,224,128]{2,1,0:T(8,128)(2,1)S(1)} collective-permute-done((bf16[4,224,128]{2,1,0:T(8,128)(2,1)S(1)}, bf16[4,224,128]{2,1,0:T(8,128)(2,1)S(1)}, u32[]{:S(2)}, u32[]{:S(2)}) %collective-permute-start.2) | collective-permute-done | bytes 229408 | tf_op jit(solution)/shard_map/ppermute | solution.py:424
  23.3 2.7 %shard_map.78 = bf16[2048,128]{1,0:T(8,128)(2,1)} custom-call(s32[5]{0:T(128)} %stack.30.pos_ref, bf16[4,224,128]{2,1,0:T(8,128)(2,1)} %copy-done.2, bf16[4,224,128]{2,1,0:T(8,128)(2,1)} %copy-done.7, bf16[4,224,128]{2,1,0:T(8,128)(2,1)} %copy-done.4, bf16[4,224,128]{2,1,0:T(8,128)(2,1)} %copy-done.8, bf16[4,224,128]{2,1,0:T(8,128)(2,1)} %copy-done.6, ...), custom_call_target="tpu_custom_call" | custom-call | flops 117440512 | bytes 1376256 | tf_op jit(solution)/shard_map/pallas_call | solution.py:151
  26.0 17.9 %all_to_all.20 = bf16[16,128,128]{2,1,0:T(8,128)(2,1)S(1)} all-to-all(bf16[16,128,128]{2,1,0:T(8,128)(2,1)} %bitcast.12), channel_id=1, replica_groups=mesh['zh'=4,'c'=2,'y'=4,'x'=4,'zl'=2] {'y','x'}, dimensions={0} | all-to-all | bytes 1048576 | tf_op jit(solution)/shard_map/all_to_all | solution.py:458
  44.9 3.2 %collective-permute-done.5 = bf16[128,128]{1,0:T(8,128)(2,1)S(1)} collective-permute-done((bf16[128,128]{1,0:T(8,128)(2,1)S(1)}, bf16[128,128]{1,0:T(8,128)(2,1)S(1)}, u32[]{:S(2)}, u32[]{:S(2)}) %collective-permute-start.5) | collective-permute-done | bytes 32800 | tf_op jit(solution)/shard_map/ppermute | solution.py:424
  48.1 2.8 %collective-permute-start.6 = (bf16[128,128]{1,0:T(8,128)(2,1)S(1)}, bf16[128,128]{1,0:T(8,128)(2,1)S(1)}, u32[]{:S(2)}, u32[]{:S(2)}) collective-permute-start(bf16[128,128]{1,0:T(8,128)(2,1)S(1)} %add_convert_fusion.1), channel_id=1, source_target_pairs={{0,192},{64,0},{128,64},{192,128},{1,193},{65,1},{129,65},{193,129... | collective-permute-start | bytes 98312 | tf_op jit(solution)/shard_map/ppermute | solution.py:424
  50.9 4.5 %collective-permute-start.7 = (bf16[128,128]{1,0:T(8,128)(2,1)S(1)}, bf16[128,128]{1,0:T(8,128)(2,1)S(1)}, u32[]{:S(2)}, u32[]{:S(2)}) collective-permute-start(bf16[128,128]{1,0:T(8,128)(2,1)S(1)} %add_convert_fusion.1), channel_id=1, source_target_pairs={{0,128},{64,192},{128,0},{192,64},{1,129},{65,193},{129,1},{193,65... | collective-permute-start | bytes 98312 | tf_op jit(solution)/shard_map/ppermute | solution.py:424
  55.4 3.4 %collective-permute-done.7 = bf16[128,128]{1,0:T(8,128)(2,1)S(1)} collective-permute-done((bf16[128,128]{1,0:T(8,128)(2,1)S(1)}, bf16[128,128]{1,0:T(8,128)(2,1)S(1)}, u32[]{:S(2)}, u32[]{:S(2)}) %collective-permute-start.7) | collective-permute-done | bytes 32800 | tf_op jit(solution)/shard_map/ppermute | solution.py:424
  63.3 5.1 %all-to-all-start.1 = ((bf16[16,512,128]{2,1,0:T(8,128)(2,1)}), bf16[16,512,128]{2,1,0:T(8,128)(2,1)S(1)}, u32[]{:S(2)}, u32[]{:S(2)}) async-start(bf16[16,512,128]{2,1,0:T(8,128)(2,1)} %broadcast_in_dim.8), calls=%async_computation.1 | async-start | bytes 4194304 | tf_op jit(solution)/shard_map/all_to_all | solution.py:429
  68.5 2.8 %collective-permute-start.11 = (bf16[128,768]{1,0:T(8,128)(2,1)S(1)}, bf16[128,768]{1,0:T(8,128)(2,1)S(1)}, u32[]{:S(2)}, u32[]{:S(2)}) collective-permute-start(bf16[128,768]{1,0:T(8,128)(2,1)S(1)} %copy-done.12), channel_id=1, source_target_pairs={{0,128},{64,192},{128,0},{192,64},{1,129},{65,193},{129,1},{193,65... | collective-permute-start | bytes 589832 | tf_op jit(solution)/shard_map/ppermute | solution.py:424
  73.3 12.0 %collective-permute-done.10.refs_2_ = bf16[128,768]{1,0:T(8,128)(2,1)S(1)} collective-permute-done((bf16[128,768]{1,0:T(8,128)(2,1)S(1)}, bf16[128,768]{1,0:T(8,128)(2,1)S(1)}, u32[]{:S(2)}, u32[]{:S(2)}) %collective-permute-start.10) | collective-permute-done | bytes 196640 | tf_op jit(solution)/shard_map/ppermute | solution.py:424
  85.3 3.1 %collective-permute-done.12.refs_6_ = bf16[128,768]{1,0:T(8,128)(2,1)S(1)} collective-permute-done((bf16[128,768]{1,0:T(8,128)(2,1)S(1)}, bf16[128,768]{1,0:T(8,128)(2,1)S(1)}, u32[]{:S(2)}, u32[]{:S(2)}) %collective-permute-start.12) | collective-permute-done | bytes 196640 | tf_op jit(solution)/shard_map/ppermute | solution.py:424
  89.1 4.3 %all-to-all-done.1 = bf16[16,512,128]{2,1,0:T(8,128)(2,1)S(1)} async-done(((bf16[16,512,128]{2,1,0:T(8,128)(2,1)}), bf16[16,512,128]{2,1,0:T(8,128)(2,1)S(1)}, u32[]{:S(2)}, u32[]{:S(2)}) %all-to-all-start.1) | async-done | bytes 2097184 | tf_op jit(solution)/shard_map/all_to_all | solution.py:429
  94.4 3.3 %collective-permute-done.14.refs_3_ = bf16[128,768]{1,0:T(8,128)(2,1)S(1)} collective-permute-done((bf16[128,768]{1,0:T(8,128)(2,1)}, bf16[128,768]{1,0:T(8,128)(2,1)S(1)}, u32[]{:S(2)}, u32[]{:S(2)}) %collective-permute-start.14) | collective-permute-done | bytes 196640 | tf_op jit(solution)/shard_map/ppermute | solution.py:424
  100.2 10.3 %shard_map.79 = (bf16[3,128,128]{2,1,0:T(8,128)(2,1)}, bf16[32,128,128]{2,1,0:T(8,128)(2,1)}) custom-call(s32[5]{0:T(128)} %stack.30.pos_ref, f32[128,128]{1,0:T(8,128)} %get-tuple-element.32.ss_ref, bf16[128,768]{1,0:T(8,128)(2,1)} %get-tuple-element.38.refs_0_, bf16[128,768]{1,0:T(8,128)(2,1)} %collective-permute-done.13.refs_1_, ...), custom_call_target="tpu_custom_call" | custom-call | flops 1409286144 | bytes 4194304 | tf_op jit(solution)/shard_map/pallas_call | solution.py:320
  110.5 6.3 %all-to-all-start.2 = ((bf16[16,256,128]{2,1,0:T(8,128)(2,1)}), bf16[16,256,128]{2,1,0:T(8,128)(2,1)S(1)}, u32[]{:S(2)}, u32[]{:S(2)}) async-start(bf16[16,256,128]{2,1,0:T(8,128)(2,1)} %bitcast.13), calls=%async_computation.2 | async-start | bytes 2097152 | tf_op jit(solution)/shard_map/all_to_all | solution.py:477
  117.7 4.0 %collective-permute-done.20.far_ref = bf16[3,128,128]{2,1,0:T(8,128)(2,1)S(1)} collective-permute-done((bf16[3,128,128]{2,1,0:T(8,128)(2,1)S(1)}, bf16[3,128,128]{2,1,0:T(8,128)(2,1)S(1)}, u32[]{:S(2)}, u32[]{:S(2)}) %collective-permute-start.20) | collective-permute-done | bytes 98336 | tf_op jit(solution)/shard_map/ppermute | solution.py:424
  122.4 5.5 %shard_map.80 = bf16[16,704,128]{2,1,0:T(8,128)(2,1)} custom-call(s32[5]{0:T(128)} %stack.30.pos_ref, bf16[128,3584]{1,0:T(8,128)(2,1)} %get-tuple-element.51.x_ref, bf16[128,3584]{1,0:T(8,128)(2,1)} %get-tuple-element.52.c_ref, bf16[128,3584]{1,0:T(8,128)(2,1)} %copy-done.3, bf16[128,3584]{1,0:T(8,128)(2,1)} %collective-permute-done.19.sib_ref, ...), custom_call_target="tpu_custom_call" | custom-call | flops 704643072 | bytes 5505024 | tf_op jit(solution)/shard_map/pallas_call | solution.py:366
  127.8 5.7 %all-to-all-done.2 = bf16[16,256,128]{2,1,0:T(8,128)(2,1)S(1)} async-done(((bf16[16,256,128]{2,1,0:T(8,128)(2,1)}), bf16[16,256,128]{2,1,0:T(8,128)(2,1)S(1)}, u32[]{:S(2)}, u32[]{:S(2)}) %all-to-all-start.2) | async-done | bytes 1048608 | tf_op jit(solution)/shard_map/all_to_all | solution.py:477
  134.5 4.2 %collective-permute-done.21 = f32[256,128]{1,0:T(8,128)S(1)} collective-permute-done((f32[256,128]{1,0:T(8,128)S(1)}, f32[256,128]{1,0:T(8,128)S(1)}, u32[]{:S(2)}, u32[]{:S(2)}) %collective-permute-start.21) | collective-permute-done | bytes 131104 | tf_op jit(solution)/shard_map/ppermute | solution.py:424
  140.0 42.2 %all_to_all.21.all_ref = bf16[16,704,128]{2,1,0:T(8,128)(2,1)} all-to-all(bf16[16,704,128]{2,1,0:T(8,128)(2,1)} %broadcast_dynamic-update-slice_fusion), channel_id=1, replica_groups=mesh['zh'=4,'c'=2,'y'=4,'x'=4,'zl'=2] {'y','x'}, dimensions={0} | all-to-all | bytes 5767168 | tf_op jit(solution)/shard_map/all_to_all | solution.py:487
  182.2 4.0 %shard_map.81 = (f32[224,128]{1,0:T(8,128)}, f32[224,128]{1,0:T(8,128)}) custom-call(s32[5]{0:T(128)} %stack.30.pos_ref, bf16[16,704,128]{2,1,0:T(8,128)(2,1)} %all_to_all.21.all_ref, bf16[4,224,128]{2,1,0:T(8,128)(2,1)} %copy-done.2, bf16[4,224,128]{2,1,0:T(8,128)(2,1)} %copy-done.7, bf16[4,224,128]{2,1,0:T(8,128)(2,1)} %copy-done.6, ...), custom_call_target="tpu_custom_call" | custom-call | tf_op jit(solution)/shard_map/pallas_call | solution.py:413
  (86 shorter events, 20.7 us)
Async XLA Ops:
  2.4 14.2 %collective-permute-start.1 = (bf16[4,224,128]{2,1,0:T(8,128)(2,1)S(1)}, bf16[4,224,128]{2,1,0:T(8,128)(2,1)S(1)}, u32[]{:S(2)}, u32[]{:S(2)}) collective-permute-start(bf16[4,224,128]{2,1,0:T(8,128)(2,1)S(1)} %pad_maximum_fusion.own_ref.refs_0_), channel_id=1, source_target_pairs={{0,64},{64,128},{128,192},{192,0},{1,65},{65,129},{129,193},{193,1... | collective-permute-start | bytes 688136 | tf_op jit(solution)/shard_map/ppermute | solution.py:424
  5.8 14.7 %collective-permute-start.2 = (bf16[4,224,128]{2,1,0:T(8,128)(2,1)S(1)}, bf16[4,224,128]{2,1,0:T(8,128)(2,1)S(1)}, u32[]{:S(2)}, u32[]{:S(2)}) collective-permute-start(bf16[4,224,128]{2,1,0:T(8,128)(2,1)S(1)} %pad_maximum_fusion.own_ref.refs_0_), channel_id=1, source_target_pairs={{0,192},{64,0},{128,64},{192,128},{1,193},{65,1},{129,65},{193,129... | collective-permute-start | bytes 688136 | tf_op jit(solution)/shard_map/ppermute | solution.py:424
  8.9 12.1 %collective-permute-start = (bf16[4,224,128]{2,1,0:T(8,128)(2,1)S(1)}, bf16[4,224,128]{2,1,0:T(8,128)(2,1)S(1)}, u32[]{:S(2)}, u32[]{:S(2)}) collective-permute-start(bf16[4,224,128]{2,1,0:T(8,128)(2,1)S(1)} %pad_maximum_fusion.own_ref.refs_0_), channel_id=1, source_target_pairs={{0,32},{32,0},{1,33},{33,1},{2,34},{34,2},{3,35},{35,3},{4,36},{36... | collective-permute-start | bytes 688136 | tf_op jit(solution)/shard_map/ppermute | solution.py:424
  20.5 1.8 collective-permute-start.4
  21.0 40.5 %collective-permute-start.9 = (bf16[128,3584]{1,0:T(8,128)(2,1)}, bf16[128,3584]{1,0:T(8,128)(2,1)S(1)}, u32[]{:S(2)}, u32[]{:S(2)}) collective-permute-start(bf16[128,3584]{1,0:T(8,128)(2,1)} %get-tuple-element.40), channel_id=1, source_target_pairs={{0,1},{1,0},{2,3},{3,2},{4,5},{5,4},{6,7},{7,6},{8,9},{9,8},{10,11... | collective-permute-start | bytes 2752520 | tf_op jit(solution)/shard_map/ppermute | solution.py:424
  44.1 4.0 %collective-permute-start.5 = (bf16[128,128]{1,0:T(8,128)(2,1)S(1)}, bf16[128,128]{1,0:T(8,128)(2,1)S(1)}, u32[]{:S(2)}, u32[]{:S(2)}) collective-permute-start(bf16[128,128]{1,0:T(8,128)(2,1)S(1)} %reduce_sum.21), channel_id=1, source_target_pairs={{0,1},{1,0},{2,3},{3,2},{4,5},{5,4},{6,7},{7,6},{8,9},{9,8},{10,11... | collective-permute-start | bytes 98312 | tf_op jit(solution)/shard_map/ppermute | solution.py:424
  48.1 7.3 %collective-permute-start.6 = (bf16[128,128]{1,0:T(8,128)(2,1)S(1)}, bf16[128,128]{1,0:T(8,128)(2,1)S(1)}, u32[]{:S(2)}, u32[]{:S(2)}) collective-permute-start(bf16[128,128]{1,0:T(8,128)(2,1)S(1)} %add_convert_fusion.1), channel_id=1, source_target_pairs={{0,192},{64,0},{128,64},{192,128},{1,193},{65,1},{129,65},{193,129... | collective-permute-start | bytes 98312 | tf_op jit(solution)/shard_map/ppermute | solution.py:424
  50.9 7.8 %collective-permute-start.7 = (bf16[128,128]{1,0:T(8,128)(2,1)S(1)}, bf16[128,128]{1,0:T(8,128)(2,1)S(1)}, u32[]{:S(2)}, u32[]{:S(2)}) collective-permute-start(bf16[128,128]{1,0:T(8,128)(2,1)S(1)} %add_convert_fusion.1), channel_id=1, source_target_pairs={{0,128},{64,192},{128,0},{192,64},{1,129},{65,193},{129,1},{193,65... | collective-permute-start | bytes 98312 | tf_op jit(solution)/shard_map/ppermute | solution.py:424
  55.4 6.0 %collective-permute-start.8 = (bf16[128,128]{1,0:T(8,128)(2,1)S(1)}, bf16[128,128]{1,0:T(8,128)(2,1)S(1)}, u32[]{:S(2)}, u32[]{:S(2)}) collective-permute-start(bf16[128,128]{1,0:T(8,128)(2,1)S(1)} %add_convert_fusion.1), channel_id=1, source_target_pairs={{0,64},{64,128},{128,192},{192,0},{1,65},{65,129},{129,193},{193,1... | collective-permute-start | bytes 98312 | tf_op jit(solution)/shard_map/ppermute | solution.py:424
  63.3 30.1 %all-to-all-start.1 = ((bf16[16,512,128]{2,1,0:T(8,128)(2,1)}), bf16[16,512,128]{2,1,0:T(8,128)(2,1)S(1)}, u32[]{:S(2)}, u32[]{:S(2)}) async-start(bf16[16,512,128]{2,1,0:T(8,128)(2,1)} %broadcast_in_dim.8), calls=%async_computation.1 | async-start | bytes 4194304 | tf_op jit(solution)/shard_map/all_to_all | solution.py:429
  68.4 16.9 %collective-permute-start.10 = (bf16[128,768]{1,0:T(8,128)(2,1)S(1)}, bf16[128,768]{1,0:T(8,128)(2,1)S(1)}, u32[]{:S(2)}, u32[]{:S(2)}) collective-permute-start(bf16[128,768]{1,0:T(8,128)(2,1)S(1)} %copy-done.12), channel_id=1, source_target_pairs={{0,192},{64,0},{128,64},{192,128},{1,193},{65,1},{129,65},{193,129... | collective-permute-start | bytes 589832 | tf_op jit(solution)/shard_map/ppermute | solution.py:424
  68.5 16.8 %collective-permute-start.11 = (bf16[128,768]{1,0:T(8,128)(2,1)S(1)}, bf16[128,768]{1,0:T(8,128)(2,1)S(1)}, u32[]{:S(2)}, u32[]{:S(2)}) collective-permute-start(bf16[128,768]{1,0:T(8,128)(2,1)S(1)} %copy-done.12), channel_id=1, source_target_pairs={{0,128},{64,192},{128,0},{192,64},{1,129},{65,193},{129,1},{193,65... | collective-permute-start | bytes 589832 | tf_op jit(solution)/shard_map/ppermute | solution.py:424
  71.3 17.2 %collective-permute-start.12 = (bf16[128,768]{1,0:T(8,128)(2,1)S(1)}, bf16[128,768]{1,0:T(8,128)(2,1)S(1)}, u32[]{:S(2)}, u32[]{:S(2)}) collective-permute-start(bf16[128,768]{1,0:T(8,128)(2,1)S(1)} %copy-done.12), channel_id=1, source_target_pairs={{0,64},{64,128},{128,192},{192,0},{1,65},{65,129},{129,193},{193,1... | collective-permute-start | bytes 589832 | tf_op jit(solution)/shard_map/ppermute | solution.py:424
  73.3 15.8 %collective-permute-start.13 = (bf16[128,768]{1,0:T(8,128)(2,1)S(1)}, bf16[128,768]{1,0:T(8,128)(2,1)}, u32[]{:S(2)}, u32[]{:S(2)}) collective-permute-start(bf16[128,768]{1,0:T(8,128)(2,1)S(1)} %copy-done.12), channel_id=1, source_target_pairs={{0,32},{32,0},{1,33},{33,1},{2,34},{34,2},{3,35},{35,3},{4,36},{36... | collective-permute-start | bytes 589832 | tf_op jit(solution)/shard_map/ppermute | solution.py:424
  93.4 5.0 %collective-permute-start.17 = (bf16[8192,128]{1,0:T(8,128)(2,1)S(1)}, bf16[8192,128]{1,0:T(8,128)(2,1)S(1)}, u32[]{:S(2)}, u32[]{:S(2)}) collective-permute-start(bf16[8192,128]{1,0:T(8,128)(2,1)S(1)} %bitcast.10), channel_id=1, source_target_pairs={{0,32},{32,0},{1,33},{33,1},{2,34},{34,2},{3,35},{35,3},{4,36},{36... | collective-permute-start | bytes 6291464 | tf_op jit(solution)/shard_map/ppermute | solution.py:424
  93.4 4.3 %collective-permute-start.14 = (bf16[128,768]{1,0:T(8,128)(2,1)}, bf16[128,768]{1,0:T(8,128)(2,1)S(1)}, u32[]{:S(2)}, u32[]{:S(2)}) collective-permute-start(bf16[128,768]{1,0:T(8,128)(2,1)} %copy-done.13), channel_id=1, source_target_pairs={{0,32},{32,0},{1,33},{33,1},{2,34},{34,2},{3,35},{35,3},{4,36},{36... | collective-permute-start | bytes 589832 | tf_op jit(solution)/shard_map/ppermute | solution.py:424
  93.9 4.2 %collective-permute-start.15 = (bf16[128,768]{1,0:T(8,128)(2,1)}, bf16[128,768]{1,0:T(8,128)(2,1)S(1)}, u32[]{:S(2)}, u32[]{:S(2)}) collective-permute-start(bf16[128,768]{1,0:T(8,128)(2,1)} %copy-done.14), channel_id=1, source_target_pairs={{0,32},{32,0},{1,33},{33,1},{2,34},{34,2},{3,35},{35,3},{4,36},{36... | collective-permute-start | bytes 589832 | tf_op jit(solution)/shard_map/ppermute | solution.py:424
  93.9 4.3 %collective-permute-start.16 = (bf16[128,768]{1,0:T(8,128)(2,1)}, bf16[128,768]{1,0:T(8,128)(2,1)S(1)}, u32[]{:S(2)}, u32[]{:S(2)}) collective-permute-start(bf16[128,768]{1,0:T(8,128)(2,1)} %copy-done.15), channel_id=1, source_target_pairs={{0,32},{32,0},{1,33},{33,1},{2,34},{34,2},{3,35},{35,3},{4,36},{36... | collective-permute-start | bytes 589832 | tf_op jit(solution)/shard_map/ppermute | solution.py:424
  94.4 16.1 %collective-permute-start.18 = (bf16[4,224,128]{2,1,0:T(8,128)(2,1)S(1)}, bf16[4,224,128]{2,1,0:T(8,128)(2,1)S(1)}, u32[]{:S(2)}, u32[]{:S(2)}) collective-permute-start(bf16[4,224,128]{2,1,0:T(8,128)(2,1)S(1)} %copy-done.5), channel_id=1, source_target_pairs={{0,64},{64,128},{128,192},{192,0},{1,65},{65,129},{129,193},{193,1... | collective-permute-start | bytes 688136 | tf_op jit(solution)/shard_map/ppermute | solution.py:424
  97.7 20.0 %collective-permute-start.19 = (bf16[128,3584]{1,0:T(8,128)(2,1)S(1)}, bf16[128,3584]{1,0:T(8,128)(2,1)}, u32[]{:S(2)}, u32[]{:S(2)}) collective-permute-start(bf16[128,3584]{1,0:T(8,128)(2,1)S(1)} %collective-permute-done.9.recv_ref), channel_id=1, source_target_pairs={{0,32},{32,0},{1,33},{33,1},{2,34},{34,2},{3,35},{35,3},{4,36},{36... | collective-permute-start | bytes 2752520 | tf_op jit(solution)/shard_map/ppermute | solution.py:424
  110.5 23.0 %all-to-all-start.2 = ((bf16[16,256,128]{2,1,0:T(8,128)(2,1)}), bf16[16,256,128]{2,1,0:T(8,128)(2,1)S(1)}, u32[]{:S(2)}, u32[]{:S(2)}) async-start(bf16[16,256,128]{2,1,0:T(8,128)(2,1)} %bitcast.13), calls=%async_computation.2 | async-start | bytes 2097152 | tf_op jit(solution)/shard_map/all_to_all | solution.py:477
  116.9 4.9 %collective-permute-start.20 = (bf16[3,128,128]{2,1,0:T(8,128)(2,1)S(1)}, bf16[3,128,128]{2,1,0:T(8,128)(2,1)S(1)}, u32[]{:S(2)}, u32[]{:S(2)}) collective-permute-start(bf16[3,128,128]{2,1,0:T(8,128)(2,1)S(1)} %copy-done.19), channel_id=1, source_target_pairs={{0,1},{1,0},{2,3},{3,2},{4,5},{5,4},{6,7},{7,6},{8,9},{9,8},{10,11... | collective-permute-start | bytes 294920 | tf_op jit(solution)/shard_map/ppermute | solution.py:424
  133.7 5.1 %collective-permute-start.21 = (f32[256,128]{1,0:T(8,128)S(1)}, f32[256,128]{1,0:T(8,128)S(1)}, u32[]{:S(2)}, u32[]{:S(2)}) collective-permute-start(f32[256,128]{1,0:T(8,128)S(1)} %convert_reduce_fusion), channel_id=1, source_target_pairs={{0,1},{1,0},{2,3},{3,2},{4,5},{5,4},{6,7},{7,6},{8,9},{9,8},{10,11... | collective-permute-start | bytes 393224 | tf_op jit(solution)/shard_map/ppermute | solution.py:424
  134.5 5.5 %collective-permute-start.22 = (bf16[4,224,128]{2,1,0:T(8,128)(2,1)S(1)}, bf16[4,224,128]{2,1,0:T(8,128)(2,1)S(1)}, u32[]{:S(2)}, u32[]{:S(2)}) collective-permute-start(bf16[4,224,128]{2,1,0:T(8,128)(2,1)S(1)} %collective-permute-done.18.refs_4_), channel_id=1, source_target_pairs={{0,32},{32,0},{1,33},{33,1},{2,34},{34,2},{3,35},{35,3},{4,36},{36... | collective-permute-start | bytes 688136 | tf_op jit(solution)/shard_map/ppermute | solution.py:424
  (22 other events, 192.0 us)

commit v4 on v3

--- a/solution.py
+++ b/solution.py
@@ -369,7 +369,7 @@
         in_specs=[pl.BlockSpec(memory_space=pltpu.SMEM), wide, wide, wide, wide, small, small],
         out_specs=pl.BlockSpec((part, 2 * slab + room, R), lambda i: (i, 0, 0)),
         out_shape=jax.ShapeDtypeStruct((width // slab, 2 * slab + room, R), BF),
-        compiler_params=pltpu.CompilerParams(vmem_limit_bytes=60 * 1024 * 1024),
+        compiler_params=pltpu.CompilerParams(vmem_limit_bytes=14 * 1024 * 1024),
         cost_estimate=pl.CostEstimate(
             flops=4 * rows * width * 3 * R, bytes_accessed=12 * rows * width, transcendentals=0
         ),
@@ -415,7 +415,7 @@
         in_specs=[pl.BlockSpec(memory_space=pltpu.SMEM)] + [vm] * 9,
         out_specs=[vm, vm],
         out_shape=[shape, shape],
-        compiler_params=pltpu.CompilerParams(vmem_limit_bytes=60 * 1024 * 1024),
+        compiler_params=pltpu.CompilerParams(vmem_limit_bytes=16 * 1024 * 1024),
     )(pos, arrived, *slices)
 
 

time: 187 us -> 184 us (0.984)
  Pallas kernels: 29.6 us -> 24.9 us
    pallas_call x1, Pallas kernels: 5.48 us -> 2.65 us  [terms(): call(terms_kernel, grid=(steps,), in_specs=[pl.BlockSpec(memory_space=plt...]
    unnamed x42 -> x56, local copies, waits for them, and re-layouts: 4.24 us -> 6.79 us
  transfers between devices with their start and end apart: 25 -> 25, of which waited for: 15 -> 15; matrix products, arithmetic and copies ran while one was open for 1% -> 1% of each run, Pallas kernels for 14% -> 12%
where the time goes in v4:
time: 184 us; the launch traced here: 183 us
  blocking collectives  58.8 us (32%)
  waiting for transfers between devices  51.3 us (28%)
  starting transfers between devices  34.7 us (19%)
  Pallas kernels  24.9 us (14%)
  local copies, waits for them, and re-layouts  11.1 us (6%)
    all_to_all x1, blocking collectives, on_device(): arrived = lax.all_to_all(mine, ('y', 'x'), 0, 0, tiled=True)  40.8 us
    ppermute x23, waiting for transfers between devices, shifted(): lax.ppermute(value, axis, [(i, (i + steps) % count) for i in range(count)])  40.6 us
    ppermute x23, starting transfers between devices, shifted(): lax.ppermute(value, axis, [(i, (i + steps) % count) for i in range(count)])  22.1 us
    all_to_all x1, blocking collectives, on_device(): lax.all_to_all(partial.reshape(ny * nx, -1, R), ('y', 'x'), 0, 0, tiled=T...  17.9 us
    pallas_call x1, Pallas kernels, relay(): call(functools.partial(relay_kernel, axes, piece, float(width)), in_specs...  10.3 us
    pallas_call x1, Pallas kernels, project(): call(functools.partial(project_kernel, slab), grid=(steps,), in_specs=[pl...  7.14 us
    all_to_all x1, starting transfers between devices, on_device(): lax.all_to_all(m_part.reshape(ny * nx, -1, R), ('y', 'x'), 0, 0, tiled=True)  6.86 us
    unnamed x56, local copies, waits for them, and re-layouts  6.79 us
  transfers between devices with their start and end apart: 25, of which 15 were waited for; matrix products, arithmetic and copies ran while one was open for 1% of the time, Pallas kernels for 12%

profile of v4, /device:TPU:2, one launch (start us, length us, event | category | flops | bytes accessed | tf_op | source)
XLA Modules:
  0.0 183.2 jit_solution(8620065826187293979)
XLA Ops:
  2.4 3.3 %collective-permute-start.1 = (bf16[4,224,128]{2,1,0:T(8,128)(2,1)S(1)}, bf16[4,224,128]{2,1,0:T(8,128)(2,1)S(1)}, u32[]{:S(2)}, u32[]{:S(2)}) collective-permute-start(bf16[4,224,128]{2,1,0:T(8,128)(2,1)S(1)} %pad_maximum_fusion.own_ref.refs_0_), channel_id=1, source_target_pairs={{0,64},{64,128},{128,192},{192,0},{1,65},{65,129},{129,193},{193,1... | collective-permute-start | bytes 688136 | tf_op jit(solution)/shard_map/ppermute | solution.py:424
  5.8 3.1 %collective-permute-start.2 = (bf16[4,224,128]{2,1,0:T(8,128)(2,1)S(1)}, bf16[4,224,128]{2,1,0:T(8,128)(2,1)S(1)}, u32[]{:S(2)}, u32[]{:S(2)}) collective-permute-start(bf16[4,224,128]{2,1,0:T(8,128)(2,1)S(1)} %pad_maximum_fusion.own_ref.refs_0_), channel_id=1, source_target_pairs={{0,192},{64,0},{128,64},{192,128},{1,193},{65,1},{129,65},{193,129... | collective-permute-start | bytes 688136 | tf_op jit(solution)/shard_map/ppermute | solution.py:424
  9.4 7.1 %shard_map.77 = (bf16[128,768]{1,0:T(8,128)(2,1)}, f32[128,128]{1,0:T(8,128)}, bf16[128,3584]{1,0:T(8,128)(2,1)}, bf16[128,3584]{1,0:T(8,128)(2,1)}, bf16[128,3584]{1,0:T(8,128)(2,1)}) custom-call(s32[5]{0:T(128)} %stack.30.pos_ref, bf16[128,7168]{1,0:T(8,128)(2,1)} %x_ref.1, bf16[128,7168]{1,0:T(8,128)(2,1)} %c_ref.1, bf16[1,7168,128]{2,1,0:T(8,128)(2,1)} %a_ref.1, ...), custom_call_target="tpu_custom_call" | custom-call | flops 1409286144 | bytes 11010048 | tf_op jit(solution)/shard_map/pallas_call | solution.py:85
  16.6 3.9 %collective-permute-done.2.next_ref.refs_2_ = bf16[4,224,128]{2,1,0:T(8,128)(2,1)S(1)} collective-permute-done((bf16[4,224,128]{2,1,0:T(8,128)(2,1)S(1)}, bf16[4,224,128]{2,1,0:T(8,128)(2,1)S(1)}, u32[]{:S(2)}, u32[]{:S(2)}) %collective-permute-start.2) | collective-permute-done | bytes 229408 | tf_op jit(solution)/shard_map/ppermute | solution.py:424
  23.4 2.7 %shard_map.78 = bf16[2048,128]{1,0:T(8,128)(2,1)} custom-call(s32[5]{0:T(128)} %stack.30.pos_ref, bf16[4,224,128]{2,1,0:T(8,128)(2,1)} %copy-done, bf16[4,224,128]{2,1,0:T(8,128)(2,1)} %copy-done.12, bf16[4,224,128]{2,1,0:T(8,128)(2,1)} %copy-done.8, bf16[4,224,128]{2,1,0:T(8,128)(2,1)} %copy-done.14, bf16[4,224,128]{2,1,0:T(8,128)(2,1)} %copy-done.10, ...), custom_call_target="tpu_custom_call" | custom-call | flops 117440512 | bytes 1376256 | tf_op jit(solution)/shard_map/pallas_call | solution.py:151
  26.1 17.9 %all_to_all.20 = bf16[16,128,128]{2,1,0:T(8,128)(2,1)S(1)} all-to-all(bf16[16,128,128]{2,1,0:T(8,128)(2,1)} %bitcast.10), channel_id=1, replica_groups=mesh['zh'=4,'c'=2,'y'=4,'x'=4,'zl'=2] {'y','x'}, dimensions={0} | all-to-all | bytes 1048576 | tf_op jit(solution)/shard_map/all_to_all | solution.py:458
  44.9 3.2 %collective-permute-done.5 = bf16[128,128]{1,0:T(8,128)(2,1)S(1)} collective-permute-done((bf16[128,128]{1,0:T(8,128)(2,1)S(1)}, bf16[128,128]{1,0:T(8,128)(2,1)S(1)}, u32[]{:S(2)}, u32[]{:S(2)}) %collective-permute-start.5) | collective-permute-done | bytes 32800 | tf_op jit(solution)/shard_map/ppermute | solution.py:424
  48.1 2.8 %collective-permute-start.6 = (bf16[128,128]{1,0:T(8,128)(2,1)S(1)}, bf16[128,128]{1,0:T(8,128)(2,1)S(1)}, u32[]{:S(2)}, u32[]{:S(2)}) collective-permute-start(bf16[128,128]{1,0:T(8,128)(2,1)S(1)} %add_convert_fusion.1), channel_id=1, source_target_pairs={{0,192},{64,0},{128,64},{192,128},{1,193},{65,1},{129,65},{193,129... | collective-permute-start | bytes 98312 | tf_op jit(solution)/shard_map/ppermute | solution.py:424
  50.9 4.5 %collective-permute-start.7 = (bf16[128,128]{1,0:T(8,128)(2,1)S(1)}, bf16[128,128]{1,0:T(8,128)(2,1)S(1)}, u32[]{:S(2)}, u32[]{:S(2)}) collective-permute-start(bf16[128,128]{1,0:T(8,128)(2,1)S(1)} %add_convert_fusion.1), channel_id=1, source_target_pairs={{0,128},{64,192},{128,0},{192,64},{1,129},{65,193},{129,1},{193,65... | collective-permute-start | bytes 98312 | tf_op jit(solution)/shard_map/ppermute | solution.py:424
  55.4 3.4 %collective-permute-done.7 = bf16[128,128]{1,0:T(8,128)(2,1)S(1)} collective-permute-done((bf16[128,128]{1,0:T(8,128)(2,1)S(1)}, bf16[128,128]{1,0:T(8,128)(2,1)S(1)}, u32[]{:S(2)}, u32[]{:S(2)}) %collective-permute-start.7) | collective-permute-done | bytes 32800 | tf_op jit(solution)/shard_map/ppermute | solution.py:424
  58.8 2.7 %collective-permute-done.8 = bf16[128,128]{1,0:T(8,128)(2,1)S(1)} collective-permute-done((bf16[128,128]{1,0:T(8,128)(2,1)S(1)}, bf16[128,128]{1,0:T(8,128)(2,1)S(1)}, u32[]{:S(2)}, u32[]{:S(2)}) %collective-permute-start.8) | collective-permute-done | bytes 32800 | tf_op jit(solution)/shard_map/ppermute | solution.py:424
  63.2 5.8 %all-to-all-start.1 = ((bf16[16,512,128]{2,1,0:T(8,128)(2,1)}), bf16[16,512,128]{2,1,0:T(8,128)(2,1)}, u32[]{:S(2)}, u32[]{:S(2)}) async-start(bf16[16,512,128]{2,1,0:T(8,128)(2,1)} %broadcast_in_dim.8), calls=%async_computation.1 | async-start | bytes 4194304 | tf_op jit(solution)/shard_map/all_to_all | solution.py:429
  69.1 2.8 %collective-permute-start.11 = (bf16[128,768]{1,0:T(8,128)(2,1)S(1)}, bf16[128,768]{1,0:T(8,128)(2,1)S(1)}, u32[]{:S(2)}, u32[]{:S(2)}) collective-permute-start(bf16[128,768]{1,0:T(8,128)(2,1)S(1)} %copy-done.20), channel_id=1, source_target_pairs={{0,128},{64,192},{128,0},{192,64},{1,129},{65,193},{129,1},{193,65... | collective-permute-start | bytes 589832 | tf_op jit(solution)/shard_map/ppermute | solution.py:424
  73.9 11.3 %collective-permute-done.10.refs_2_ = bf16[128,768]{1,0:T(8,128)(2,1)S(1)} collective-permute-done((bf16[128,768]{1,0:T(8,128)(2,1)S(1)}, bf16[128,768]{1,0:T(8,128)(2,1)S(1)}, u32[]{:S(2)}, u32[]{:S(2)}) %collective-permute-start.10) | collective-permute-done | bytes 196640 | tf_op jit(solution)/shard_map/ppermute | solution.py:424
  85.2 2.8 %collective-permute-done.12.refs_6_ = bf16[128,768]{1,0:T(8,128)(2,1)S(1)} collective-permute-done((bf16[128,768]{1,0:T(8,128)(2,1)S(1)}, bf16[128,768]{1,0:T(8,128)(2,1)S(1)}, u32[]{:S(2)}, u32[]{:S(2)}) %collective-permute-start.12) | collective-permute-done | bytes 196640 | tf_op jit(solution)/shard_map/ppermute | solution.py:424
  88.0 6.1 %all-to-all-done.1 = bf16[16,512,128]{2,1,0:T(8,128)(2,1)} async-done(((bf16[16,512,128]{2,1,0:T(8,128)(2,1)}), bf16[16,512,128]{2,1,0:T(8,128)(2,1)}, u32[]{:S(2)}, u32[]{:S(2)}) %all-to-all-start.1) | async-done | bytes 2097184 | tf_op jit(solution)/shard_map/all_to_all | solution.py:429
  95.1 3.0 %collective-permute-done.14.refs_3_ = bf16[128,768]{1,0:T(8,128)(2,1)S(1)} collective-permute-done((bf16[128,768]{1,0:T(8,128)(2,1)S(1)}, bf16[128,768]{1,0:T(8,128)(2,1)S(1)}, u32[]{:S(2)}, u32[]{:S(2)}) %collective-permute-start.14) | collective-permute-done | bytes 196640 | tf_op jit(solution)/shard_map/ppermute | solution.py:424
  99.5 10.3 %shard_map.79 = (bf16[3,128,128]{2,1,0:T(8,128)(2,1)}, bf16[32,128,128]{2,1,0:T(8,128)(2,1)}) custom-call(s32[5]{0:T(128)} %stack.30.pos_ref, f32[128,128]{1,0:T(8,128)} %get-tuple-element.32.ss_ref, bf16[128,768]{1,0:T(8,128)(2,1)} %get-tuple-element.38.refs_0_, bf16[128,768]{1,0:T(8,128)(2,1)} %copy-done.24, bf16[128,768]{1,0:T(8,128)(2,1)} %copy-done.21, ...), custom_call_target="tpu_custom_call" | custom-call | flops 1409286144 | bytes 4194304 | tf_op jit(solution)/shard_map/pallas_call | solution.py:320
  109.8 6.9 %all-to-all-start.2 = ((bf16[16,256,128]{2,1,0:T(8,128)(2,1)}), bf16[16,256,128]{2,1,0:T(8,128)(2,1)}, u32[]{:S(2)}, u32[]{:S(2)}) async-start(bf16[16,256,128]{2,1,0:T(8,128)(2,1)} %bitcast.11), calls=%async_computation.2 | async-start | bytes 2097152 | tf_op jit(solution)/shard_map/all_to_all | solution.py:477
  118.0 3.5 %collective-permute-done.20.far_ref = bf16[3,128,128]{2,1,0:T(8,128)(2,1)S(1)} collective-permute-done((bf16[3,128,128]{2,1,0:T(8,128)(2,1)S(1)}, bf16[3,128,128]{2,1,0:T(8,128)(2,1)S(1)}, u32[]{:S(2)}, u32[]{:S(2)}) %collective-permute-start.20) | collective-permute-done | bytes 98336 | tf_op jit(solution)/shard_map/ppermute | solution.py:424
  126.2 2.7 %shard_map.80 = bf16[16,704,128]{2,1,0:T(8,128)(2,1)S(1)} custom-call(s32[5]{0:T(128)S(1)} %copy-done.19, bf16[128,3584]{1,0:T(8,128)(2,1)S(1)} %copy-done.2, bf16[128,3584]{1,0:T(8,128)(2,1)S(1)} %copy-done.3, bf16[128,3584]{1,0:T(8,128)(2,1)S(1)} %copy-done.5, bf16[128,3584]{1,0:T(8,128)(2,1)S(1)} %copy-done.7, bf16[3,128,128]{2,1,0:T(8,128)(2,1)S(1)} %copy-done.18, ...), custom_call_target="tpu_custom_call" | custom-call | flops 704643072 | bytes 5505024 | tf_op jit(solution)/shard_map/pallas_call | solution.py:366
  128.9 4.6 %all-to-all-done.2 = bf16[16,256,128]{2,1,0:T(8,128)(2,1)} async-done(((bf16[16,256,128]{2,1,0:T(8,128)(2,1)}), bf16[16,256,128]{2,1,0:T(8,128)(2,1)}, u32[]{:S(2)}, u32[]{:S(2)}) %all-to-all-start.2) | async-done | bytes 1048608 | tf_op jit(solution)/shard_map/all_to_all | solution.py:477
  135.2 4.7 %collective-permute-done.21 = f32[256,128]{1,0:T(8,128)S(1)} collective-permute-done((f32[256,128]{1,0:T(8,128)S(1)}, f32[256,128]{1,0:T(8,128)S(1)}, u32[]{:S(2)}, u32[]{:S(2)}) %collective-permute-start.21) | collective-permute-done | bytes 131104 | tf_op jit(solution)/shard_map/ppermute | solution.py:424
  140.2 40.8 %all_to_all.21.all_ref = bf16[16,704,128]{2,1,0:T(8,128)(2,1)S(1)} all-to-all(bf16[16,704,128]{2,1,0:T(8,128)(2,1)S(1)} %broadcast_dynamic-update-slice_fusion), channel_id=1, replica_groups=mesh['zh'=4,'c'=2,'y'=4,'x'=4,'zl'=2] {'y','x'}, dimensions={0} | all-to-all | bytes 5767168 | tf_op jit(solution)/shard_map/all_to_all | solution.py:487
  (100 shorter events, 22.5 us)
Async XLA Ops:
  2.4 14.2 %collective-permute-start.1 = (bf16[4,224,128]{2,1,0:T(8,128)(2,1)S(1)}, bf16[4,224,128]{2,1,0:T(8,128)(2,1)S(1)}, u32[]{:S(2)}, u32[]{:S(2)}) collective-permute-start(bf16[4,224,128]{2,1,0:T(8,128)(2,1)S(1)} %pad_maximum_fusion.own_ref.refs_0_), channel_id=1, source_target_pairs={{0,64},{64,128},{128,192},{192,0},{1,65},{65,129},{129,193},{193,1... | collective-permute-start | bytes 688136 | tf_op jit(solution)/shard_map/ppermute | solution.py:424
  5.8 14.7 %collective-permute-start.2 = (bf16[4,224,128]{2,1,0:T(8,128)(2,1)S(1)}, bf16[4,224,128]{2,1,0:T(8,128)(2,1)S(1)}, u32[]{:S(2)}, u32[]{:S(2)}) collective-permute-start(bf16[4,224,128]{2,1,0:T(8,128)(2,1)S(1)} %pad_maximum_fusion.own_ref.refs_0_), channel_id=1, source_target_pairs={{0,192},{64,0},{128,64},{192,128},{1,193},{65,1},{129,65},{193,129... | collective-permute-start | bytes 688136 | tf_op jit(solution)/shard_map/ppermute | solution.py:424
  8.9 12.1 %collective-permute-start = (bf16[4,224,128]{2,1,0:T(8,128)(2,1)S(1)}, bf16[4,224,128]{2,1,0:T(8,128)(2,1)S(1)}, u32[]{:S(2)}, u32[]{:S(2)}) collective-permute-start(bf16[4,224,128]{2,1,0:T(8,128)(2,1)S(1)} %pad_maximum_fusion.own_ref.refs_0_), channel_id=1, source_target_pairs={{0,32},{32,0},{1,33},{33,1},{2,34},{34,2},{3,35},{35,3},{4,36},{36... | collective-permute-start | bytes 688136 | tf_op jit(solution)/shard_map/ppermute | solution.py:424
  20.5 1.8 collective-permute-start.4
  21.0 40.5 %collective-permute-start.9 = (bf16[128,3584]{1,0:T(8,128)(2,1)}, bf16[128,3584]{1,0:T(8,128)(2,1)S(1)}, u32[]{:S(2)}, u32[]{:S(2)}) collective-permute-start(bf16[128,3584]{1,0:T(8,128)(2,1)} %get-tuple-element.40), channel_id=1, source_target_pairs={{0,1},{1,0},{2,3},{3,2},{4,5},{5,4},{6,7},{7,6},{8,9},{9,8},{10,11... | collective-permute-start | bytes 2752520 | tf_op jit(solution)/shard_map/ppermute | solution.py:424
  44.1 4.0 %collective-permute-start.5 = (bf16[128,128]{1,0:T(8,128)(2,1)S(1)}, bf16[128,128]{1,0:T(8,128)(2,1)S(1)}, u32[]{:S(2)}, u32[]{:S(2)}) collective-permute-start(bf16[128,128]{1,0:T(8,128)(2,1)S(1)} %reduce_sum.21), channel_id=1, source_target_pairs={{0,1},{1,0},{2,3},{3,2},{4,5},{5,4},{6,7},{7,6},{8,9},{9,8},{10,11... | collective-permute-start | bytes 98312 | tf_op jit(solution)/shard_map/ppermute | solution.py:424
  48.1 7.3 %collective-permute-start.6 = (bf16[128,128]{1,0:T(8,128)(2,1)S(1)}, bf16[128,128]{1,0:T(8,128)(2,1)S(1)}, u32[]{:S(2)}, u32[]{:S(2)}) collective-permute-start(bf16[128,128]{1,0:T(8,128)(2,1)S(1)} %add_convert_fusion.1), channel_id=1, source_target_pairs={{0,192},{64,0},{128,64},{192,128},{1,193},{65,1},{129,65},{193,129... | collective-permute-start | bytes 98312 | tf_op jit(solution)/shard_map/ppermute | solution.py:424
  50.9 7.8 %collective-permute-start.7 = (bf16[128,128]{1,0:T(8,128)(2,1)S(1)}, bf16[128,128]{1,0:T(8,128)(2,1)S(1)}, u32[]{:S(2)}, u32[]{:S(2)}) collective-permute-start(bf16[128,128]{1,0:T(8,128)(2,1)S(1)} %add_convert_fusion.1), channel_id=1, source_target_pairs={{0,128},{64,192},{128,0},{192,64},{1,129},{65,193},{129,1},{193,65... | collective-permute-start | bytes 98312 | tf_op jit(solution)/shard_map/ppermute | solution.py:424
  55.4 6.0 %collective-permute-start.8 = (bf16[128,128]{1,0:T(8,128)(2,1)S(1)}, bf16[128,128]{1,0:T(8,128)(2,1)S(1)}, u32[]{:S(2)}, u32[]{:S(2)}) collective-permute-start(bf16[128,128]{1,0:T(8,128)(2,1)S(1)} %add_convert_fusion.1), channel_id=1, source_target_pairs={{0,64},{64,128},{128,192},{192,0},{1,65},{65,129},{129,193},{193,1... | collective-permute-start | bytes 98312 | tf_op jit(solution)/shard_map/ppermute | solution.py:424
  63.2 30.8 %all-to-all-start.1 = ((bf16[16,512,128]{2,1,0:T(8,128)(2,1)}), bf16[16,512,128]{2,1,0:T(8,128)(2,1)}, u32[]{:S(2)}, u32[]{:S(2)}) async-start(bf16[16,512,128]{2,1,0:T(8,128)(2,1)} %broadcast_in_dim.8), calls=%async_computation.1 | async-start | bytes 4194304 | tf_op jit(solution)/shard_map/all_to_all | solution.py:429
  69.0 16.1 %collective-permute-start.10 = (bf16[128,768]{1,0:T(8,128)(2,1)S(1)}, bf16[128,768]{1,0:T(8,128)(2,1)S(1)}, u32[]{:S(2)}, u32[]{:S(2)}) collective-permute-start(bf16[128,768]{1,0:T(8,128)(2,1)S(1)} %copy-done.20), channel_id=1, source_target_pairs={{0,192},{64,0},{128,64},{192,128},{1,193},{65,1},{129,65},{193,129... | collective-permute-start | bytes 589832 | tf_op jit(solution)/shard_map/ppermute | solution.py:424
  69.1 16.1 %collective-permute-start.11 = (bf16[128,768]{1,0:T(8,128)(2,1)S(1)}, bf16[128,768]{1,0:T(8,128)(2,1)S(1)}, u32[]{:S(2)}, u32[]{:S(2)}) collective-permute-start(bf16[128,768]{1,0:T(8,128)(2,1)S(1)} %copy-done.20), channel_id=1, source_target_pairs={{0,128},{64,192},{128,0},{192,64},{1,129},{65,193},{129,1},{193,65... | collective-permute-start | bytes 589832 | tf_op jit(solution)/shard_map/ppermute | solution.py:424
  71.9 16.1 %collective-permute-start.12 = (bf16[128,768]{1,0:T(8,128)(2,1)S(1)}, bf16[128,768]{1,0:T(8,128)(2,1)S(1)}, u32[]{:S(2)}, u32[]{:S(2)}) collective-permute-start(bf16[128,768]{1,0:T(8,128)(2,1)S(1)} %copy-done.20), channel_id=1, source_target_pairs={{0,64},{64,128},{128,192},{192,0},{1,65},{65,129},{129,193},{193,1... | collective-permute-start | bytes 589832 | tf_op jit(solution)/shard_map/ppermute | solution.py:424
  73.9 14.1 %collective-permute-start.13 = (bf16[128,768]{1,0:T(8,128)(2,1)S(1)}, bf16[128,768]{1,0:T(8,128)(2,1)S(1)}, u32[]{:S(2)}, u32[]{:S(2)}) collective-permute-start(bf16[128,768]{1,0:T(8,128)(2,1)S(1)} %copy-done.20), channel_id=1, source_target_pairs={{0,32},{32,0},{1,33},{33,1},{2,34},{34,2},{3,35},{35,3},{4,36},{36... | collective-permute-start | bytes 589832 | tf_op jit(solution)/shard_map/ppermute | solution.py:424
  94.1 5.3 %collective-permute-start.17 = (bf16[8192,128]{1,0:T(8,128)(2,1)}, bf16[8192,128]{1,0:T(8,128)(2,1)}, u32[]{:S(2)}, u32[]{:S(2)}) collective-permute-start(bf16[8192,128]{1,0:T(8,128)(2,1)} %bitcast.6.refs_8_), channel_id=1, source_target_pairs={{0,32},{32,0},{1,33},{33,1},{2,34},{34,2},{3,35},{35,3},{4,36},{36... | collective-permute-start | bytes 6291464 | tf_op jit(solution)/shard_map/ppermute | solution.py:424
  94.1 4.1 %collective-permute-start.14 = (bf16[128,768]{1,0:T(8,128)(2,1)S(1)}, bf16[128,768]{1,0:T(8,128)(2,1)S(1)}, u32[]{:S(2)}, u32[]{:S(2)}) collective-permute-start(bf16[128,768]{1,0:T(8,128)(2,1)S(1)} %collective-permute-done.10.refs_2_), channel_id=1, source_target_pairs={{0,32},{32,0},{1,33},{33,1},{2,34},{34,2},{3,35},{35,3},{4,36},{36... | collective-permute-start | bytes 589832 | tf_op jit(solution)/shard_map/ppermute | solution.py:424
  94.6 3.9 %collective-permute-start.15 = (bf16[128,768]{1,0:T(8,128)(2,1)S(1)}, bf16[128,768]{1,0:T(8,128)(2,1)S(1)}, u32[]{:S(2)}, u32[]{:S(2)}) collective-permute-start(bf16[128,768]{1,0:T(8,128)(2,1)S(1)} %collective-permute-done.11.refs_4_), channel_id=1, source_target_pairs={{0,32},{32,0},{1,33},{33,1},{2,34},{34,2},{3,35},{35,3},{4,36},{36... | collective-permute-start | bytes 589832 | tf_op jit(solution)/shard_map/ppermute | solution.py:424
  94.6 4.1 %collective-permute-start.16 = (bf16[128,768]{1,0:T(8,128)(2,1)S(1)}, bf16[128,768]{1,0:T(8,128)(2,1)S(1)}, u32[]{:S(2)}, u32[]{:S(2)}) collective-permute-start(bf16[128,768]{1,0:T(8,128)(2,1)S(1)} %collective-permute-done.12.refs_6_), channel_id=1, source_target_pairs={{0,32},{32,0},{1,33},{33,1},{2,34},{34,2},{3,35},{35,3},{4,36},{36... | collective-permute-start | bytes 589832 | tf_op jit(solution)/shard_map/ppermute | solution.py:424
  95.1 14.7 %collective-permute-start.18 = (bf16[4,224,128]{2,1,0:T(8,128)(2,1)S(1)}, bf16[4,224,128]{2,1,0:T(8,128)(2,1)S(1)}, u32[]{:S(2)}, u32[]{:S(2)}) collective-permute-start(bf16[4,224,128]{2,1,0:T(8,128)(2,1)S(1)} %copy-done.9), channel_id=1, source_target_pairs={{0,64},{64,128},{128,192},{192,0},{1,65},{65,129},{129,193},{193,1... | collective-permute-start | bytes 688136 | tf_op jit(solution)/shard_map/ppermute | solution.py:424
  98.2 18.9 %collective-permute-start.19 = (bf16[128,3584]{1,0:T(8,128)(2,1)S(1)}, bf16[128,3584]{1,0:T(8,128)(2,1)S(1)}, u32[]{:S(2)}, u32[]{:S(2)}) collective-permute-start(bf16[128,3584]{1,0:T(8,128)(2,1)S(1)} %collective-permute-done.9.recv_ref), channel_id=1, source_target_pairs={{0,32},{32,0},{1,33},{33,1},{2,34},{34,2},{3,35},{35,3},{4,36},{36... | collective-permute-start | bytes 2752520 | tf_op jit(solution)/shard_map/ppermute | solution.py:424
  109.8 23.6 %all-to-all-start.2 = ((bf16[16,256,128]{2,1,0:T(8,128)(2,1)}), bf16[16,256,128]{2,1,0:T(8,128)(2,1)}, u32[]{:S(2)}, u32[]{:S(2)}) async-start(bf16[16,256,128]{2,1,0:T(8,128)(2,1)} %bitcast.11), calls=%async_computation.2 | async-start | bytes 2097152 | tf_op jit(solution)/shard_map/all_to_all | solution.py:477
  116.7 4.8 %collective-permute-start.20 = (bf16[3,128,128]{2,1,0:T(8,128)(2,1)S(1)}, bf16[3,128,128]{2,1,0:T(8,128)(2,1)S(1)}, u32[]{:S(2)}, u32[]{:S(2)}) collective-permute-start(bf16[3,128,128]{2,1,0:T(8,128)(2,1)S(1)} %copy-done.18), channel_id=1, source_target_pairs={{0,1},{1,0},{2,3},{3,2},{4,5},{5,4},{6,7},{7,6},{8,9},{9,8},{10,11... | collective-permute-start | bytes 294920 | tf_op jit(solution)/shard_map/ppermute | solution.py:424
  134.8 5.1 %collective-permute-start.21 = (f32[256,128]{1,0:T(8,128)S(1)}, f32[256,128]{1,0:T(8,128)S(1)}, u32[]{:S(2)}, u32[]{:S(2)}) collective-permute-start(f32[256,128]{1,0:T(8,128)S(1)} %convert_reduce_fusion), channel_id=1, source_target_pairs={{0,1},{1,0},{2,3},{3,2},{4,5},{5,4},{6,7},{7,6},{8,9},{9,8},{10,11... | collective-permute-start | bytes 393224 | tf_op jit(solution)/shard_map/ppermute | solution.py:424
  135.2 5.1 %collective-permute-start.22 = (bf16[4,224,128]{2,1,0:T(8,128)(2,1)S(1)}, bf16[4,224,128]{2,1,0:T(8,128)(2,1)S(1)}, u32[]{:S(2)}, u32[]{:S(2)}) collective-permute-start(bf16[4,224,128]{2,1,0:T(8,128)(2,1)S(1)} %collective-permute-done.18.refs_4_), channel_id=1, source_target_pairs={{0,32},{32,0},{1,33},{33,1},{2,34},{34,2},{3,35},{35,3},{4,36},{36... | collective-permute-start | bytes 688136 | tf_op jit(solution)/shard_map/ppermute | solution.py:424
  (29 other events, 383.2 us)

commit v5 on v4

--- a/solution.py
+++ b/solution.py
@@ -176,31 +176,19 @@
 
 def relay_kernel(axes, piece, width, pos_ref, ss_ref, *refs):
     nzh, nc, ny, nx, nzl = axes
-    parts, (g_mine, g_sib, own_ref, m_ref, g, pxc, sem, sem_p, saved, coef) = refs[:8], refs[8:]
+    parts, (g_mine, g_sib, own_ref, m_ref, g, pxc, saved, coef) = refs[:8], refs[8:]
     chip, core = pos_ref[0], pos_ref[1]
 
     for n in range(8):
-        section = lax.rem(chip + n // 2, nzh) * nc + (core if n % 2 == 0 else 1 - core)
-        pltpu.make_async_copy(parts[n], pxc.at[section], sem_p).start()
-    for source, c in ((g_mine, core), (g_sib, 1 - core)):
-
-        def fetch(index, _):
-            owner = lax.rem(chip + index, nzh) * nc + c
-            to = (owner * (ny * nx) + index // nzh) * piece
-            pltpu.make_async_copy(
-                source.at[pl.ds(pl.multiple_of(index * piece, 16), piece)],
-                g.at[pl.ds(pl.multiple_of(to, 16), piece)],
-                sem,
-            ).start()
-            return 0
-
-        lax.fori_loop(0, nzh * ny * nx, fetch, 0)
-    pltpu.make_async_copy(pxc, pxc, sem_p).wait()
-    pltpu.make_async_copy(g, g, sem).wait()
+        rel, c = n // 2, core if n % 2 == 0 else 1 - core
+        section = lax.rem(chip + rel, nzh) * nc + c
+        pxc[section] = parts[n][...]
+        source = g_mine if n % 2 == 0 else g_sib
+        g[section] = source[:, rel]
 
     def block(at):
-        start = (at[0] * BLOCKS + at[1]) * R
-        return g[start : start + R]
+        first = at[1] % (piece // R) * R
+        return g[at[0], at[1] // (piece // R), first : first + R]
 
     def pair(at):
         plain = jnp.concatenate([block(at[0]), block(at[1])], axis=1)
@@ -313,27 +301,24 @@
 
 def relay(axes, width, pos, ss, parts, g_mine, g_sib):
     rows = ss.shape[0]
-    total = 2 * g_mine.shape[0]
-    piece = total // (axes[0] * axes[1] * axes[2] * axes[3])
+    shape = g_mine.shape
+    total = 2 * g_mine.size // R
     vm = pl.BlockSpec(memory_space=pltpu.VMEM)
-    far = pl.BlockSpec(memory_space=pl.ANY)
     return call(
-        functools.partial(relay_kernel, axes, piece, float(width)),
-        in_specs=[pl.BlockSpec(memory_space=pltpu.SMEM), vm] + [far] * 10,
+        functools.partial(relay_kernel, axes, shape[2], float(width)),
+        in_specs=[pl.BlockSpec(memory_space=pltpu.SMEM)] + [vm] * 11,
         out_specs=[vm, vm],
         out_shape=[
             jax.ShapeDtypeStruct((3, rows, R), BF),
             jax.ShapeDtypeStruct((4 * SECTIONS, R, R), BF),
         ],
         scratch_shapes=[
-            pltpu.VMEM((total, R), BF),
+            pltpu.VMEM((SECTIONS, shape[0]) + shape[2:], BF),
             pltpu.VMEM((SECTIONS, rows, 6 * R), BF),
-            pltpu.SemaphoreType.DMA,
-            pltpu.SemaphoreType.DMA,
             pltpu.VMEM((SECTIONS, 6, rows, R), F32),
             pltpu.VMEM((SECTIONS, 6, rows, R), BF),
         ],
-        compiler_params=pltpu.CompilerParams(vmem_limit_bytes=60 * 1024 * 1024),
+        compiler_params=pltpu.CompilerParams(vmem_limit_bytes=32 * 1024 * 1024),
         cost_estimate=pl.CostEstimate(
             flops=2 * 28 * 12 * rows * R * R, bytes_accessed=total * R * 2, transcendentals=0
         ),
@@ -369,7 +354,7 @@
         in_specs=[pl.BlockSpec(memory_space=pltpu.SMEM), wide, wide, wide, wide, small, small],
         out_specs=pl.BlockSpec((part, 2 * slab + room, R), lambda i: (i, 0, 0)),
         out_shape=jax.ShapeDtypeStruct((width // slab, 2 * slab + room, R), BF),
-        compiler_params=pltpu.CompilerParams(vmem_limit_bytes=14 * 1024 * 1024),
+        compiler_params=pltpu.CompilerParams(vmem_limit_bytes=60 * 1024 * 1024),
         cost_estimate=pl.CostEstimate(
             flops=4 * rows * width * 3 * R, bytes_accessed=12 * rows * width, transcendentals=0
         ),
@@ -470,6 +455,8 @@
     opposite = shifted(prev, "zh", 1)
     parts = [projected, projected_sib] + [v for w in near[1:] for v in (w, sib(w))]
     g_sib = sib(g_mine)
+    lines = (ny * nx, nzh, -1, R)
+    g_mine, g_sib = g_mine.reshape(lines), g_sib.reshape(lines)
 
     own3, m_part = relay(axes, width, pos, ss, parts, g_mine, g_sib)
     own3, m_part, opposite = lax.optimization_barrier((own3, m_part, opposite))

time: 184 us -> 179 us (0.973)
  local copies, waits for them, and re-layouts: 11.1 us -> 8.51 us
    unnamed x56 -> x40, local copies, waits for them, and re-layouts: 6.79 us -> 3.22 us
    pallas_call x1, Pallas kernels: 2.65 us -> 5.47 us  [terms(): call(terms_kernel, grid=(steps,), in_specs=[pl.BlockSpec(memory_space=plt...]
    pallas_call x1, Pallas kernels: 10.3 us -> 7.55 us  [relay(): call(functools.partial(relay_kernel, axes, shape[2], float(width)), in_sp...]
    ppermute x23, starting transfers between devices: 22.1 us -> 24 us  [shifted(): lax.ppermute(value, axis, [(i, (i + steps) % count) for i in range(count)])]
  transfers between devices with their start and end apart: 25 -> 25, of which waited for: 15 -> 16; matrix products, arithmetic and copies ran while one was open for 1% -> 1% of each run, Pallas kernels for 12% -> 13%
where the time goes in v5:
time: 179 us; the launch traced here: 178 us
  blocking collectives  57.3 us (32%)
  waiting for transfers between devices  50.9 us (28%)
  starting transfers between devices  35.2 us (20%)
  Pallas kernels  25 us (14%)
  local copies, waits for them, and re-layouts  8.51 us (5%)
    ppermute x23, waiting for transfers between devices, shifted(): lax.ppermute(value, axis, [(i, (i + steps) % count) for i in range(count)])  41 us
    all_to_all x1, blocking collectives, on_device(): arrived = lax.all_to_all(mine, ('y', 'x'), 0, 0, tiled=True)  39.3 us
    ppermute x23, starting transfers between devices, shifted(): lax.ppermute(value, axis, [(i, (i + steps) % count) for i in range(count)])  24 us
    all_to_all x1, blocking collectives, on_device(): lax.all_to_all(partial.reshape(ny * nx, -1, R), ('y', 'x'), 0, 0, tiled=T...  17.9 us
    pallas_call x1, Pallas kernels, relay(): call(functools.partial(relay_kernel, axes, shape[2], float(width)), in_sp...  7.55 us
    pallas_call x1, Pallas kernels, project(): call(functools.partial(project_kernel, slab), grid=(steps,), in_specs=[pl...  7.13 us
    all_to_all x1, starting transfers between devices, on_device(): lax.all_to_all(m_part.reshape(ny * nx, -1, R), ('y', 'x'), 0, 0, tiled=True)  6.09 us
    pallas_call x1, Pallas kernels, terms(): call(terms_kernel, grid=(steps,), in_specs=[pl.BlockSpec(memory_space=plt...  5.47 us
  transfers between devices with their start and end apart: 25, of which 16 were waited for; matrix products, arithmetic and copies ran while one was open for 1% of the time, Pallas kernels for 13%

profile of v5, /device:TPU:2, one launch (start us, length us, event | category | flops | bytes accessed | tf_op | source)
XLA Modules:
  0.0 178.1 jit_solution(2628226288147367255)
XLA Ops:
  2.4 3.3 %collective-permute-start.1 = (bf16[4,224,128]{2,1,0:T(8,128)(2,1)S(1)}, bf16[4,224,128]{2,1,0:T(8,128)(2,1)S(1)}, u32[]{:S(2)}, u32[]{:S(2)}) collective-permute-start(bf16[4,224,128]{2,1,0:T(8,128)(2,1)S(1)} %pad_maximum_fusion.own_ref.refs_0_), channel_id=1, source_target_pairs={{0,64},{64,128},{128,192},{192,0},{1,65},{65,129},{129,193},{193,1... | collective-permute-start | bytes 688136 | tf_op jit(solution)/shard_map/ppermute | solution.py:409
  5.8 3.1 %collective-permute-start.2 = (bf16[4,224,128]{2,1,0:T(8,128)(2,1)S(1)}, bf16[4,224,128]{2,1,0:T(8,128)(2,1)S(1)}, u32[]{:S(2)}, u32[]{:S(2)}) collective-permute-start(bf16[4,224,128]{2,1,0:T(8,128)(2,1)S(1)} %pad_maximum_fusion.own_ref.refs_0_), channel_id=1, source_target_pairs={{0,192},{64,0},{128,64},{192,128},{1,193},{65,1},{129,65},{193,129... | collective-permute-start | bytes 688136 | tf_op jit(solution)/shard_map/ppermute | solution.py:409
  9.5 7.1 %shard_map.77 = (bf16[128,768]{1,0:T(8,128)(2,1)}, f32[128,128]{1,0:T(8,128)}, bf16[128,3584]{1,0:T(8,128)(2,1)}, bf16[128,3584]{1,0:T(8,128)(2,1)}, bf16[128,3584]{1,0:T(8,128)(2,1)}) custom-call(s32[5]{0:T(128)} %stack.30.pos_ref, bf16[128,7168]{1,0:T(8,128)(2,1)} %x_ref.1, bf16[128,7168]{1,0:T(8,128)(2,1)} %c_ref.1, bf16[1,7168,128]{2,1,0:T(8,128)(2,1)} %a_ref.1, ...), custom_call_target="tpu_custom_call" | custom-call | flops 1409286144 | bytes 11010048 | tf_op jit(solution)/shard_map/pallas_call | solution.py:85
  16.7 3.8 %collective-permute-done.2.next_ref.refs_2_ = bf16[4,224,128]{2,1,0:T(8,128)(2,1)S(1)} collective-permute-done((bf16[4,224,128]{2,1,0:T(8,128)(2,1)S(1)}, bf16[4,224,128]{2,1,0:T(8,128)(2,1)S(1)}, u32[]{:S(2)}, u32[]{:S(2)}) %collective-permute-start.2) | collective-permute-done | bytes 229408 | tf_op jit(solution)/shard_map/ppermute | solution.py:409
  23.3 2.7 %shard_map.78 = bf16[2048,128]{1,0:T(8,128)(2,1)} custom-call(s32[5]{0:T(128)} %stack.30.pos_ref, bf16[4,224,128]{2,1,0:T(8,128)(2,1)} %copy-done, bf16[4,224,128]{2,1,0:T(8,128)(2,1)} %copy-done.6, bf16[4,224,128]{2,1,0:T(8,128)(2,1)} %copy-done.2, bf16[4,224,128]{2,1,0:T(8,128)(2,1)} %copy-done.8, bf16[4,224,128]{2,1,0:T(8,128)(2,1)} %copy-done.4, ...), custom_call_target="tpu_custom_call" | custom-call | flops 117440512 | bytes 1376256 | tf_op jit(solution)/shard_map/pallas_call | solution.py:151
  26.0 17.9 %all_to_all.20 = bf16[16,128,128]{2,1,0:T(8,128)(2,1)S(1)} all-to-all(bf16[16,128,128]{2,1,0:T(8,128)(2,1)} %bitcast.15), channel_id=1, replica_groups=mesh['zh'=4,'c'=2,'y'=4,'x'=4,'zl'=2] {'y','x'}, dimensions={0} | all-to-all | bytes 1048576 | tf_op jit(solution)/shard_map/all_to_all | solution.py:443
  44.9 3.2 %collective-permute-done.5 = bf16[128,128]{1,0:T(8,128)(2,1)S(1)} collective-permute-done((bf16[128,128]{1,0:T(8,128)(2,1)S(1)}, bf16[128,128]{1,0:T(8,128)(2,1)S(1)}, u32[]{:S(2)}, u32[]{:S(2)}) %collective-permute-start.5) | collective-permute-done | bytes 32800 | tf_op jit(solution)/shard_map/ppermute | solution.py:409
  48.1 2.8 %collective-permute-start.6 = (bf16[128,128]{1,0:T(8,128)(2,1)S(1)}, bf16[128,128]{1,0:T(8,128)(2,1)S(1)}, u32[]{:S(2)}, u32[]{:S(2)}) collective-permute-start(bf16[128,128]{1,0:T(8,128)(2,1)S(1)} %add_convert_fusion.1), channel_id=1, source_target_pairs={{0,192},{64,0},{128,64},{192,128},{1,193},{65,1},{129,65},{193,129... | collective-permute-start | bytes 98312 | tf_op jit(solution)/shard_map/ppermute | solution.py:409
  50.9 4.5 %collective-permute-start.7 = (bf16[128,128]{1,0:T(8,128)(2,1)S(1)}, bf16[128,128]{1,0:T(8,128)(2,1)S(1)}, u32[]{:S(2)}, u32[]{:S(2)}) collective-permute-start(bf16[128,128]{1,0:T(8,128)(2,1)S(1)} %add_convert_fusion.1), channel_id=1, source_target_pairs={{0,128},{64,192},{128,0},{192,64},{1,129},{65,193},{129,1},{193,65... | collective-permute-start | bytes 98312 | tf_op jit(solution)/shard_map/ppermute | solution.py:409
  55.4 3.4 %collective-permute-done.7 = bf16[128,128]{1,0:T(8,128)(2,1)S(1)} collective-permute-done((bf16[128,128]{1,0:T(8,128)(2,1)S(1)}, bf16[128,128]{1,0:T(8,128)(2,1)S(1)}, u32[]{:S(2)}, u32[]{:S(2)}) %collective-permute-start.7) | collective-permute-done | bytes 32800 | tf_op jit(solution)/shard_map/ppermute | solution.py:409
  58.8 2.7 %collective-permute-done.8 = bf16[128,128]{1,0:T(8,128)(2,1)S(1)} collective-permute-done((bf16[128,128]{1,0:T(8,128)(2,1)S(1)}, bf16[128,128]{1,0:T(8,128)(2,1)S(1)}, u32[]{:S(2)}, u32[]{:S(2)}) %collective-permute-start.8) | collective-permute-done | bytes 32800 | tf_op jit(solution)/shard_map/ppermute | solution.py:409
  63.2 5.1 %all-to-all-start.1 = ((bf16[16,512,128]{2,1,0:T(8,128)(2,1)}), bf16[16,512,128]{2,1,0:T(8,128)(2,1)S(1)}, u32[]{:S(2)}, u32[]{:S(2)}) async-start(bf16[16,512,128]{2,1,0:T(8,128)(2,1)} %broadcast_in_dim.8), calls=%async_computation.1 | async-start | bytes 4194304 | tf_op jit(solution)/shard_map/all_to_all | solution.py:414
  68.4 2.8 %collective-permute-start.11 = (bf16[128,768]{1,0:T(8,128)(2,1)S(1)}, bf16[128,768]{1,0:T(8,128)(2,1)S(1)}, u32[]{:S(2)}, u32[]{:S(2)}) collective-permute-start(bf16[128,768]{1,0:T(8,128)(2,1)S(1)} %copy-done.12), channel_id=1, source_target_pairs={{0,128},{64,192},{128,0},{192,64},{1,129},{65,193},{129,1},{193,65... | collective-permute-start | bytes 589832 | tf_op jit(solution)/shard_map/ppermute | solution.py:409
  73.2 12.0 %collective-permute-done.10.refs_2_ = bf16[128,768]{1,0:T(8,128)(2,1)S(1)} collective-permute-done((bf16[128,768]{1,0:T(8,128)(2,1)S(1)}, bf16[128,768]{1,0:T(8,128)(2,1)S(1)}, u32[]{:S(2)}, u32[]{:S(2)}) %collective-permute-start.10) | collective-permute-done | bytes 196640 | tf_op jit(solution)/shard_map/ppermute | solution.py:409
  85.2 3.2 %collective-permute-done.12.refs_6_ = bf16[128,768]{1,0:T(8,128)(2,1)S(1)} collective-permute-done((bf16[128,768]{1,0:T(8,128)(2,1)S(1)}, bf16[128,768]{1,0:T(8,128)(2,1)S(1)}, u32[]{:S(2)}, u32[]{:S(2)}) %collective-permute-start.12) | collective-permute-done | bytes 196640 | tf_op jit(solution)/shard_map/ppermute | solution.py:409
  88.4 4.9 %all-to-all-done.1 = bf16[16,512,128]{2,1,0:T(8,128)(2,1)S(1)} async-done(((bf16[16,512,128]{2,1,0:T(8,128)(2,1)}), bf16[16,512,128]{2,1,0:T(8,128)(2,1)S(1)}, u32[]{:S(2)}, u32[]{:S(2)}) %all-to-all-start.1) | async-done | bytes 2097184 | tf_op jit(solution)/shard_map/all_to_all | solution.py:414
  94.3 3.4 %collective-permute-done.14.refs_3_ = bf16[128,768]{1,0:T(8,128)(2,1)S(1)} collective-permute-done((bf16[128,768]{1,0:T(8,128)(2,1)S(1)}, bf16[128,768]{1,0:T(8,128)(2,1)S(1)}, u32[]{:S(2)}, u32[]{:S(2)}) %collective-permute-start.14) | collective-permute-done | bytes 196640 | tf_op jit(solution)/shard_map/ppermute | solution.py:409
  99.2 7.6 %shard_map.79 = (bf16[3,128,128]{2,1,0:T(8,128)(2,1)S(1)}, bf16[32,128,128]{2,1,0:T(8,128)(2,1)}) custom-call(s32[5]{0:T(128)S(1)} %copy-done.16, f32[128,128]{1,0:T(8,128)S(1)} %copy-done.15, bf16[128,768]{1,0:T(8,128)(2,1)S(1)} %copy-done.12, bf16[128,768]{1,0:T(8,128)(2,1)S(1)} %collective-permute-done.13.refs_1_, ...), custom_call_target="tpu_custom_call" | custom-call | flops 1409286144 | bytes 4194304 | tf_op jit(solution)/shard_map/pallas_call | solution.py:307
  108.1 6.1 %all-to-all-start.2 = ((bf16[16,256,128]{2,1,0:T(8,128)(2,1)}), bf16[16,256,128]{2,1,0:T(8,128)(2,1)S(1)}, u32[]{:S(2)}, u32[]{:S(2)}) async-start(bf16[16,256,128]{2,1,0:T(8,128)(2,1)} %bitcast.9), calls=%async_computation.2 | async-start | bytes 2097152 | tf_op jit(solution)/shard_map/all_to_all | solution.py:464
  116.0 2.9 %collective-permute-done.20.far_ref = bf16[3,128,128]{2,1,0:T(8,128)(2,1)S(1)} collective-permute-done((bf16[3,128,128]{2,1,0:T(8,128)(2,1)S(1)}, bf16[3,128,128]{2,1,0:T(8,128)(2,1)S(1)}, u32[]{:S(2)}, u32[]{:S(2)}) %collective-permute-start.20) | collective-permute-done | bytes 98336 | tf_op jit(solution)/shard_map/ppermute | solution.py:409
  119.5 5.5 %shard_map.80 = bf16[16,704,128]{2,1,0:T(8,128)(2,1)} custom-call(s32[5]{0:T(128)} %stack.30.pos_ref, bf16[128,3584]{1,0:T(8,128)(2,1)} %get-tuple-element.51.x_ref, bf16[128,3584]{1,0:T(8,128)(2,1)} %get-tuple-element.52.c_ref, bf16[128,3584]{1,0:T(8,128)(2,1)} %copy-done.18, bf16[128,3584]{1,0:T(8,128)(2,1)} %collective-permute-done.19.sib_ref, ...), custom_call_target="tpu_custom_call" | custom-call | flops 704643072 | bytes 5505024 | tf_op jit(solution)/shard_map/pallas_call | solution.py:351
  125.0 5.1 %all-to-all-done.2 = bf16[16,256,128]{2,1,0:T(8,128)(2,1)S(1)} async-done(((bf16[16,256,128]{2,1,0:T(8,128)(2,1)}), bf16[16,256,128]{2,1,0:T(8,128)(2,1)S(1)}, u32[]{:S(2)}, u32[]{:S(2)}) %all-to-all-start.2) | async-done | bytes 1048608 | tf_op jit(solution)/shard_map/all_to_all | solution.py:464
  131.3 4.0 %collective-permute-done.21 = f32[256,128]{1,0:T(8,128)S(1)} collective-permute-done((f32[256,128]{1,0:T(8,128)S(1)}, f32[256,128]{1,0:T(8,128)S(1)}, u32[]{:S(2)}, u32[]{:S(2)}) %collective-permute-start.21) | collective-permute-done | bytes 131104 | tf_op jit(solution)/shard_map/ppermute | solution.py:409
  136.6 39.3 %all_to_all.21.all_ref = bf16[16,704,128]{2,1,0:T(8,128)(2,1)S(1)} all-to-all(bf16[16,704,128]{2,1,0:T(8,128)(2,1)} %broadcast_dynamic-update-slice_fusion), channel_id=1, replica_groups=mesh['zh'=4,'c'=2,'y'=4,'x'=4,'zl'=2] {'y','x'}, dimensions={0} | all-to-all | bytes 5767168 | tf_op jit(solution)/shard_map/all_to_all | solution.py:474
  (84 shorter events, 20.9 us)
Async XLA Ops:
  2.4 14.2 %collective-permute-start.1 = (bf16[4,224,128]{2,1,0:T(8,128)(2,1)S(1)}, bf16[4,224,128]{2,1,0:T(8,128)(2,1)S(1)}, u32[]{:S(2)}, u32[]{:S(2)}) collective-permute-start(bf16[4,224,128]{2,1,0:T(8,128)(2,1)S(1)} %pad_maximum_fusion.own_ref.refs_0_), channel_id=1, source_target_pairs={{0,64},{64,128},{128,192},{192,0},{1,65},{65,129},{129,193},{193,1... | collective-permute-start | bytes 688136 | tf_op jit(solution)/shard_map/ppermute | solution.py:409
  5.8 14.7 %collective-permute-start.2 = (bf16[4,224,128]{2,1,0:T(8,128)(2,1)S(1)}, bf16[4,224,128]{2,1,0:T(8,128)(2,1)S(1)}, u32[]{:S(2)}, u32[]{:S(2)}) collective-permute-start(bf16[4,224,128]{2,1,0:T(8,128)(2,1)S(1)} %pad_maximum_fusion.own_ref.refs_0_), channel_id=1, source_target_pairs={{0,192},{64,0},{128,64},{192,128},{1,193},{65,1},{129,65},{193,129... | collective-permute-start | bytes 688136 | tf_op jit(solution)/shard_map/ppermute | solution.py:409
  8.9 12.1 %collective-permute-start = (bf16[4,224,128]{2,1,0:T(8,128)(2,1)S(1)}, bf16[4,224,128]{2,1,0:T(8,128)(2,1)S(1)}, u32[]{:S(2)}, u32[]{:S(2)}) collective-permute-start(bf16[4,224,128]{2,1,0:T(8,128)(2,1)S(1)} %pad_maximum_fusion.own_ref.refs_0_), channel_id=1, source_target_pairs={{0,32},{32,0},{1,33},{33,1},{2,34},{34,2},{3,35},{35,3},{4,36},{36... | collective-permute-start | bytes 688136 | tf_op jit(solution)/shard_map/ppermute | solution.py:409
  20.5 1.8 %collective-permute-start.4 = (bf16[4,224,128]{2,1,0:T(8,128)(2,1)S(1)}, bf16[4,224,128]{2,1,0:T(8,128)(2,1)S(1)}, u32[]{:S(2)}, u32[]{:S(2)}) collective-permute-start(bf16[4,224,128]{2,1,0:T(8,128)(2,1)S(1)} %collective-permute-done.2.next_ref.refs_2_), channel_id=1, source_target_pairs={{0,32},{32,0},{1,33},{33,1},{2,34},{34,2},{3,35},{35,3},{4,36},{36... | collective-permute-start | bytes 688136 | tf_op jit(solution)/shard_map/ppermute | solution.py:409
  21.0 40.5 %collective-permute-start.9 = (bf16[128,3584]{1,0:T(8,128)(2,1)}, bf16[128,3584]{1,0:T(8,128)(2,1)S(1)}, u32[]{:S(2)}, u32[]{:S(2)}) collective-permute-start(bf16[128,3584]{1,0:T(8,128)(2,1)} %get-tuple-element.40), channel_id=1, source_target_pairs={{0,1},{1,0},{2,3},{3,2},{4,5},{5,4},{6,7},{7,6},{8,9},{9,8},{10,11... | collective-permute-start | bytes 2752520 | tf_op jit(solution)/shard_map/ppermute | solution.py:409
  44.1 4.0 %collective-permute-start.5 = (bf16[128,128]{1,0:T(8,128)(2,1)S(1)}, bf16[128,128]{1,0:T(8,128)(2,1)S(1)}, u32[]{:S(2)}, u32[]{:S(2)}) collective-permute-start(bf16[128,128]{1,0:T(8,128)(2,1)S(1)} %reduce_sum.21), channel_id=1, source_target_pairs={{0,1},{1,0},{2,3},{3,2},{4,5},{5,4},{6,7},{7,6},{8,9},{9,8},{10,11... | collective-permute-start | bytes 98312 | tf_op jit(solution)/shard_map/ppermute | solution.py:409
  48.1 7.3 %collective-permute-start.6 = (bf16[128,128]{1,0:T(8,128)(2,1)S(1)}, bf16[128,128]{1,0:T(8,128)(2,1)S(1)}, u32[]{:S(2)}, u32[]{:S(2)}) collective-permute-start(bf16[128,128]{1,0:T(8,128)(2,1)S(1)} %add_convert_fusion.1), channel_id=1, source_target_pairs={{0,192},{64,0},{128,64},{192,128},{1,193},{65,1},{129,65},{193,129... | collective-permute-start | bytes 98312 | tf_op jit(solution)/shard_map/ppermute | solution.py:409
  50.9 7.8 %collective-permute-start.7 = (bf16[128,128]{1,0:T(8,128)(2,1)S(1)}, bf16[128,128]{1,0:T(8,128)(2,1)S(1)}, u32[]{:S(2)}, u32[]{:S(2)}) collective-permute-start(bf16[128,128]{1,0:T(8,128)(2,1)S(1)} %add_convert_fusion.1), channel_id=1, source_target_pairs={{0,128},{64,192},{128,0},{192,64},{1,129},{65,193},{129,1},{193,65... | collective-permute-start | bytes 98312 | tf_op jit(solution)/shard_map/ppermute | solution.py:409
  55.4 6.0 %collective-permute-start.8 = (bf16[128,128]{1,0:T(8,128)(2,1)S(1)}, bf16[128,128]{1,0:T(8,128)(2,1)S(1)}, u32[]{:S(2)}, u32[]{:S(2)}) collective-permute-start(bf16[128,128]{1,0:T(8,128)(2,1)S(1)} %add_convert_fusion.1), channel_id=1, source_target_pairs={{0,64},{64,128},{128,192},{192,0},{1,65},{65,129},{129,193},{193,1... | collective-permute-start | bytes 98312 | tf_op jit(solution)/shard_map/ppermute | solution.py:409
  63.2 30.1 %all-to-all-start.1 = ((bf16[16,512,128]{2,1,0:T(8,128)(2,1)}), bf16[16,512,128]{2,1,0:T(8,128)(2,1)S(1)}, u32[]{:S(2)}, u32[]{:S(2)}) async-start(bf16[16,512,128]{2,1,0:T(8,128)(2,1)} %broadcast_in_dim.8), calls=%async_computation.1 | async-start | bytes 4194304 | tf_op jit(solution)/shard_map/all_to_all | solution.py:414
  68.3 16.9 %collective-permute-start.10 = (bf16[128,768]{1,0:T(8,128)(2,1)S(1)}, bf16[128,768]{1,0:T(8,128)(2,1)S(1)}, u32[]{:S(2)}, u32[]{:S(2)}) collective-permute-start(bf16[128,768]{1,0:T(8,128)(2,1)S(1)} %copy-done.12), channel_id=1, source_target_pairs={{0,192},{64,0},{128,64},{192,128},{1,193},{65,1},{129,65},{193,129... | collective-permute-start | bytes 589832 | tf_op jit(solution)/shard_map/ppermute | solution.py:409
  68.4 16.8 %collective-permute-start.11 = (bf16[128,768]{1,0:T(8,128)(2,1)S(1)}, bf16[128,768]{1,0:T(8,128)(2,1)S(1)}, u32[]{:S(2)}, u32[]{:S(2)}) collective-permute-start(bf16[128,768]{1,0:T(8,128)(2,1)S(1)} %copy-done.12), channel_id=1, source_target_pairs={{0,128},{64,192},{128,0},{192,64},{1,129},{65,193},{129,1},{193,65... | collective-permute-start | bytes 589832 | tf_op jit(solution)/shard_map/ppermute | solution.py:409
  71.2 17.2 %collective-permute-start.12 = (bf16[128,768]{1,0:T(8,128)(2,1)S(1)}, bf16[128,768]{1,0:T(8,128)(2,1)S(1)}, u32[]{:S(2)}, u32[]{:S(2)}) collective-permute-start(bf16[128,768]{1,0:T(8,128)(2,1)S(1)} %copy-done.12), channel_id=1, source_target_pairs={{0,64},{64,128},{128,192},{192,0},{1,65},{65,129},{129,193},{193,1... | collective-permute-start | bytes 589832 | tf_op jit(solution)/shard_map/ppermute | solution.py:409
  73.2 15.2 %collective-permute-start.13 = (bf16[128,768]{1,0:T(8,128)(2,1)S(1)}, bf16[128,768]{1,0:T(8,128)(2,1)S(1)}, u32[]{:S(2)}, u32[]{:S(2)}) collective-permute-start(bf16[128,768]{1,0:T(8,128)(2,1)S(1)} %copy-done.12), channel_id=1, source_target_pairs={{0,32},{32,0},{1,33},{33,1},{2,34},{34,2},{3,35},{35,3},{4,36},{36... | collective-permute-start | bytes 589832 | tf_op jit(solution)/shard_map/ppermute | solution.py:409
  93.3 5.0 %collective-permute-start.17 = (bf16[8192,128]{1,0:T(8,128)(2,1)S(1)}, bf16[8192,128]{1,0:T(8,128)(2,1)S(1)}, u32[]{:S(2)}, u32[]{:S(2)}) collective-permute-start(bf16[8192,128]{1,0:T(8,128)(2,1)S(1)} %bitcast.12), channel_id=1, source_target_pairs={{0,32},{32,0},{1,33},{33,1},{2,34},{34,2},{3,35},{35,3},{4,36},{36... | collective-permute-start | bytes 6291464 | tf_op jit(solution)/shard_map/ppermute | solution.py:409
  93.3 4.4 %collective-permute-start.14 = (bf16[128,768]{1,0:T(8,128)(2,1)S(1)}, bf16[128,768]{1,0:T(8,128)(2,1)S(1)}, u32[]{:S(2)}, u32[]{:S(2)}) collective-permute-start(bf16[128,768]{1,0:T(8,128)(2,1)S(1)} %collective-permute-done.10.refs_2_), channel_id=1, source_target_pairs={{0,32},{32,0},{1,33},{33,1},{2,34},{34,2},{3,35},{35,3},{4,36},{36... | collective-permute-start | bytes 589832 | tf_op jit(solution)/shard_map/ppermute | solution.py:409
  93.8 4.2 %collective-permute-start.15 = (bf16[128,768]{1,0:T(8,128)(2,1)S(1)}, bf16[128,768]{1,0:T(8,128)(2,1)S(1)}, u32[]{:S(2)}, u32[]{:S(2)}) collective-permute-start(bf16[128,768]{1,0:T(8,128)(2,1)S(1)} %collective-permute-done.11.refs_4_), channel_id=1, source_target_pairs={{0,32},{32,0},{1,33},{33,1},{2,34},{34,2},{3,35},{35,3},{4,36},{36... | collective-permute-start | bytes 589832 | tf_op jit(solution)/shard_map/ppermute | solution.py:409
  93.8 4.5 %collective-permute-start.16 = (bf16[128,768]{1,0:T(8,128)(2,1)S(1)}, bf16[128,768]{1,0:T(8,128)(2,1)S(1)}, u32[]{:S(2)}, u32[]{:S(2)}) collective-permute-start(bf16[128,768]{1,0:T(8,128)(2,1)S(1)} %collective-permute-done.12.refs_6_), channel_id=1, source_target_pairs={{0,32},{32,0},{1,33},{33,1},{2,34},{34,2},{3,35},{35,3},{4,36},{36... | collective-permute-start | bytes 589832 | tf_op jit(solution)/shard_map/ppermute | solution.py:409
  94.3 13.8 %collective-permute-start.18 = (bf16[4,224,128]{2,1,0:T(8,128)(2,1)S(1)}, bf16[4,224,128]{2,1,0:T(8,128)(2,1)S(1)}, u32[]{:S(2)}, u32[]{:S(2)}) collective-permute-start(bf16[4,224,128]{2,1,0:T(8,128)(2,1)S(1)} %copy-done.3), channel_id=1, source_target_pairs={{0,64},{64,128},{128,192},{192,0},{1,65},{65,129},{129,193},{193,1... | collective-permute-start | bytes 688136 | tf_op jit(solution)/shard_map/ppermute | solution.py:409
  97.8 18.2 %collective-permute-start.19 = (bf16[128,3584]{1,0:T(8,128)(2,1)}, bf16[128,3584]{1,0:T(8,128)(2,1)}, u32[]{:S(2)}, u32[]{:S(2)}) collective-permute-start(bf16[128,3584]{1,0:T(8,128)(2,1)} %copy-done.18), channel_id=1, source_target_pairs={{0,32},{32,0},{1,33},{33,1},{2,34},{34,2},{3,35},{35,3},{4,36},{36... | collective-permute-start | bytes 2752520 | tf_op jit(solution)/shard_map/ppermute | solution.py:409
  108.1 22.0 %all-to-all-start.2 = ((bf16[16,256,128]{2,1,0:T(8,128)(2,1)}), bf16[16,256,128]{2,1,0:T(8,128)(2,1)S(1)}, u32[]{:S(2)}, u32[]{:S(2)}) async-start(bf16[16,256,128]{2,1,0:T(8,128)(2,1)} %bitcast.9), calls=%async_computation.2 | async-start | bytes 2097152 | tf_op jit(solution)/shard_map/all_to_all | solution.py:464
  114.2 4.7 %collective-permute-start.20 = (bf16[3,128,128]{2,1,0:T(8,128)(2,1)S(1)}, bf16[3,128,128]{2,1,0:T(8,128)(2,1)S(1)}, u32[]{:S(2)}, u32[]{:S(2)}) collective-permute-start(bf16[3,128,128]{2,1,0:T(8,128)(2,1)S(1)} %copy-done.14), channel_id=1, source_target_pairs={{0,1},{1,0},{2,3},{3,2},{4,5},{5,4},{6,7},{7,6},{8,9},{9,8},{10,11... | collective-permute-start | bytes 294920 | tf_op jit(solution)/shard_map/ppermute | solution.py:409
  130.2 5.1 %collective-permute-start.21 = (f32[256,128]{1,0:T(8,128)S(1)}, f32[256,128]{1,0:T(8,128)S(1)}, u32[]{:S(2)}, u32[]{:S(2)}) collective-permute-start(f32[256,128]{1,0:T(8,128)S(1)} %convert_reduce_fusion), channel_id=1, source_target_pairs={{0,1},{1,0},{2,3},{3,2},{4,5},{5,4},{6,7},{7,6},{8,9},{9,8},{10,11... | collective-permute-start | bytes 393224 | tf_op jit(solution)/shard_map/ppermute | solution.py:409
  131.3 5.2 %collective-permute-start.22 = (bf16[4,224,128]{2,1,0:T(8,128)(2,1)S(1)}, bf16[4,224,128]{2,1,0:T(8,128)(2,1)S(1)}, u32[]{:S(2)}, u32[]{:S(2)}) collective-permute-start(bf16[4,224,128]{2,1,0:T(8,128)(2,1)S(1)} %collective-permute-done.18.refs_4_), channel_id=1, source_target_pairs={{0,32},{32,0},{1,33},{33,1},{2,34},{34,2},{3,35},{35,3},{4,36},{36... | collective-permute-start | bytes 688136 | tf_op jit(solution)/shard_map/ppermute | solution.py:409
  (21 other events, 343.5 us)

commit v6 on v5

--- a/solution.py
+++ b/solution.py
@@ -111,6 +111,26 @@
     )(pos, x, c, a, p, b, q)
 
 
+def slice_kernel(dp_ref, *refs):
+    for n in range(4):
+        refs[4][n] = refs[n][0]
+
+
+def own_slices(dp, slab, *weights):
+    block = pl.BlockSpec((1, slab, R), lambda i, dp: (0, dp[0], 0))
+    return call(
+        slice_kernel,
+        grid_spec=pltpu.PrefetchScalarGridSpec(
+            num_scalar_prefetch=1,
+            grid=(1,),
+            in_specs=[block] * 4,
+            out_specs=pl.BlockSpec((4, slab, R), lambda i, dp: (0, 0, 0)),
+        ),
+        out_shape=jax.ShapeDtypeStruct((4, slab, R), BF),
+        compiler_params=pltpu.CompilerParams(vmem_limit_bytes=60 * 1024 * 1024),
+    )(dp, *weights)
+
+
 def gram_kernel(pos_ref, own_ref, own_sib_ref, prev_ref, prev_sib_ref, next_ref, next_sib_ref, out_ref):
     chip, core = pos_ref[0], pos_ref[1]
 
@@ -118,8 +138,8 @@
         return jnp.concatenate([value[n] for n in names], axis=1)
 
     def four(low, high):
-        from_b = mm_tn(low[2], cols(high, (0, 2, 1, 3)))
-        from_q = mm_tn(low[3], cols(high, (0, 2)))
+        full = mm_tn(cols(low, (2, 3)), cols(high, (0, 2, 1, 3)))
+        from_b, from_q = full[:R], full[R:, : 2 * R]
         mixed = from_b[:, 2 * R :] + from_q
         return [from_b[:, :R], from_b[:, R : 2 * R], mixed[:, :R], mixed[:, R:]]
 
@@ -142,9 +162,9 @@
     pair = four(jnp.where(first, own, own_sib), jnp.where(first, own_sib, own))
     for i in range(2):
         put(12 + i, jnp.where(first, pair[i], pair[2 + i]))
-    self_b = mm_tn(own[2], cols(own, (2, 3)))
-    put(14, self_b[:, :R])
-    put(15, self_b[:, R:] + mm_tn(own[3], own[2]))
+    self_pair = mm_tn(cols(own, (2, 3)), cols(own, (2, 3)))
+    put(14, self_pair[:R, :R])
+    put(15, self_pair[:R, R:] + self_pair[R:, :R])
 
 
 def gram(pos, *slices):
@@ -423,12 +443,7 @@
     dp = lax.axis_index(DP)
     sib = lambda w: shifted(w, "c", 1)
 
-    own = jnp.stack(
-        [
-            lax.dynamic_slice_in_dim(w[0], dp * slab, slab, 0)
-            for w in (adapt_in, probe_in, adapt_out, probe_out)
-        ]
-    )
+    own = own_slices(dp.astype(jnp.int32).reshape(1), slab, adapt_in, probe_in, adapt_out, probe_out)
     prev, after = shifted(own, "zh", 1), shifted(own, "zh", -1)
     own_sib = sib(own)
     projected, ss, keep_x, keep_c, send = project(

time: 179 us -> 179 us (level)
  no operation moved by 1% of the time
where the time goes in v6:
time: 179 us; the launch traced here: 178 us
  blocking collectives  57.3 us (32%)
  waiting for transfers between devices  51.4 us (29%)
  starting transfers between devices  35 us (20%)
  Pallas kernels  26.7 us (15%)
  local copies, waits for them, and re-layouts  6.88 us (4%)
    ppermute x23, waiting for transfers between devices, shifted(): lax.ppermute(value, axis, [(i, (i + steps) % count) for i in range(count)])  41 us
    all_to_all x1, blocking collectives, on_device(): arrived = lax.all_to_all(mine, ('y', 'x'), 0, 0, tiled=True)  39.4 us
    ppermute x23, starting transfers between devices, shifted(): lax.ppermute(value, axis, [(i, (i + steps) % count) for i in range(count)])  23.6 us
    all_to_all x1, blocking collectives, on_device(): lax.all_to_all(partial.reshape(ny * nx, -1, R), ('y', 'x'), 0, 0, tiled=T...  17.9 us
    pallas_call x1, Pallas kernels, relay(): call(functools.partial(relay_kernel, axes, shape[2], float(width)), in_sp...  7.55 us
    pallas_call x1, Pallas kernels, project(): call(functools.partial(project_kernel, slab), grid=(steps,), in_specs=[pl...  7.16 us
    all_to_all x1, starting transfers between devices, on_device(): lax.all_to_all(m_part.reshape(ny * nx, -1, R), ('y', 'x'), 0, 0, tiled=True)  6.22 us
    pallas_call x1, Pallas kernels, terms(): call(terms_kernel, grid=(steps,), in_specs=[pl.BlockSpec(memory_space=plt...  5.48 us
  transfers between devices with their start and end apart: 25, of which 16 were waited for; matrix products, arithmetic and copies ran while one was open for 1% of the time, Pallas kernels for 13%

profile of v6, /device:TPU:2, one launch (start us, length us, event | category | flops | bytes accessed | tf_op | source)
XLA Modules:
  0.0 178.3 jit_solution(12665975455120569022)
XLA Ops:
  2.3 3.3 %collective-permute-start.1 = (bf16[4,224,128]{2,1,0:T(8,128)(2,1)}, bf16[4,224,128]{2,1,0:T(8,128)(2,1)S(1)}, u32[]{:S(2)}, u32[]{:S(2)}) collective-permute-start(bf16[4,224,128]{2,1,0:T(8,128)(2,1)} %shard_map.78.own_ref.refs_0_), channel_id=1, source_target_pairs={{0,64},{64,128},{128,192},{192,0},{1,65},{65,129},{129,193},{193,1... | collective-permute-start | bytes 688136 | tf_op jit(solution)/shard_map/ppermute | solution.py:429
  5.6 3.0 %collective-permute-start.2 = (bf16[4,224,128]{2,1,0:T(8,128)(2,1)}, bf16[4,224,128]{2,1,0:T(8,128)(2,1)S(1)}, u32[]{:S(2)}, u32[]{:S(2)}) collective-permute-start(bf16[4,224,128]{2,1,0:T(8,128)(2,1)} %shard_map.78.own_ref.refs_0_), channel_id=1, source_target_pairs={{0,192},{64,0},{128,64},{192,128},{1,193},{65,1},{129,65},{193,129... | collective-permute-start | bytes 688136 | tf_op jit(solution)/shard_map/ppermute | solution.py:429
  9.3 7.2 %shard_map.77 = (bf16[128,768]{1,0:T(8,128)(2,1)}, f32[128,128]{1,0:T(8,128)}, bf16[128,3584]{1,0:T(8,128)(2,1)}, bf16[128,3584]{1,0:T(8,128)(2,1)}, bf16[128,3584]{1,0:T(8,128)(2,1)}) custom-call(s32[5]{0:T(128)} %stack.23.pos_ref, bf16[128,7168]{1,0:T(8,128)(2,1)} %x_ref.1, bf16[128,7168]{1,0:T(8,128)(2,1)} %c_ref.1, bf16[1,7168,128]{2,1,0:T(8,128)(2,1)} %refs_0_.1, ...), custom_call_target="tpu_custom_call" | custom-call | flops 1409286144 | bytes 11010048 | tf_op jit(solution)/shard_map/pallas_call | solution.py:85
  16.4 4.1 %collective-permute-done.2.next_ref.refs_2_ = bf16[4,224,128]{2,1,0:T(8,128)(2,1)S(1)} collective-permute-done((bf16[4,224,128]{2,1,0:T(8,128)(2,1)}, bf16[4,224,128]{2,1,0:T(8,128)(2,1)S(1)}, u32[]{:S(2)}, u32[]{:S(2)}) %collective-permute-start.2) | collective-permute-done | bytes 229408 | tf_op jit(solution)/shard_map/ppermute | solution.py:429
  23.4 2.7 %shard_map.79 = bf16[2048,128]{1,0:T(8,128)(2,1)} custom-call(s32[5]{0:T(128)} %stack.23.pos_ref, bf16[4,224,128]{2,1,0:T(8,128)(2,1)} %shard_map.78.own_ref.refs_0_, bf16[4,224,128]{2,1,0:T(8,128)(2,1)} %copy-done.5, bf16[4,224,128]{2,1,0:T(8,128)(2,1)} %copy-done.1, bf16[4,224,128]{2,1,0:T(8,128)(2,1)} %copy-done.7, bf16[4,224,128]{2,1,0:T(8,128)(2,1)} %copy-done.3, ...), custom_call_target="tpu_custom_call" | custom-call | flops 117440512 | bytes 1376256 | tf_op jit(solution)/shard_map/pallas_call | solution.py:171
  26.1 17.9 %all_to_all.20 = bf16[16,128,128]{2,1,0:T(8,128)(2,1)S(1)} all-to-all(bf16[16,128,128]{2,1,0:T(8,128)(2,1)} %bitcast.16), channel_id=1, replica_groups=mesh['zh'=4,'c'=2,'y'=4,'x'=4,'zl'=2] {'y','x'}, dimensions={0} | all-to-all | bytes 1048576 | tf_op jit(solution)/shard_map/all_to_all | solution.py:458
  45.0 3.2 %collective-permute-done.5 = bf16[128,128]{1,0:T(8,128)(2,1)S(1)} collective-permute-done((bf16[128,128]{1,0:T(8,128)(2,1)S(1)}, bf16[128,128]{1,0:T(8,128)(2,1)S(1)}, u32[]{:S(2)}, u32[]{:S(2)}) %collective-permute-start.5) | collective-permute-done | bytes 32800 | tf_op jit(solution)/shard_map/ppermute | solution.py:429
  48.2 2.7 %collective-permute-start.6 = (bf16[128,128]{1,0:T(8,128)(2,1)S(1)}, bf16[128,128]{1,0:T(8,128)(2,1)S(1)}, u32[]{:S(2)}, u32[]{:S(2)}) collective-permute-start(bf16[128,128]{1,0:T(8,128)(2,1)S(1)} %add_convert_fusion.1), channel_id=1, source_target_pairs={{0,192},{64,0},{128,64},{192,128},{1,193},{65,1},{129,65},{193,129... | collective-permute-start | bytes 98312 | tf_op jit(solution)/shard_map/ppermute | solution.py:429
  50.9 4.6 %collective-permute-start.7 = (bf16[128,128]{1,0:T(8,128)(2,1)S(1)}, bf16[128,128]{1,0:T(8,128)(2,1)S(1)}, u32[]{:S(2)}, u32[]{:S(2)}) collective-permute-start(bf16[128,128]{1,0:T(8,128)(2,1)S(1)} %add_convert_fusion.1), channel_id=1, source_target_pairs={{0,128},{64,192},{128,0},{192,64},{1,129},{65,193},{129,1},{193,65... | collective-permute-start | bytes 98312 | tf_op jit(solution)/shard_map/ppermute | solution.py:429
  55.5 3.3 %collective-permute-done.7 = bf16[128,128]{1,0:T(8,128)(2,1)S(1)} collective-permute-done((bf16[128,128]{1,0:T(8,128)(2,1)S(1)}, bf16[128,128]{1,0:T(8,128)(2,1)S(1)}, u32[]{:S(2)}, u32[]{:S(2)}) %collective-permute-start.7) | collective-permute-done | bytes 32800 | tf_op jit(solution)/shard_map/ppermute | solution.py:429
  58.7 2.8 %collective-permute-done.8 = bf16[128,128]{1,0:T(8,128)(2,1)S(1)} collective-permute-done((bf16[128,128]{1,0:T(8,128)(2,1)S(1)}, bf16[128,128]{1,0:T(8,128)(2,1)S(1)}, u32[]{:S(2)}, u32[]{:S(2)}) %collective-permute-start.8) | collective-permute-done | bytes 32800 | tf_op jit(solution)/shard_map/ppermute | solution.py:429
  63.3 5.1 %all-to-all-start.1 = ((bf16[16,512,128]{2,1,0:T(8,128)(2,1)}), bf16[16,512,128]{2,1,0:T(8,128)(2,1)S(1)}, u32[]{:S(2)}, u32[]{:S(2)}) async-start(bf16[16,512,128]{2,1,0:T(8,128)(2,1)} %broadcast_in_dim.8), calls=%async_computation.1 | async-start | bytes 4194304 | tf_op jit(solution)/shard_map/all_to_all | solution.py:434
  68.5 2.8 %collective-permute-start.11 = (bf16[128,768]{1,0:T(8,128)(2,1)S(1)}, bf16[128,768]{1,0:T(8,128)(2,1)S(1)}, u32[]{:S(2)}, u32[]{:S(2)}) collective-permute-start(bf16[128,768]{1,0:T(8,128)(2,1)S(1)} %copy-done.11), channel_id=1, source_target_pairs={{0,128},{64,192},{128,0},{192,64},{1,129},{65,193},{129,1},{193,65... | collective-permute-start | bytes 589832 | tf_op jit(solution)/shard_map/ppermute | solution.py:429
  73.3 12.0 %collective-permute-done.10.refs_2_ = bf16[128,768]{1,0:T(8,128)(2,1)S(1)} collective-permute-done((bf16[128,768]{1,0:T(8,128)(2,1)S(1)}, bf16[128,768]{1,0:T(8,128)(2,1)S(1)}, u32[]{:S(2)}, u32[]{:S(2)}) %collective-permute-start.10) | collective-permute-done | bytes 196640 | tf_op jit(solution)/shard_map/ppermute | solution.py:429
  85.3 2.7 %collective-permute-done.12.refs_6_ = bf16[128,768]{1,0:T(8,128)(2,1)S(1)} collective-permute-done((bf16[128,768]{1,0:T(8,128)(2,1)S(1)}, bf16[128,768]{1,0:T(8,128)(2,1)S(1)}, u32[]{:S(2)}, u32[]{:S(2)}) %collective-permute-start.12) | collective-permute-done | bytes 196640 | tf_op jit(solution)/shard_map/ppermute | solution.py:429
  88.0 5.3 %all-to-all-done.1 = bf16[16,512,128]{2,1,0:T(8,128)(2,1)S(1)} async-done(((bf16[16,512,128]{2,1,0:T(8,128)(2,1)}), bf16[16,512,128]{2,1,0:T(8,128)(2,1)S(1)}, u32[]{:S(2)}, u32[]{:S(2)}) %all-to-all-start.1) | async-done | bytes 2097184 | tf_op jit(solution)/shard_map/all_to_all | solution.py:434
  94.4 3.4 %collective-permute-done.14.refs_3_ = bf16[128,768]{1,0:T(8,128)(2,1)S(1)} collective-permute-done((bf16[128,768]{1,0:T(8,128)(2,1)S(1)}, bf16[128,768]{1,0:T(8,128)(2,1)S(1)}, u32[]{:S(2)}, u32[]{:S(2)}) %collective-permute-start.14) | collective-permute-done | bytes 196640 | tf_op jit(solution)/shard_map/ppermute | solution.py:429
  99.2 7.5 %shard_map.80 = (bf16[3,128,128]{2,1,0:T(8,128)(2,1)S(1)}, bf16[32,128,128]{2,1,0:T(8,128)(2,1)}) custom-call(s32[5]{0:T(128)S(1)} %copy-done.15, f32[128,128]{1,0:T(8,128)S(1)} %copy-done.14, bf16[128,768]{1,0:T(8,128)(2,1)S(1)} %copy-done.11, bf16[128,768]{1,0:T(8,128)(2,1)S(1)} %collective-permute-done.13.refs_1_, ...), custom_call_target="tpu_custom_call" | custom-call | flops 1409286144 | bytes 4194304 | tf_op jit(solution)/shard_map/pallas_call | solution.py:327
  108.2 6.2 %all-to-all-start.2 = ((bf16[16,256,128]{2,1,0:T(8,128)(2,1)}), bf16[16,256,128]{2,1,0:T(8,128)(2,1)S(1)}, u32[]{:S(2)}, u32[]{:S(2)}) async-start(bf16[16,256,128]{2,1,0:T(8,128)(2,1)} %bitcast.10), calls=%async_computation.2 | async-start | bytes 2097152 | tf_op jit(solution)/shard_map/all_to_all | solution.py:479
  116.1 3.1 %collective-permute-done.20.far_ref = bf16[3,128,128]{2,1,0:T(8,128)(2,1)S(1)} collective-permute-done((bf16[3,128,128]{2,1,0:T(8,128)(2,1)S(1)}, bf16[3,128,128]{2,1,0:T(8,128)(2,1)S(1)}, u32[]{:S(2)}, u32[]{:S(2)}) %collective-permute-start.20) | collective-permute-done | bytes 98336 | tf_op jit(solution)/shard_map/ppermute | solution.py:429
  119.8 5.5 %shard_map.81 = bf16[16,704,128]{2,1,0:T(8,128)(2,1)} custom-call(s32[5]{0:T(128)} %stack.23.pos_ref, bf16[128,3584]{1,0:T(8,128)(2,1)} %get-tuple-element.51.x_ref, bf16[128,3584]{1,0:T(8,128)(2,1)} %get-tuple-element.52.c_ref, bf16[128,3584]{1,0:T(8,128)(2,1)} %copy-done.17, bf16[128,3584]{1,0:T(8,128)(2,1)} %collective-permute-done.19.sib_ref, ...), custom_call_target="tpu_custom_call" | custom-call | flops 704643072 | bytes 5505024 | tf_op jit(solution)/shard_map/pallas_call | solution.py:371
  125.2 5.0 %all-to-all-done.2 = bf16[16,256,128]{2,1,0:T(8,128)(2,1)S(1)} async-done(((bf16[16,256,128]{2,1,0:T(8,128)(2,1)}), bf16[16,256,128]{2,1,0:T(8,128)(2,1)S(1)}, u32[]{:S(2)}, u32[]{:S(2)}) %all-to-all-start.2) | async-done | bytes 1048608 | tf_op jit(solution)/shard_map/all_to_all | solution.py:479
  131.4 4.0 %collective-permute-done.21 = f32[256,128]{1,0:T(8,128)S(1)} collective-permute-done((f32[256,128]{1,0:T(8,128)S(1)}, f32[256,128]{1,0:T(8,128)S(1)}, u32[]{:S(2)}, u32[]{:S(2)}) %collective-permute-start.21) | collective-permute-done | bytes 131104 | tf_op jit(solution)/shard_map/ppermute | solution.py:429
  136.7 39.4 %all_to_all.21.all_ref = bf16[16,704,128]{2,1,0:T(8,128)(2,1)S(1)} all-to-all(bf16[16,704,128]{2,1,0:T(8,128)(2,1)} %broadcast_dynamic-update-slice_fusion), channel_id=1, replica_groups=mesh['zh'=4,'c'=2,'y'=4,'x'=4,'zl'=2] {'y','x'}, dimensions={0} | all-to-all | bytes 5767168 | tf_op jit(solution)/shard_map/all_to_all | solution.py:489
  (80 shorter events, 20.7 us)
Async XLA Ops:
  2.3 14.1 %collective-permute-start.1 = (bf16[4,224,128]{2,1,0:T(8,128)(2,1)}, bf16[4,224,128]{2,1,0:T(8,128)(2,1)S(1)}, u32[]{:S(2)}, u32[]{:S(2)}) collective-permute-start(bf16[4,224,128]{2,1,0:T(8,128)(2,1)} %shard_map.78.own_ref.refs_0_), channel_id=1, source_target_pairs={{0,64},{64,128},{128,192},{192,0},{1,65},{65,129},{129,193},{193,1... | collective-permute-start | bytes 688136 | tf_op jit(solution)/shard_map/ppermute | solution.py:429
  5.6 15.0 %collective-permute-start.2 = (bf16[4,224,128]{2,1,0:T(8,128)(2,1)}, bf16[4,224,128]{2,1,0:T(8,128)(2,1)S(1)}, u32[]{:S(2)}, u32[]{:S(2)}) collective-permute-start(bf16[4,224,128]{2,1,0:T(8,128)(2,1)} %shard_map.78.own_ref.refs_0_), channel_id=1, source_target_pairs={{0,192},{64,0},{128,64},{192,128},{1,193},{65,1},{129,65},{193,129... | collective-permute-start | bytes 688136 | tf_op jit(solution)/shard_map/ppermute | solution.py:429
  8.6 12.4 %collective-permute-start = (bf16[4,224,128]{2,1,0:T(8,128)(2,1)}, bf16[4,224,128]{2,1,0:T(8,128)(2,1)S(1)}, u32[]{:S(2)}, u32[]{:S(2)}) collective-permute-start(bf16[4,224,128]{2,1,0:T(8,128)(2,1)} %shard_map.78.own_ref.refs_0_), channel_id=1, source_target_pairs={{0,32},{32,0},{1,33},{33,1},{2,34},{34,2},{3,35},{35,3},{4,36},{36... | collective-permute-start | bytes 688136 | tf_op jit(solution)/shard_map/ppermute | solution.py:429
  20.5 1.8 %collective-permute-start.4 = (bf16[4,224,128]{2,1,0:T(8,128)(2,1)S(1)}, bf16[4,224,128]{2,1,0:T(8,128)(2,1)S(1)}, u32[]{:S(2)}, u32[]{:S(2)}) collective-permute-start(bf16[4,224,128]{2,1,0:T(8,128)(2,1)S(1)} %collective-permute-done.2.next_ref.refs_2_), channel_id=1, source_target_pairs={{0,32},{32,0},{1,33},{33,1},{2,34},{34,2},{3,35},{35,3},{4,36},{36... | collective-permute-start | bytes 688136 | tf_op jit(solution)/shard_map/ppermute | solution.py:429
  21.0 40.5 %collective-permute-start.9 = (bf16[128,3584]{1,0:T(8,128)(2,1)}, bf16[128,3584]{1,0:T(8,128)(2,1)S(1)}, u32[]{:S(2)}, u32[]{:S(2)}) collective-permute-start(bf16[128,3584]{1,0:T(8,128)(2,1)} %get-tuple-element.40), channel_id=1, source_target_pairs={{0,1},{1,0},{2,3},{3,2},{4,5},{5,4},{6,7},{7,6},{8,9},{9,8},{10,11... | collective-permute-start | bytes 2752520 | tf_op jit(solution)/shard_map/ppermute | solution.py:429
  44.2 4.0 %collective-permute-start.5 = (bf16[128,128]{1,0:T(8,128)(2,1)S(1)}, bf16[128,128]{1,0:T(8,128)(2,1)S(1)}, u32[]{:S(2)}, u32[]{:S(2)}) collective-permute-start(bf16[128,128]{1,0:T(8,128)(2,1)S(1)} %reduce_sum.21), channel_id=1, source_target_pairs={{0,1},{1,0},{2,3},{3,2},{4,5},{5,4},{6,7},{7,6},{8,9},{9,8},{10,11... | collective-permute-start | bytes 98312 | tf_op jit(solution)/shard_map/ppermute | solution.py:429
  48.2 7.3 %collective-permute-start.6 = (bf16[128,128]{1,0:T(8,128)(2,1)S(1)}, bf16[128,128]{1,0:T(8,128)(2,1)S(1)}, u32[]{:S(2)}, u32[]{:S(2)}) collective-permute-start(bf16[128,128]{1,0:T(8,128)(2,1)S(1)} %add_convert_fusion.1), channel_id=1, source_target_pairs={{0,192},{64,0},{128,64},{192,128},{1,193},{65,1},{129,65},{193,129... | collective-permute-start | bytes 98312 | tf_op jit(solution)/shard_map/ppermute | solution.py:429
  50.9 7.8 %collective-permute-start.7 = (bf16[128,128]{1,0:T(8,128)(2,1)S(1)}, bf16[128,128]{1,0:T(8,128)(2,1)S(1)}, u32[]{:S(2)}, u32[]{:S(2)}) collective-permute-start(bf16[128,128]{1,0:T(8,128)(2,1)S(1)} %add_convert_fusion.1), channel_id=1, source_target_pairs={{0,128},{64,192},{128,0},{192,64},{1,129},{65,193},{129,1},{193,65... | collective-permute-start | bytes 98312 | tf_op jit(solution)/shard_map/ppermute | solution.py:429
  55.5 6.0 %collective-permute-start.8 = (bf16[128,128]{1,0:T(8,128)(2,1)S(1)}, bf16[128,128]{1,0:T(8,128)(2,1)S(1)}, u32[]{:S(2)}, u32[]{:S(2)}) collective-permute-start(bf16[128,128]{1,0:T(8,128)(2,1)S(1)} %add_convert_fusion.1), channel_id=1, source_target_pairs={{0,64},{64,128},{128,192},{192,0},{1,65},{65,129},{129,193},{193,1... | collective-permute-start | bytes 98312 | tf_op jit(solution)/shard_map/ppermute | solution.py:429
  63.3 30.1 %all-to-all-start.1 = ((bf16[16,512,128]{2,1,0:T(8,128)(2,1)}), bf16[16,512,128]{2,1,0:T(8,128)(2,1)S(1)}, u32[]{:S(2)}, u32[]{:S(2)}) async-start(bf16[16,512,128]{2,1,0:T(8,128)(2,1)} %broadcast_in_dim.8), calls=%async_computation.1 | async-start | bytes 4194304 | tf_op jit(solution)/shard_map/all_to_all | solution.py:434
  68.4 16.9 %collective-permute-start.10 = (bf16[128,768]{1,0:T(8,128)(2,1)S(1)}, bf16[128,768]{1,0:T(8,128)(2,1)S(1)}, u32[]{:S(2)}, u32[]{:S(2)}) collective-permute-start(bf16[128,768]{1,0:T(8,128)(2,1)S(1)} %copy-done.11), channel_id=1, source_target_pairs={{0,192},{64,0},{128,64},{192,128},{1,193},{65,1},{129,65},{193,129... | collective-permute-start | bytes 589832 | tf_op jit(solution)/shard_map/ppermute | solution.py:429
  68.5 16.8 %collective-permute-start.11 = (bf16[128,768]{1,0:T(8,128)(2,1)S(1)}, bf16[128,768]{1,0:T(8,128)(2,1)S(1)}, u32[]{:S(2)}, u32[]{:S(2)}) collective-permute-start(bf16[128,768]{1,0:T(8,128)(2,1)S(1)} %copy-done.11), channel_id=1, source_target_pairs={{0,128},{64,192},{128,0},{192,64},{1,129},{65,193},{129,1},{193,65... | collective-permute-start | bytes 589832 | tf_op jit(solution)/shard_map/ppermute | solution.py:429
  71.3 16.8 %collective-permute-start.12 = (bf16[128,768]{1,0:T(8,128)(2,1)S(1)}, bf16[128,768]{1,0:T(8,128)(2,1)S(1)}, u32[]{:S(2)}, u32[]{:S(2)}) collective-permute-start(bf16[128,768]{1,0:T(8,128)(2,1)S(1)} %copy-done.11), channel_id=1, source_target_pairs={{0,64},{64,128},{128,192},{192,0},{1,65},{65,129},{129,193},{193,1... | collective-permute-start | bytes 589832 | tf_op jit(solution)/shard_map/ppermute | solution.py:429
  73.3 14.7 %collective-permute-start.13 = (bf16[128,768]{1,0:T(8,128)(2,1)S(1)}, bf16[128,768]{1,0:T(8,128)(2,1)S(1)}, u32[]{:S(2)}, u32[]{:S(2)}) collective-permute-start(bf16[128,768]{1,0:T(8,128)(2,1)S(1)} %copy-done.11), channel_id=1, source_target_pairs={{0,32},{32,0},{1,33},{33,1},{2,34},{34,2},{3,35},{35,3},{4,36},{36... | collective-permute-start | bytes 589832 | tf_op jit(solution)/shard_map/ppermute | solution.py:429
  93.4 5.0 %collective-permute-start.17 = (bf16[8192,128]{1,0:T(8,128)(2,1)S(1)}, bf16[8192,128]{1,0:T(8,128)(2,1)S(1)}, u32[]{:S(2)}, u32[]{:S(2)}) collective-permute-start(bf16[8192,128]{1,0:T(8,128)(2,1)S(1)} %bitcast.13), channel_id=1, source_target_pairs={{0,32},{32,0},{1,33},{33,1},{2,34},{34,2},{3,35},{35,3},{4,36},{36... | collective-permute-start | bytes 6291464 | tf_op jit(solution)/shard_map/ppermute | solution.py:429
  93.4 4.4 %collective-permute-start.14 = (bf16[128,768]{1,0:T(8,128)(2,1)S(1)}, bf16[128,768]{1,0:T(8,128)(2,1)S(1)}, u32[]{:S(2)}, u32[]{:S(2)}) collective-permute-start(bf16[128,768]{1,0:T(8,128)(2,1)S(1)} %collective-permute-done.10.refs_2_), channel_id=1, source_target_pairs={{0,32},{32,0},{1,33},{33,1},{2,34},{34,2},{3,35},{35,3},{4,36},{36... | collective-permute-start | bytes 589832 | tf_op jit(solution)/shard_map/ppermute | solution.py:429
  93.9 4.2 %collective-permute-start.15 = (bf16[128,768]{1,0:T(8,128)(2,1)S(1)}, bf16[128,768]{1,0:T(8,128)(2,1)S(1)}, u32[]{:S(2)}, u32[]{:S(2)}) collective-permute-start(bf16[128,768]{1,0:T(8,128)(2,1)S(1)} %collective-permute-done.11.refs_4_), channel_id=1, source_target_pairs={{0,32},{32,0},{1,33},{33,1},{2,34},{34,2},{3,35},{35,3},{4,36},{36... | collective-permute-start | bytes 589832 | tf_op jit(solution)/shard_map/ppermute | solution.py:429
  93.9 4.5 %collective-permute-start.16 = (bf16[128,768]{1,0:T(8,128)(2,1)S(1)}, bf16[128,768]{1,0:T(8,128)(2,1)S(1)}, u32[]{:S(2)}, u32[]{:S(2)}) collective-permute-start(bf16[128,768]{1,0:T(8,128)(2,1)S(1)} %collective-permute-done.12.refs_6_), channel_id=1, source_target_pairs={{0,32},{32,0},{1,33},{33,1},{2,34},{34,2},{3,35},{35,3},{4,36},{36... | collective-permute-start | bytes 589832 | tf_op jit(solution)/shard_map/ppermute | solution.py:429
  94.4 13.8 %collective-permute-start.18 = (bf16[4,224,128]{2,1,0:T(8,128)(2,1)S(1)}, bf16[4,224,128]{2,1,0:T(8,128)(2,1)S(1)}, u32[]{:S(2)}, u32[]{:S(2)}) collective-permute-start(bf16[4,224,128]{2,1,0:T(8,128)(2,1)S(1)} %copy-done.2), channel_id=1, source_target_pairs={{0,64},{64,128},{128,192},{192,0},{1,65},{65,129},{129,193},{193,1... | collective-permute-start | bytes 688136 | tf_op jit(solution)/shard_map/ppermute | solution.py:429
  97.8 18.2 %collective-permute-start.19 = (bf16[128,3584]{1,0:T(8,128)(2,1)}, bf16[128,3584]{1,0:T(8,128)(2,1)}, u32[]{:S(2)}, u32[]{:S(2)}) collective-permute-start(bf16[128,3584]{1,0:T(8,128)(2,1)} %copy-done.17), channel_id=1, source_target_pairs={{0,32},{32,0},{1,33},{33,1},{2,34},{34,2},{3,35},{35,3},{4,36},{36... | collective-permute-start | bytes 2752520 | tf_op jit(solution)/shard_map/ppermute | solution.py:429
  108.2 22.1 %all-to-all-start.2 = ((bf16[16,256,128]{2,1,0:T(8,128)(2,1)}), bf16[16,256,128]{2,1,0:T(8,128)(2,1)S(1)}, u32[]{:S(2)}, u32[]{:S(2)}) async-start(bf16[16,256,128]{2,1,0:T(8,128)(2,1)} %bitcast.10), calls=%async_computation.2 | async-start | bytes 2097152 | tf_op jit(solution)/shard_map/all_to_all | solution.py:479
  114.4 4.7 %collective-permute-start.20 = (bf16[3,128,128]{2,1,0:T(8,128)(2,1)S(1)}, bf16[3,128,128]{2,1,0:T(8,128)(2,1)S(1)}, u32[]{:S(2)}, u32[]{:S(2)}) collective-permute-start(bf16[3,128,128]{2,1,0:T(8,128)(2,1)S(1)} %copy-done.13), channel_id=1, source_target_pairs={{0,1},{1,0},{2,3},{3,2},{4,5},{5,4},{6,7},{7,6},{8,9},{9,8},{10,11... | collective-permute-start | bytes 294920 | tf_op jit(solution)/shard_map/ppermute | solution.py:429
  130.4 5.1 %collective-permute-start.21 = (f32[256,128]{1,0:T(8,128)S(1)}, f32[256,128]{1,0:T(8,128)S(1)}, u32[]{:S(2)}, u32[]{:S(2)}) collective-permute-start(f32[256,128]{1,0:T(8,128)S(1)} %convert_reduce_fusion), channel_id=1, source_target_pairs={{0,1},{1,0},{2,3},{3,2},{4,5},{5,4},{6,7},{7,6},{8,9},{9,8},{10,11... | collective-permute-start | bytes 393224 | tf_op jit(solution)/shard_map/ppermute | solution.py:429
  131.4 5.3 %collective-permute-start.22 = (bf16[4,224,128]{2,1,0:T(8,128)(2,1)S(1)}, bf16[4,224,128]{2,1,0:T(8,128)(2,1)S(1)}, u32[]{:S(2)}, u32[]{:S(2)}) collective-permute-start(bf16[4,224,128]{2,1,0:T(8,128)(2,1)S(1)} %collective-permute-done.18.refs_4_), channel_id=1, source_target_pairs={{0,32},{32,0},{1,33},{33,1},{2,34},{34,2},{3,35},{35,3},{4,36},{36... | collective-permute-start | bytes 688136 | tf_op jit(solution)/shard_map/ppermute | solution.py:429
  (20 other events, 329.9 us)
